TPU v7x, 32 devices: a whole 2x2x4 slice. The times are simulated.
32 devices in a mesh: occ: 8 (over y, x, core), vir: 4 (over z).
Axes of the slice: x: 2, y: 2, z: 4, core: 2. Of those that a mesh axis runs over, the one named last changes fastest.
Arguments:
- amplitudes: bfloat16 [8, 128, 4096], P(None, 'occ', 'vir'), may hold values from -8 to 8
- integrals: bfloat16 [8, 2048, 4096], P(None, 'occ', 'vir'), may hold values from -0.09375 to 0.09375
- occ_energy: float32 [8, 128], P(None, ('occ', 'vir')), may hold values from 0.5 to 2
- vir_energy: float32 [8, 2048], replicated, may hold values from 1 to 3
Outputs:
- amplitude_update: float32 [8, 128, 2048], P(None, ('occ', 'vir'))
All inputs are finite; a program needn't handle non-finite values.
Results may differ from a plain program's by a relative error of at most 0.0003.
Values may be sent and summed in bfloat16 or wider, within the bound.
No kernel may reach another device: no remote copies, remote signals or barrier semaphores. Data moves between devices by JAX's collectives and lax.ppermute only.
A program may use at most 64 MiB of HBM per device.

v0:
```python
import jax
import jax.numpy as jnp
from jax import lax
from jax.sharding import PartitionSpec as P


def contract(piece, int_block):
    return jnp.einsum("gic,gac->gia", piece, int_block, preferred_element_type=jnp.float32)


def local(amplitudes, integrals, occ_energy, vir_energy):
    n_occ = lax.axis_size("occ")
    n_vir = lax.axis_size("vir")
    irreps = amplitudes.shape[0]
    rows_dev = amplitudes.shape[1]
    share = rows_dev // n_vir
    ladder = contract(lax.all_gather(amplitudes, "occ", axis=1, tiled=True), integrals)
    partial_cols = lax.psum_scatter(ladder, "vir", scatter_dimension=2, tiled=True)
    width = partial_cols.shape[2]
    moved = lax.all_to_all(
        lax.all_to_all(partial_cols, "occ", split_axis=1, concat_axis=2, tiled=True),
        "vir",
        split_axis=1,
        concat_axis=2,
        tiled=True,
    )
    moved = moved.reshape(irreps, share, n_vir, n_occ, width)
    moved = jnp.transpose(moved, (0, 1, 3, 2, 4)).reshape(irreps, share, n_occ * n_vir * width)
    return moved / (occ_energy[:, :, None] + vir_energy[:, None, :])


def solution(mesh):
    placed = (P(None, "occ", "vir"), P(None, "occ", "vir"), P(None, ("occ", "vir")), P())
    return jax.shard_map(
        local, mesh=mesh, in_specs=placed, out_specs=P(None, ("occ", "vir"), None), check_vma=False
    )
```

profile of v0, /device:TPU:0, one launch (start us, length us, event | category | flops | bytes accessed | tf_op | source)
XLA Modules:
  0.0 106.3 jit_solution(2403504100493387479)
XLA Ops:
  6.5 0.0 all-gather.2.cloned.1.call-start
  6.5 0.7 all-gather.2.cloned.1.call-update
  7.3 0.0 reduce-scatter.2.cloned.1.call-start
  7.3 32.6 %all-gather.2.cloned.1.call-done = bf16[8,128,1024]{2,1,0:T(8,128)(2,1)} async-done(((bf16[8,16,1024]{2,1,0:T(8,128)(2,1)}), bf16[8,128,1024]{2,1,0:T(8,128)(2,1)}) %all-gather.2.cloned.1.call-update) | async-done | bytes 2097168 | tf_op jit(solution)/shard_map/all_gather | solution.py:17
  39.9 5.1 %fusion = f32[8,128,256]{1,2,0:T(8,128)} fusion(bf16[8,128,1024]{2,1,0:T(8,128)(2,1)} %all-gather.2.cloned.1.call-done, bf16[8,256,1024]{2,1,0:T(8,128)(2,1)} %param.5), kind=kOutput, calls=%fused_computation.2 | convolution fusion | flops 536870912 | bytes 7340032 | tf_op jit(solution)/shard_map/gic,gac->gia/dot_general | solution.py:8
  45.0 0.0 reduce-scatter.2.cloned.1.call-update
  45.0 27.3 %reduce-scatter.2.cloned.1.call-done = f32[8,128,64]{1,2,0:T(8,128)} async-done(((f32[8,128,256]{1,2,0:T(8,128)}), f32[8,128,64]{1,2,0:T(8,128)}) %reduce-scatter.2.cloned.1.call-update) | async-done | bytes 262160 | tf_op jit(solution)/shard_map/reduce_scatter | solution.py:18
  72.3 1.2 %copy.15 = f32[8,128,64]{2,0,1:T(8,128)S(1)} copy(f32[8,128,64]{1,2,0:T(8,128)} %reduce-scatter.2.cloned.1.call-done) | data formatting | bytes 524288 | tf_op jit(solution)/shard_map/reduce_scatter | solution.py:18
  73.5 0.0 copy-start
  73.5 0.0 copy-start.1
  73.5 0.3 reshape.12
  73.8 10.4 %all_to_all.33 = f32[8,1,8192]{2,1,0:T(1,128)S(1)} all-to-all(f32[8,1,8192]{2,1,0:T(1,128)S(1)} %reshape.12), channel_id=1, replica_groups=mesh['occ'=8,'vir'=4] {'occ'}, dimensions={0} | all-to-all | bytes 524288 | tf_op jit(solution)/shard_map/all_to_all | solution.py:21
  84.2 0.5 broadcast.2
  84.7 1.3 %reduce = f32[8,8192]{1,0:T(8,128)S(1)} reduce(f32[8,1,8192]{2,1,0:T(1,128)S(1)} %all_to_all.33, f32[]{:T(128)} %broadcast.2), dimensions={1}, to_apply=%all_to_all.24.reduce_sub_computation | reduce | bytes 524292 | tf_op jit(solution)/shard_map/all_to_all | solution.py:21
  86.0 0.2 reshape.13
  86.2 0.3 copy.23
  86.5 0.1 reshape.11
  86.7 10.9 %all_to_all.34 = f32[8,16,512]{2,0,1:T(8,128)S(1)} all-to-all(f32[8,16,512]{2,0,1:T(8,128)S(1)} %reshape.11), channel_id=1, replica_groups=mesh['occ'=8,'vir'=4] {'vir'}, dimensions={1} | all-to-all | bytes 524288 | tf_op jit(solution)/shard_map/all_to_all | solution.py:20
  97.6 0.1 reshape.9
  97.7 0.3 copy.20
  98.1 0.4 reshape.10
  98.5 0.0 copy-done
  98.5 0.0 copy-done.1
  98.5 0.1 add_divide_fusion
  98.6 0.9 copy.21
  (1 shorter events, 0.0 us)
Async XLA Ops:
  6.5 33.4 %all-gather.2.cloned.1.call-start = ((), (), s32[]{:S(2)}) async-start(), calls=%async_computation.3 | async-start | bytes 2359296 | tf_op jit(solution)/shard_map/all_gather | solution.py:17
  7.3 65.0 %reduce-scatter.2.cloned.1.call-start = ((), (), s32[]{:S(2)}) async-start(), calls=%async_computation.4 | async-start | bytes 1310720 | tf_op jit(solution)/shard_map/reduce_scatter | solution.py:18
  73.5 25.0 %copy-start = (f32[8,2048]{1,0:T(8,128)S(1)}, f32[8,2048]{1,0:T(8,128)}, u32[]{:S(2)}) copy-start(f32[8,2048]{1,0:T(8,128)} %param.7) | copy-start | bytes 196612
  73.5 25.0 %copy-start.1 = (f32[8,4]{0,1:T(4,128)S(1)}, f32[8,4]{0,1:T(4,128)}, u32[]{:S(2)}) copy-start(f32[8,4]{0,1:T(4,128)} %param.6) | copy-start | bytes 388
Sparse Core Ops, SparseCore 0:
  9.3 30.5 all-gather.1
  45.1 27.1 reduce-scatter.1
where the time goes:
time: 107 us; the launch traced here: 106 us
  waiting for transfers between devices  60.6 us (57%)
  blocking collectives  21.3 us (20%)
  between operations  13.5 us (13%)
  matrix products  5.07 us (5%)
  local copies, waits for them, and re-layouts  4.48 us (4%)
  other arithmetic  1.37 us (1%)
    all_gather x1, waiting for transfers between devices, local(): lax.all_gather(amplitudes, 'occ', axis=1, tiled=True)  32.6 us
    reduce_scatter x1, waiting for transfers between devices, local(): lax.psum_scatter(ladder, 'vir', scatter_dimension=2, tiled=True)  27.3 us
    all_to_all x1, blocking collectives, local(): lax.all_to_all(lax.all_to_all(partial_cols, 'occ', split_axis=1, concat_a...  10.9 us
    all_to_all x1, blocking collectives, local(): lax.all_to_all(partial_cols, 'occ', split_axis=1, concat_axis=2, tiled=True)  10.4 us
    dot_general x1, matrix products, contract(): jnp.einsum('gic,gac->gia', piece, int_block, preferred_element_type=jnp.f...  5.07 us
  transfers between devices with their start and end apart: 2, of which 2 were waited for; matrix products, arithmetic and copies ran while one was open for 0% of the time, Pallas kernels for 0%

commit v1 on v0

v1 whole, which is shorter than its diff:
```python
import functools

import jax
import jax.numpy as jnp
from jax import lax
from jax.experimental import pallas as pl
from jax.experimental.pallas import tpu as pltpu
from jax.sharding import PartitionSpec as P

VMEM = pl.BlockSpec(memory_space=pltpu.VMEM)
SMEM = pl.BlockSpec(memory_space=pltpu.SMEM)
PARAMS = pltpu.CompilerParams(vmem_limit_bytes=16 << 20)


def contract_kernel(blocks, place_ref, *refs):
    amp_refs, int_ref, out_ref = refs[:blocks], refs[blocks], refs[blocks + 1]
    vir = place_ref[0]
    upper = lax.broadcasted_iota(jnp.int32, (8, int_ref.shape[1]), 0) < 4

    for g in range(int_ref.shape[0]):
        rows = jnp.concatenate([a[g] for a in amp_refs], axis=0) if blocks > 1 else amp_refs[0][g]
        sums = lax.dot_general(
            rows, int_ref[g], (((1,), (1,)), ((), ())), preferred_element_type=jnp.float32
        )
        for pair in range(blocks // 2):
            for half in range(2):
                first = sums[32 * pair + 8 * half : 32 * pair + 8 * half + 8]
                second = sums[32 * pair + 16 + 8 * half : 32 * pair + 24 + 8 * half]
                low = jnp.where(upper, first, pltpu.roll(second, 4, 0))
                high = jnp.where(upper, pltpu.roll(first, 4, 0), second)
                at = pl.ds(8 * pair, 8)
                out_ref[(2 * half) ^ vir, g, at, :] = low
                out_ref[(2 * half + 1) ^ vir, g, at, :] = high


def contract(place, pieces, integrals):
    irreps, width = integrals.shape[0], integrals.shape[1]
    rows = 4 * len(pieces)
    depth = integrals.shape[2]
    return pl.pallas_call(
        functools.partial(contract_kernel, len(pieces)),
        out_shape=jax.ShapeDtypeStruct((4, irreps, rows, width), jnp.float32),
        in_specs=[SMEM] + [VMEM] * (len(pieces) + 1),
        out_specs=VMEM,
        compiler_params=PARAMS,
        cost_estimate=pl.CostEstimate(
            flops=2 * irreps * 4 * rows * depth * width,
            bytes_accessed=2 * irreps * depth * (width + 4 * rows) + 16 * irreps * rows * width,
            transcendentals=0,
        ),
    )(place, *pieces, integrals)


def update_kernel(masks, place_ref, occ_ref, vir_ref, *refs):
    out_ref = refs[len(masks)]
    width = refs[0].shape[2]
    share = out_ref.shape[1]
    for mask, piece in zip(masks, refs):
        at = pl.ds(pl.multiple_of((place_ref[1] ^ mask) * width, width), width)
        for g in range(out_ref.shape[0]):
            levels = occ_ref[g][:, None] + vir_ref[g, at][None, :]
            out_ref[g, :, at] = piece[g] / levels


def update(place, occ_energy, vir_energy, masks, pieces):
    irreps, share = occ_energy.shape
    return pl.pallas_call(
        functools.partial(update_kernel, masks),
        out_shape=jax.ShapeDtypeStruct((irreps, share, vir_energy.shape[1]), jnp.float32),
        in_specs=[SMEM] + [VMEM] * (2 + len(pieces)),
        out_specs=VMEM,
        compiler_params=PARAMS,
    )(place, occ_energy, vir_energy, *pieces)


def swap(x, axis, mask):
    return lax.ppermute(x, axis, [(i, i ^ mask) for i in range(lax.axis_size(axis))])


def paired(groups, amplitudes, integrals, occ_energy, vir_energy):
    place = jnp.stack([lax.axis_index("vir"), lax.axis_index("occ")]).astype(jnp.int32)
    held = {0: amplitudes, 1: swap(amplitudes, "occ", 1)}
    for mask in (2, 4, 6):
        held[mask] = swap(amplitudes, "occ", mask)
        held[mask + 1] = swap(held[mask], "occ", 1)
    done = {}
    for group in groups:
        sums = contract(place, [held[m] for m in group], integrals)
        total = sums[0]
        for j in range(1, 4):
            total = total + swap(sums[j].astype(jnp.float16), "vir", j).astype(jnp.float32)
        for n, m in enumerate(group):
            part = total[:, 4 * n : 4 * n + 4]
            done[m] = swap(part, "occ", m) if m else part
    masks = sorted(done)
    return update(place, occ_energy, vir_energy, masks, [done[m] for m in masks])


def plain(amplitudes, integrals, occ_energy, vir_energy):
    n_occ = lax.axis_size("occ")
    n_vir = lax.axis_size("vir")
    irreps, rows_dev = amplitudes.shape[:2]
    share = rows_dev // n_vir
    held = lax.all_gather(amplitudes, "occ", axis=1, tiled=True)
    ladder = jnp.einsum("gic,gac->gia", held, integrals, preferred_element_type=jnp.float32)
    partial_cols = lax.psum_scatter(ladder, "vir", scatter_dimension=2, tiled=True)
    width = partial_cols.shape[2]
    moved = lax.all_to_all(partial_cols, "occ", split_axis=1, concat_axis=2, tiled=True)
    moved = lax.all_to_all(moved, "vir", split_axis=1, concat_axis=2, tiled=True)
    moved = moved.reshape(irreps, share, n_vir, n_occ, width)
    moved = jnp.transpose(moved, (0, 1, 3, 2, 4)).reshape(irreps, share, n_occ * n_vir * width)
    return moved / (occ_energy[:, :, None] + vir_energy[:, None, :])


def local(amplitudes, integrals, occ_energy, vir_energy):
    fits = lax.axis_size("occ") == 8 and lax.axis_size("vir") == 4 and amplitudes.shape[1] == 16
    if not fits:
        return plain(amplitudes, integrals, occ_energy, vir_energy)
    groups = [(0, 1, 2, 3, 4, 5, 6, 7)]
    return paired(groups, amplitudes, integrals, occ_energy, vir_energy)


def solution(mesh):
    placed = (P(None, "occ", "vir"), P(None, "occ", "vir"), P(None, ("occ", "vir")), P())
    return jax.shard_map(
        local, mesh=mesh, in_specs=placed, out_specs=P(None, ("occ", "vir"), None), check_vma=False
    )
```

time: 107 us -> 49.5 us (0.46)
  waiting for transfers between devices: 60.6 us -> 26.4 us
  blocking collectives: 21.3 us -> 0 us
  starting transfers between devices: 0.04 us -> 15.8 us
  between operations: 13.5 us -> 0.07 us
  matrix products: 5.07 us -> 0 us
  Pallas kernels: 0 us -> 3.45 us
  local copies, waits for them, and re-layouts: 4.48 us -> 3.35 us
  other arithmetic: 1.37 us -> 0.27 us
    all_gather x1 -> x0, waiting for transfers between devices: 32.6 us -> none  [local(): lax.all_gather(amplitudes, 'occ', axis=1, tiled=True)]
    reduce_scatter x1 -> x0, waiting for transfers between devices: 27.3 us -> none  [local(): lax.psum_scatter(ladder, 'vir', scatter_dimension=2, tiled=True)]
    ppermute x0 -> x17, waiting for transfers between devices: none -> 26.4 us  [swap(): lax.ppermute(x, axis, [(i, i ^ mask) for i in range(lax.axis_size(axis))])]
    all_to_all x2 -> x0, blocking collectives: 21.3 us -> none  [the longest x1 10.9 us: local(): lax.all_to_all(lax.all_to_all(partial_cols, 'occ', split_axis=1, concat_a...]
    ppermute x0 -> x17, starting transfers between devices: none -> 15.8 us  [swap(): lax.ppermute(x, axis, [(i, i ^ mask) for i in range(lax.axis_size(axis))])]
    dot_general x1 -> x0, matrix products: 5.07 us -> none  [contract(): jnp.einsum('gic,gac->gia', piece, int_block, preferred_element_type=jnp.f...]
    pallas_call x0 -> x2, Pallas kernels: none -> 3.45 us  [the longest x1 2.05 us: contract(): pl.pallas_call(functools.partial(contract_kernel, len(pieces)), out_shape...]
    unnamed x6 -> x9, local copies, waits for them, and re-layouts: 0.55 us -> 3.23 us
  transfers between devices with their start and end apart: 2 -> 17, of which waited for: 2 -> 9; matrix products, arithmetic and copies ran while one was open for 0% -> 0% of each run, Pallas kernels for 0% -> 0%
where the time goes in v1:
time: 49.5 us; the launch traced here: 49.3 us
  waiting for transfers between devices  26.4 us (53%)
  starting transfers between devices  15.8 us (32%)
  Pallas kernels  3.45 us (7%)
  local copies, waits for them, and re-layouts  3.35 us (7%)
    ppermute x17, waiting for transfers between devices, swap(): lax.ppermute(x, axis, [(i, i ^ mask) for i in range(lax.axis_size(axis))])  26.4 us
    ppermute x17, starting transfers between devices, swap(): lax.ppermute(x, axis, [(i, i ^ mask) for i in range(lax.axis_size(axis))])  15.8 us
    unnamed x9, local copies, waits for them, and re-layouts  3.23 us
    pallas_call x1, Pallas kernels, contract(): pl.pallas_call(functools.partial(contract_kernel, len(pieces)), out_shape...  2.05 us
    pallas_call x1, Pallas kernels, update(): pl.pallas_call(functools.partial(update_kernel, masks), out_shape=jax.Sha...  1.39 us
  transfers between devices with their start and end apart: 17, of which 9 were waited for; matrix products, arithmetic and copies ran while one was open for 0% of the time, Pallas kernels for 0%

profile of v1, /device:TPU:0, one launch (start us, length us, event | category | flops | bytes accessed | tf_op | source)
XLA Modules:
  0.0 49.3 jit_solution(16746382973666584606)
XLA Ops:
  0.0 2.9 %collective-permute-start.1 = (bf16[8,16,1024]{2,1,0:T(8,128)(2,1)}, bf16[8,16,1024]{2,1,0:T(8,128)(2,1)S(1)}, u32[]{:S(2)}, u32[]{:S(2)}) collective-permute-start(bf16[8,16,1024]{2,1,0:T(8,128)(2,1)} %refs_0_.1), channel_id=1, source_target_pairs={{0,8},{4,12},{8,0},{12,4},{16,24},{20,28},{24,16},{28,20},{1,9},{5... | collective-permute-start | bytes 786440 | tf_op jit(solution)/shard_map/ppermute | solution.py:77
  2.9 1.5 %collective-permute-start.3 = (bf16[8,16,1024]{2,1,0:T(8,128)(2,1)}, bf16[8,16,1024]{2,1,0:T(8,128)(2,1)S(1)}, u32[]{:S(2)}, u32[]{:S(2)}) collective-permute-start(bf16[8,16,1024]{2,1,0:T(8,128)(2,1)} %refs_0_.1), channel_id=1, source_target_pairs={{0,16},{4,20},{8,24},{12,28},{16,0},{20,4},{24,8},{28,12},{1,17},{... | collective-permute-start | bytes 786440 | tf_op jit(solution)/shard_map/ppermute | solution.py:77
  4.5 0.0 collective-permute-start.5
  4.5 0.0 collective-permute-start
  4.5 5.8 %collective-permute-done.1.refs_2_ = bf16[8,16,1024]{2,1,0:T(8,128)(2,1)S(1)} collective-permute-done((bf16[8,16,1024]{2,1,0:T(8,128)(2,1)}, bf16[8,16,1024]{2,1,0:T(8,128)(2,1)S(1)}, u32[]{:S(2)}, u32[]{:S(2)}) %collective-permute-start.1) | collective-permute-done | bytes 262176 | tf_op jit(solution)/shard_map/ppermute | solution.py:77
  10.3 0.0 collective-permute-start.2
  10.3 6.2 %collective-permute-done.3.refs_4_ = bf16[8,16,1024]{2,1,0:T(8,128)(2,1)S(1)} collective-permute-done((bf16[8,16,1024]{2,1,0:T(8,128)(2,1)}, bf16[8,16,1024]{2,1,0:T(8,128)(2,1)S(1)}, u32[]{:S(2)}, u32[]{:S(2)}) %collective-permute-start.3) | collective-permute-done | bytes 262176 | tf_op jit(solution)/shard_map/ppermute | solution.py:77
  16.5 0.0 collective-permute-start.4
  16.5 0.0 collective-permute-done.5.refs_6_
  16.5 0.5 %collective-permute-start.6 = (bf16[8,16,1024]{2,1,0:T(8,128)(2,1)S(1)}, bf16[8,16,1024]{2,1,0:T(8,128)(2,1)S(1)}, u32[]{:S(2)}, u32[]{:S(2)}) collective-permute-start(bf16[8,16,1024]{2,1,0:T(8,128)(2,1)S(1)} %collective-permute-done.5.refs_6_), channel_id=1, source_target_pairs={{0,4},{4,0},{8,12},{12,8},{16,20},{20,16},{24,28},{28,24},{1,5},{5... | collective-permute-start | bytes 786440 | tf_op jit(solution)/shard_map/ppermute | solution.py:77
  17.0 0.0 copy-start.3
  17.1 0.1 pad_add_fusion.place_ref
  17.1 0.0 collective-permute-done.refs_1_
  17.1 0.0 collective-permute-done.2.refs_3_
  17.1 0.9 %collective-permute-done.4.refs_5_ = bf16[8,16,1024]{2,1,0:T(8,128)(2,1)S(1)} collective-permute-done((bf16[8,16,1024]{2,1,0:T(8,128)(2,1)S(1)}, bf16[8,16,1024]{2,1,0:T(8,128)(2,1)S(1)}, u32[]{:S(2)}, u32[]{:S(2)}) %collective-permute-start.4) | collective-permute-done | bytes 262176 | tf_op jit(solution)/shard_map/ppermute | solution.py:77
  18.1 0.4 collective-permute-done.6.refs_7_
  18.4 0.0 copy-start
  18.4 2.2 %copy-done = bf16[8,256,1024]{2,1,0:T(8,128)(2,1)S(1)} copy-done((bf16[8,256,1024]{2,1,0:T(8,128)(2,1)S(1)}, bf16[8,256,1024]{2,1,0:T(8,128)(2,1)}, u32[]{:S(2)}) %copy-start) | copy-done | bytes 4194328
  20.6 0.0 copy-start.1
  20.6 0.9 %copy-done.1 = bf16[8,16,1024]{2,1,0:T(8,128)(2,1)S(1)} copy-done((bf16[8,16,1024]{2,1,0:T(8,128)(2,1)S(1)}, bf16[8,16,1024]{2,1,0:T(8,128)(2,1)}, u32[]{:S(2)}) %copy-start.1) | copy-done | bytes 262168
  21.6 2.1 %shard_map.46 = f32[4,8,32,256]{3,2,1,0:T(8,128)S(1)} custom-call(s32[2]{0:T(128)S(1)} %pad_add_fusion.place_ref, bf16[8,16,1024]{2,1,0:T(8,128)(2,1)S(1)} %copy-done.1, bf16[8,16,1024]{2,1,0:T(8,128)(2,1)S(1)} %collective-permute-done.refs_1_, bf16[8,16,1024]{2,1,0:T(8,128)(2,1)S(1)} %collective-permute-done.1.refs_2_, ...), custom_call_target="tpu_custom_call" | custom-call | flops 536870912 | bytes 7340032 | tf_op jit(solution)/shard_map/pallas_call | solution.py:40
  23.6 0.1 convert.5
  23.8 0.1 slice_bitcast_fusion.3
  23.9 1.6 %collective-permute-start.7 = (f16[8,32,256]{2,1,0:T(8,128)(2,1)S(1)}, f16[8,32,256]{2,1,0:T(8,128)(2,1)S(1)}, u32[]{:S(2)}, u32[]{:S(2)}) collective-permute-start(f16[8,32,256]{2,1,0:T(8,128)(2,1)S(1)} %get-tuple-element.5), channel_id=1, source_target_pairs={{0,1},{1,0},{2,3},{3,2},{4,5},{5,4},{6,7},{7,6},{8,9},{9,8},{10,11... | collective-permute-start | bytes 393224 | tf_op jit(solution)/shard_map/ppermute | solution.py:77
  25.5 2.6 %collective-permute-start.8 = (f16[8,32,256]{2,1,0:T(8,128)(2,1)S(1)}, f16[8,32,256]{2,1,0:T(8,128)(2,1)S(1)}, u32[]{:S(2)}, u32[]{:S(2)}) collective-permute-start(f16[8,32,256]{2,1,0:T(8,128)(2,1)S(1)} %get-tuple-element.7), channel_id=1, source_target_pairs={{0,2},{1,3},{2,0},{3,1},{4,6},{5,7},{6,4},{7,5},{8,10},{9,11},{10,... | collective-permute-start | bytes 393224 | tf_op jit(solution)/shard_map/ppermute | solution.py:77
  28.1 0.2 collective-permute-start.9
  28.3 3.1 %collective-permute-done.7 = f16[8,32,256]{2,1,0:T(8,128)(2,1)S(1)} collective-permute-done((f16[8,32,256]{2,1,0:T(8,128)(2,1)S(1)}, f16[8,32,256]{2,1,0:T(8,128)(2,1)S(1)}, u32[]{:S(2)}, u32[]{:S(2)}) %collective-permute-start.7) | collective-permute-done | bytes 131104 | tf_op jit(solution)/shard_map/ppermute | solution.py:77
  31.4 7.0 %collective-permute-done.8 = f16[8,32,256]{2,1,0:T(8,128)(2,1)S(1)} collective-permute-done((f16[8,32,256]{2,1,0:T(8,128)(2,1)S(1)}, f16[8,32,256]{2,1,0:T(8,128)(2,1)S(1)}, u32[]{:S(2)}, u32[]{:S(2)}) %collective-permute-start.8) | collective-permute-done | bytes 131104 | tf_op jit(solution)/shard_map/ppermute | solution.py:77
  38.4 0.0 collective-permute-done.9
  38.4 0.1 fusion.2
  38.6 0.1 collective-permute-start.10
  38.6 0.9 %collective-permute-start.11 = (f32[8,4,256]{2,1,0:T(4,128)S(1)}, f32[8,4,256]{2,1,0:T(4,128)S(1)}, u32[]{:S(2)}, u32[]{:S(2)}) collective-permute-start(f32[8,4,256]{2,1,0:T(4,128)S(1)} %get-tuple-element.13), channel_id=1, source_target_pairs={{0,8},{4,12},{8,0},{12,4},{16,24},{20,28},{24,16},{28,20},{1,9},{5... | collective-permute-start | bytes 98312 | tf_op jit(solution)/shard_map/ppermute | solution.py:77
  39.6 0.9 %collective-permute-start.12 = (f32[8,4,256]{2,1,0:T(4,128)S(1)}, f32[8,4,256]{2,1,0:T(4,128)S(1)}, u32[]{:S(2)}, u32[]{:S(2)}) collective-permute-start(f32[8,4,256]{2,1,0:T(4,128)S(1)} %get-tuple-element.12), channel_id=1, source_target_pairs={{0,12},{4,8},{8,4},{12,0},{16,28},{20,24},{24,20},{28,16},{1,13},{... | collective-permute-start | bytes 98312 | tf_op jit(solution)/shard_map/ppermute | solution.py:77
  40.5 1.5 %collective-permute-start.13 = (f32[8,4,256]{2,1,0:T(4,128)S(1)}, f32[8,4,256]{2,1,0:T(4,128)S(1)}, u32[]{:S(2)}, u32[]{:S(2)}) collective-permute-start(f32[8,4,256]{2,1,0:T(4,128)S(1)} %get-tuple-element.11), channel_id=1, source_target_pairs={{0,16},{4,20},{8,24},{12,28},{16,0},{20,4},{24,8},{28,12},{1,17},{... | collective-permute-start | bytes 98312 | tf_op jit(solution)/shard_map/ppermute | solution.py:77
  42.0 0.2 collective-permute-start.14
  42.2 0.0 collective-permute-done.10.refs_1_
  42.2 1.5 %collective-permute-start.15 = (f32[8,4,256]{2,1,0:T(4,128)S(1)}, f32[8,4,256]{2,1,0:T(4,128)S(1)}, u32[]{:S(2)}, u32[]{:S(2)}) collective-permute-start(f32[8,4,256]{2,1,0:T(4,128)S(1)} %get-tuple-element.9), channel_id=1, source_target_pairs={{0,24},{4,28},{8,16},{12,20},{16,8},{20,12},{24,0},{28,4},{1,25},{... | collective-permute-start | bytes 98312 | tf_op jit(solution)/shard_map/ppermute | solution.py:77
  43.7 0.0 collective-permute-done.11.refs_2_
  43.7 1.2 %collective-permute-start.16 = (f32[8,4,256]{2,1,0:T(4,128)S(1)}, f32[8,4,256]{2,1,0:T(4,128)S(1)}, u32[]{:S(2)}, u32[]{:S(2)}) collective-permute-start(f32[8,4,256]{2,1,0:T(4,128)S(1)} %get-tuple-element.8), channel_id=1, source_target_pairs={{0,28},{4,24},{8,20},{12,16},{16,12},{20,8},{24,4},{28,0},{1,29},{... | collective-permute-start | bytes 98312 | tf_op jit(solution)/shard_map/ppermute | solution.py:77
  44.9 0.0 copy-done.3
  44.9 0.1 copy.5.occ_ref
  45.0 0.0 collective-permute-done.12.refs_3_
  45.0 0.0 collective-permute-done.13.refs_4_
  45.0 0.5 collective-permute-done.14.refs_5_
  45.5 1.6 %collective-permute-done.15.refs_6_ = f32[8,4,256]{2,1,0:T(4,128)S(1)} collective-permute-done((f32[8,4,256]{2,1,0:T(4,128)S(1)}, f32[8,4,256]{2,1,0:T(4,128)S(1)}, u32[]{:S(2)}, u32[]{:S(2)}) %collective-permute-start.15) | collective-permute-done | bytes 32800 | tf_op jit(solution)/shard_map/ppermute | solution.py:77
  47.0 0.9 %collective-permute-done.16.refs_7_ = f32[8,4,256]{2,1,0:T(4,128)S(1)} collective-permute-done((f32[8,4,256]{2,1,0:T(4,128)S(1)}, f32[8,4,256]{2,1,0:T(4,128)S(1)}, u32[]{:S(2)}, u32[]{:S(2)}) %collective-permute-start.16) | collective-permute-done | bytes 32800 | tf_op jit(solution)/shard_map/ppermute | solution.py:77
  47.9 0.0 copy-done.2
  47.9 1.4 %shard_map.47 = f32[8,4,2048]{2,1,0:T(4,128)} custom-call(s32[2]{0:T(128)S(1)} %pad_add_fusion.place_ref, f32[8,4]{1,0:T(8,128)S(1)} %copy.5.occ_ref, f32[8,2048]{1,0:T(8,128)S(1)} %copy-done.2, f32[8,4,256]{2,1,0:T(4,128)S(1)} %get-tuple-element.15.refs_0_, f32[8,4,256]{2,1,0:T(4,128)S(1)} %collective-permute-done.10.refs_1_, ...), custom_call_target="tpu_custom_call" | custom-call | tf_op jit(solution)/shard_map/pallas_call | solution.py:67
  (2 shorter events, 0.0 us)
Async XLA Ops:
  0.0 10.3 %collective-permute-start.1 = (bf16[8,16,1024]{2,1,0:T(8,128)(2,1)}, bf16[8,16,1024]{2,1,0:T(8,128)(2,1)S(1)}, u32[]{:S(2)}, u32[]{:S(2)}) collective-permute-start(bf16[8,16,1024]{2,1,0:T(8,128)(2,1)} %refs_0_.1), channel_id=1, source_target_pairs={{0,8},{4,12},{8,0},{12,4},{16,24},{20,28},{24,16},{28,20},{1,9},{5... | collective-permute-start | bytes 786440 | tf_op jit(solution)/shard_map/ppermute | solution.py:77
  2.9 13.6 %collective-permute-start.3 = (bf16[8,16,1024]{2,1,0:T(8,128)(2,1)}, bf16[8,16,1024]{2,1,0:T(8,128)(2,1)S(1)}, u32[]{:S(2)}, u32[]{:S(2)}) collective-permute-start(bf16[8,16,1024]{2,1,0:T(8,128)(2,1)} %refs_0_.1), channel_id=1, source_target_pairs={{0,16},{4,20},{8,24},{12,28},{16,0},{20,4},{24,8},{28,12},{1,17},{... | collective-permute-start | bytes 786440 | tf_op jit(solution)/shard_map/ppermute | solution.py:77
  4.5 12.1 %collective-permute-start.5 = (bf16[8,16,1024]{2,1,0:T(8,128)(2,1)}, bf16[8,16,1024]{2,1,0:T(8,128)(2,1)S(1)}, u32[]{:S(2)}, u32[]{:S(2)}) collective-permute-start(bf16[8,16,1024]{2,1,0:T(8,128)(2,1)} %refs_0_.1), channel_id=1, source_target_pairs={{0,24},{4,28},{8,16},{12,20},{16,8},{20,12},{24,0},{28,4},{1,25},{... | collective-permute-start | bytes 786440 | tf_op jit(solution)/shard_map/ppermute | solution.py:77
  4.5 12.7 %collective-permute-start = (bf16[8,16,1024]{2,1,0:T(8,128)(2,1)}, bf16[8,16,1024]{2,1,0:T(8,128)(2,1)S(1)}, u32[]{:S(2)}, u32[]{:S(2)}) collective-permute-start(bf16[8,16,1024]{2,1,0:T(8,128)(2,1)} %refs_0_.1), channel_id=1, source_target_pairs={{0,4},{4,0},{8,12},{12,8},{16,20},{20,16},{24,28},{28,24},{1,5},{5... | collective-permute-start | bytes 786440 | tf_op jit(solution)/shard_map/ppermute | solution.py:77
  10.3 6.9 %collective-permute-start.2 = (bf16[8,16,1024]{2,1,0:T(8,128)(2,1)S(1)}, bf16[8,16,1024]{2,1,0:T(8,128)(2,1)S(1)}, u32[]{:S(2)}, u32[]{:S(2)}) collective-permute-start(bf16[8,16,1024]{2,1,0:T(8,128)(2,1)S(1)} %collective-permute-done.1.refs_2_), channel_id=1, source_target_pairs={{0,4},{4,0},{8,12},{12,8},{16,20},{20,16},{24,28},{28,24},{1,5},{5... | collective-permute-start | bytes 786440 | tf_op jit(solution)/shard_map/ppermute | solution.py:77
  16.5 1.5 %collective-permute-start.4 = (bf16[8,16,1024]{2,1,0:T(8,128)(2,1)S(1)}, bf16[8,16,1024]{2,1,0:T(8,128)(2,1)S(1)}, u32[]{:S(2)}, u32[]{:S(2)}) collective-permute-start(bf16[8,16,1024]{2,1,0:T(8,128)(2,1)S(1)} %collective-permute-done.3.refs_4_), channel_id=1, source_target_pairs={{0,4},{4,0},{8,12},{12,8},{16,20},{20,16},{24,28},{28,24},{1,5},{5... | collective-permute-start | bytes 786440 | tf_op jit(solution)/shard_map/ppermute | solution.py:77
  16.5 1.9 %collective-permute-start.6 = (bf16[8,16,1024]{2,1,0:T(8,128)(2,1)S(1)}, bf16[8,16,1024]{2,1,0:T(8,128)(2,1)S(1)}, u32[]{:S(2)}, u32[]{:S(2)}) collective-permute-start(bf16[8,16,1024]{2,1,0:T(8,128)(2,1)S(1)} %collective-permute-done.5.refs_6_), channel_id=1, source_target_pairs={{0,4},{4,0},{8,12},{12,8},{16,20},{20,16},{24,28},{28,24},{1,5},{5... | collective-permute-start | bytes 786440 | tf_op jit(solution)/shard_map/ppermute | solution.py:77
  17.0 27.8 %copy-start.3 = (f32[8,4]{0,1:T(4,128)S(1)}, f32[8,4]{0,1:T(4,128)}, u32[]{:S(2)}) copy-start(f32[8,4]{0,1:T(4,128)} %param.6) | copy-start | bytes 388
  18.4 2.2 %copy-start = (bf16[8,256,1024]{2,1,0:T(8,128)(2,1)S(1)}, bf16[8,256,1024]{2,1,0:T(8,128)(2,1)}, u32[]{:S(2)}) copy-start(bf16[8,256,1024]{2,1,0:T(8,128)(2,1)} %refs_8_.1) | copy-start | bytes 12582916
  20.6 0.9 %copy-start.1 = (bf16[8,16,1024]{2,1,0:T(8,128)(2,1)S(1)}, bf16[8,16,1024]{2,1,0:T(8,128)(2,1)}, u32[]{:S(2)}) copy-start(bf16[8,16,1024]{2,1,0:T(8,128)(2,1)} %refs_0_.1) | copy-start | bytes 786436
  21.6 26.3 %copy-start.2 = (f32[8,2048]{1,0:T(8,128)S(1)}, f32[8,2048]{1,0:T(8,128)}, u32[]{:S(2)}) copy-start(f32[8,2048]{1,0:T(8,128)} %vir_ref.1) | copy-start | bytes 196612
  23.9 7.5 %collective-permute-start.7 = (f16[8,32,256]{2,1,0:T(8,128)(2,1)S(1)}, f16[8,32,256]{2,1,0:T(8,128)(2,1)S(1)}, u32[]{:S(2)}, u32[]{:S(2)}) collective-permute-start(f16[8,32,256]{2,1,0:T(8,128)(2,1)S(1)} %get-tuple-element.5), channel_id=1, source_target_pairs={{0,1},{1,0},{2,3},{3,2},{4,5},{5,4},{6,7},{7,6},{8,9},{9,8},{10,11... | collective-permute-start | bytes 393224 | tf_op jit(solution)/shard_map/ppermute | solution.py:77
  25.5 12.9 %collective-permute-start.8 = (f16[8,32,256]{2,1,0:T(8,128)(2,1)S(1)}, f16[8,32,256]{2,1,0:T(8,128)(2,1)S(1)}, u32[]{:S(2)}, u32[]{:S(2)}) collective-permute-start(f16[8,32,256]{2,1,0:T(8,128)(2,1)S(1)} %get-tuple-element.7), channel_id=1, source_target_pairs={{0,2},{1,3},{2,0},{3,1},{4,6},{5,7},{6,4},{7,5},{8,10},{9,11},{10,... | collective-permute-start | bytes 393224 | tf_op jit(solution)/shard_map/ppermute | solution.py:77
  28.1 10.3 %collective-permute-start.9 = (f16[8,32,256]{2,1,0:T(8,128)(2,1)S(1)}, f16[8,32,256]{2,1,0:T(8,128)(2,1)S(1)}, u32[]{:S(2)}, u32[]{:S(2)}) collective-permute-start(f16[8,32,256]{2,1,0:T(8,128)(2,1)S(1)} %get-tuple-element.6), channel_id=1, source_target_pairs={{0,3},{1,2},{2,1},{3,0},{4,7},{5,6},{6,5},{7,4},{8,11},{9,10},{10,... | collective-permute-start | bytes 393224 | tf_op jit(solution)/shard_map/ppermute | solution.py:77
  38.6 3.6 %collective-permute-start.10 = (f32[8,4,256]{2,1,0:T(4,128)S(1)}, f32[8,4,256]{2,1,0:T(4,128)S(1)}, u32[]{:S(2)}, u32[]{:S(2)}) collective-permute-start(f32[8,4,256]{2,1,0:T(4,128)S(1)} %get-tuple-element.14), channel_id=1, source_target_pairs={{0,4},{4,0},{8,12},{12,8},{16,20},{20,16},{24,28},{28,24},{1,5},{5... | collective-permute-start | bytes 98312 | tf_op jit(solution)/shard_map/ppermute | solution.py:77
  38.6 5.1 %collective-permute-start.11 = (f32[8,4,256]{2,1,0:T(4,128)S(1)}, f32[8,4,256]{2,1,0:T(4,128)S(1)}, u32[]{:S(2)}, u32[]{:S(2)}) collective-permute-start(f32[8,4,256]{2,1,0:T(4,128)S(1)} %get-tuple-element.13), channel_id=1, source_target_pairs={{0,8},{4,12},{8,0},{12,4},{16,24},{20,28},{24,16},{28,20},{1,9},{5... | collective-permute-start | bytes 98312 | tf_op jit(solution)/shard_map/ppermute | solution.py:77
  39.6 5.4 %collective-permute-start.12 = (f32[8,4,256]{2,1,0:T(4,128)S(1)}, f32[8,4,256]{2,1,0:T(4,128)S(1)}, u32[]{:S(2)}, u32[]{:S(2)}) collective-permute-start(f32[8,4,256]{2,1,0:T(4,128)S(1)} %get-tuple-element.12), channel_id=1, source_target_pairs={{0,12},{4,8},{8,4},{12,0},{16,28},{20,24},{24,20},{28,16},{1,13},{... | collective-permute-start | bytes 98312 | tf_op jit(solution)/shard_map/ppermute | solution.py:77
  40.5 4.5 %collective-permute-start.13 = (f32[8,4,256]{2,1,0:T(4,128)S(1)}, f32[8,4,256]{2,1,0:T(4,128)S(1)}, u32[]{:S(2)}, u32[]{:S(2)}) collective-permute-start(f32[8,4,256]{2,1,0:T(4,128)S(1)} %get-tuple-element.11), channel_id=1, source_target_pairs={{0,16},{4,20},{8,24},{12,28},{16,0},{20,4},{24,8},{28,12},{1,17},{... | collective-permute-start | bytes 98312 | tf_op jit(solution)/shard_map/ppermute | solution.py:77
  42.0 3.4 %collective-permute-start.14 = (f32[8,4,256]{2,1,0:T(4,128)S(1)}, f32[8,4,256]{2,1,0:T(4,128)S(1)}, u32[]{:S(2)}, u32[]{:S(2)}) collective-permute-start(f32[8,4,256]{2,1,0:T(4,128)S(1)} %get-tuple-element.10), channel_id=1, source_target_pairs={{0,20},{4,16},{8,28},{12,24},{16,4},{20,0},{24,12},{28,8},{1,21},{... | collective-permute-start | bytes 98312 | tf_op jit(solution)/shard_map/ppermute | solution.py:77
  42.2 4.8 %collective-permute-start.15 = (f32[8,4,256]{2,1,0:T(4,128)S(1)}, f32[8,4,256]{2,1,0:T(4,128)S(1)}, u32[]{:S(2)}, u32[]{:S(2)}) collective-permute-start(f32[8,4,256]{2,1,0:T(4,128)S(1)} %get-tuple-element.9), channel_id=1, source_target_pairs={{0,24},{4,28},{8,16},{12,20},{16,8},{20,12},{24,0},{28,4},{1,25},{... | collective-permute-start | bytes 98312 | tf_op jit(solution)/shard_map/ppermute | solution.py:77
  43.7 4.2 %collective-permute-start.16 = (f32[8,4,256]{2,1,0:T(4,128)S(1)}, f32[8,4,256]{2,1,0:T(4,128)S(1)}, u32[]{:S(2)}, u32[]{:S(2)}) collective-permute-start(f32[8,4,256]{2,1,0:T(4,128)S(1)} %get-tuple-element.8), channel_id=1, source_target_pairs={{0,28},{4,24},{8,20},{12,16},{16,12},{20,8},{24,4},{28,0},{1,29},{... | collective-permute-start | bytes 98312 | tf_op jit(solution)/shard_map/ppermute | solution.py:77

commit v2 on v1

v2 whole, which is shorter than its diff:
```python
import functools

import jax
import jax.numpy as jnp
from jax import lax
from jax.experimental import pallas as pl
from jax.experimental.pallas import tpu as pltpu
from jax.sharding import PartitionSpec as P

VMEM = pl.BlockSpec(memory_space=pltpu.VMEM)
SMEM = pl.BlockSpec(memory_space=pltpu.SMEM)
SCALE = 64.0
MARK = jax.ShapeDtypeStruct((8, 128), jnp.float32)
PARAMS = pltpu.CompilerParams(vmem_limit_bytes=16 << 20)


def load_kernel(int_ref, slab_ref, mark_ref, sems):
    copies = [pltpu.make_async_copy(int_ref.at[g], slab_ref.at[g], sems.at[g]) for g in range(int_ref.shape[0])]
    for copy in copies:
        copy.start()
    for copy in copies:
        copy.wait()
    mark_ref[...] = jnp.zeros_like(mark_ref)


def load(integrals):
    return pl.pallas_call(
        load_kernel,
        out_shape=(jax.ShapeDtypeStruct(integrals.shape, integrals.dtype), MARK),
        in_specs=[pl.BlockSpec(memory_space=pl.ANY)],
        out_specs=(VMEM, VMEM),
        scratch_shapes=[pltpu.SemaphoreType.DMA((integrals.shape[0],))],
        compiler_params=PARAMS,
        cost_estimate=pl.CostEstimate(flops=0, bytes_accessed=4 * integrals.size, transcendentals=0),
    )(pltpu.with_memory_space_constraint(integrals, pltpu.HBM))


def contract_kernel(blocks, place_ref, seen_ref, *refs):
    amp_refs, int_ref, out_ref, mark_ref = refs[:blocks], refs[blocks], refs[blocks + 1], refs[blocks + 2]
    mark_ref[...] = jnp.zeros_like(mark_ref)
    vir = place_ref[0]
    upper = lax.broadcasted_iota(jnp.int32, (8, int_ref.shape[1]), 0) < 4
    for g in range(int_ref.shape[0]):
        rows = jnp.concatenate([a[g] for a in amp_refs], axis=0)
        sums = lax.dot_general(
            rows, int_ref[g], (((1,), (1,)), ((), ())), preferred_element_type=jnp.float32
        )
        for pair in range(blocks // 2):
            for half in range(2):
                low = sums[32 * pair + 8 * half : 32 * pair + 8 * half + 8]
                high = sums[32 * pair + 16 + 8 * half : 32 * pair + 24 + 8 * half]
                at = pl.ds(8 * pair, 8)
                out_ref[(2 * half) ^ vir, g, at, :] = jnp.where(upper, low, pltpu.roll(high, 4, 0))
                out_ref[(2 * half + 1) ^ vir, g, at, :] = jnp.where(upper, pltpu.roll(low, 4, 0), high)


def contract(place, seen, pieces, integrals):
    irreps, width, depth = integrals.shape
    rows = 4 * len(pieces)
    return pl.pallas_call(
        functools.partial(contract_kernel, len(pieces)),
        out_shape=(jax.ShapeDtypeStruct((4, irreps, rows, width), jnp.float32), MARK),
        in_specs=[SMEM] + [VMEM] * (len(pieces) + 2),
        out_specs=(VMEM, VMEM),
        compiler_params=PARAMS,
        cost_estimate=pl.CostEstimate(
            flops=2 * irreps * 4 * rows * depth * width,
            bytes_accessed=2 * irreps * depth * (width + 4 * rows) + 16 * irreps * rows * width,
            transcendentals=0,
        ),
    )(place, seen, *pieces, integrals)


def update_kernel(masks, place_ref, seen_ref, occ_ref, vir_ref, *refs):
    out_ref = refs[-1]
    width = refs[0].shape[2]
    share = out_ref.shape[1]
    for (mask, n, first), _ in zip(masks, range(len(masks))):
        piece = refs[n]
        at = pl.ds(pl.multiple_of((place_ref[1] ^ mask) * width, width), width)
        for g in range(out_ref.shape[0]):
            levels = occ_ref[g][:, None] + vir_ref[g, at][None, :]
            out_ref[g, :, at] = piece[g, first : first + share, :] / levels


def update(place, seen, occ_energy, vir_energy, masks, pieces):
    irreps, share = occ_energy.shape
    return pl.pallas_call(
        functools.partial(update_kernel, masks),
        out_shape=jax.ShapeDtypeStruct((irreps, share, vir_energy.shape[1]), jnp.float32),
        in_specs=[SMEM] + [VMEM] * (3 + len(pieces)),
        out_specs=VMEM,
        compiler_params=PARAMS,
    )(place, seen, occ_energy, vir_energy, *pieces)


def swap(x, axis, mask):
    return lax.ppermute(x, axis, [(i, i ^ mask) for i in range(lax.axis_size(axis))])


def reduced(own, sums, size):
    pieces = [swap((sums[j] * SCALE).astype(jnp.float16), "vir", j) for j in range(1, size)]
    total = pieces[0].astype(jnp.float32)
    for piece in pieces[1:]:
        total = total + piece.astype(jnp.float32)
    return own + total * (1 / SCALE)


def paired(amplitudes, integrals, occ_energy, vir_energy):
    size = lax.axis_size("vir")
    place = jnp.stack([lax.axis_index("vir"), lax.axis_index("occ")]).astype(jnp.int32)
    place, amplitudes = lax.optimization_barrier((place, amplitudes))
    half = amplitudes.shape[0] // 2
    sib = swap(amplitudes, "occ", 1)
    x = swap(amplitudes, "occ", 2)
    y = swap(amplitudes, "occ", 4)
    slab, mark = load(integrals)
    source = amplitudes
    x, y, mark = lax.optimization_barrier((x, y, mark))
    d_low, d_high = swap(x[:half], "occ", 4), swap(y[half:], "occ", 2)
    x_sib, y_sib = swap(x, "occ", 1), swap(y, "occ", 1)
    sums_b, mark = contract(place, mark, [amplitudes, sib, x, x_sib, y, y_sib], slab)
    d_low, d_high, mark = lax.optimization_barrier((d_low, d_high, mark))
    d = jnp.concatenate([d_low, d_high], axis=0)
    d_sib = swap(d, "occ", 1)
    sums_c, mark = contract(place, mark, [d, d_sib], slab)
    own, mark = lax.optimization_barrier((sums_b[0], mark))
    total_b = reduced(own, sums_b, size)
    own_c = sums_c[0]
    parts_c = [swap((sums_c[j] * SCALE).astype(jnp.float16), "vir", j) for j in range(1, size)]
    b = [swap(p, "occ", k) for k, p in ((1, total_b[:, 4:8]), (2, total_b[:, 8:12]), (3, total_b[:, 12:16]), (4, total_b[:, 16:20]), (5, total_b[:, 20:24]))]
    total_c = parts_c[0].astype(jnp.float32) + parts_c[1].astype(jnp.float32) + parts_c[2].astype(jnp.float32)
    total_c = own_c + total_c * (1 / SCALE)
    b += [swap(total_c[:, :4], "occ", 6), swap(total_c[:, 4:], "occ", 7)]
    return update(place, mark, occ_energy, vir_energy, [(k, k, 0) for k in range(8)], [total_b] + b)


def plain(amplitudes, integrals, occ_energy, vir_energy):
    n_occ = lax.axis_size("occ")
    n_vir = lax.axis_size("vir")
    irreps, rows_dev = amplitudes.shape[:2]
    share = rows_dev // n_vir
    held = lax.all_gather(amplitudes, "occ", axis=1, tiled=True)
    ladder = jnp.einsum("gic,gac->gia", held, integrals, preferred_element_type=jnp.float32)
    partial_cols = lax.psum_scatter(ladder, "vir", scatter_dimension=2, tiled=True)
    width = partial_cols.shape[2]
    moved = lax.all_to_all(partial_cols, "occ", split_axis=1, concat_axis=2, tiled=True)
    moved = lax.all_to_all(moved, "vir", split_axis=1, concat_axis=2, tiled=True)
    moved = moved.reshape(irreps, share, n_vir, n_occ, width)
    moved = jnp.transpose(moved, (0, 1, 3, 2, 4)).reshape(irreps, share, n_occ * n_vir * width)
    return moved / (occ_energy[:, :, None] + vir_energy[:, None, :])


def local(amplitudes, integrals, occ_energy, vir_energy):
    fits = lax.axis_size("occ") == 8 and lax.axis_size("vir") == 4 and amplitudes.shape[1] == 16
    if not fits:
        return plain(amplitudes, integrals, occ_energy, vir_energy)
    return paired(amplitudes, integrals, occ_energy, vir_energy)


def solution(mesh):
    placed = (P(None, "occ", "vir"), P(None, "occ", "vir"), P(None, ("occ", "vir")), P())
    return jax.shard_map(
        local, mesh=mesh, in_specs=placed, out_specs=P(None, ("occ", "vir"), None), check_vma=False
    )
```

time: 49.5 us -> 42.7 us (0.86)
  waiting for transfers between devices: 26.4 us -> 12 us
  starting transfers between devices: 15.8 us -> 22.6 us
  Pallas kernels: 3.45 us -> 7.48 us
  local copies, waits for them, and re-layouts: 3.35 us -> 0.18 us
    ppermute x17 -> x21, waiting for transfers between devices: 26.4 us -> 12 us  [swap(): lax.ppermute(x, axis, [(i, i ^ mask) for i in range(lax.axis_size(axis))])]
    ppermute x17 -> x21, starting transfers between devices: 15.8 us -> 22.6 us  [swap(): lax.ppermute(x, axis, [(i, i ^ mask) for i in range(lax.axis_size(axis))])]
    unnamed x9 -> x8, local copies, waits for them, and re-layouts: 3.23 us -> 0.11 us
    pallas_call x0 -> x1, Pallas kernels: none -> 2.21 us  [load(): pl.pallas_call(load_kernel, out_shape=(jax.ShapeDtypeStruct(integrals.sha...]
    pallas_call x1 -> x2, Pallas kernels: 2.05 us -> 3.87 us  [contract(): pl.pallas_call(functools.partial(contract_kernel, len(pieces)), out_shape...]
  transfers between devices with their start and end apart: 17 -> 21, of which waited for: 9 -> 9; matrix products, arithmetic and copies ran while one was open for 0% -> 1% of each run, Pallas kernels for 0% -> 14%
where the time goes in v2:
time: 42.7 us; the launch traced here: 42.6 us
  starting transfers between devices  22.6 us (53%)
  waiting for transfers between devices  12 us (28%)
  Pallas kernels  7.48 us (18%)
    ppermute x21, starting transfers between devices, swap(): lax.ppermute(x, axis, [(i, i ^ mask) for i in range(lax.axis_size(axis))])  22.6 us
    ppermute x21, waiting for transfers between devices, swap(): lax.ppermute(x, axis, [(i, i ^ mask) for i in range(lax.axis_size(axis))])  12 us
    pallas_call x2, Pallas kernels, contract(): pl.pallas_call(functools.partial(contract_kernel, len(pieces)), out_shape...  3.87 us
    pallas_call x1, Pallas kernels, load(): pl.pallas_call(load_kernel, out_shape=(jax.ShapeDtypeStruct(integrals.sha...  2.21 us
    pallas_call x1, Pallas kernels, update(): pl.pallas_call(functools.partial(update_kernel, masks), out_shape=jax.Sha...  1.39 us
  transfers between devices with their start and end apart: 21, of which 9 were waited for; matrix products, arithmetic and copies ran while one was open for 1% of the time, Pallas kernels for 14%

profile of v2, /device:TPU:0, one launch (start us, length us, event | category | flops | bytes accessed | tf_op | source)
XLA Modules:
  0.0 42.6 jit_solution(5897221762344441731)
XLA Ops:
  0.0 0.1 pad_add_fusion.place_ref
  0.1 2.9 %collective-permute-start = (bf16[8,16,1024]{2,1,0:T(8,128)(2,1)}, bf16[8,16,1024]{2,1,0:T(8,128)(2,1)S(1)}, u32[]{:S(2)}, u32[]{:S(2)}) collective-permute-start(bf16[8,16,1024]{2,1,0:T(8,128)(2,1)} %refs_0_), channel_id=1, source_target_pairs={{0,8},{4,12},{8,0},{12,4},{16,24},{20,28},{24,16},{28,20},{1,9},{5... | collective-permute-start | bytes 786440 | tf_op jit(solution)/shard_map/ppermute | solution.py:98
  3.0 1.5 %collective-permute-start.1 = (bf16[8,16,1024]{2,1,0:T(8,128)(2,1)}, bf16[8,16,1024]{2,1,0:T(8,128)(2,1)S(1)}, u32[]{:S(2)}, u32[]{:S(2)}) collective-permute-start(bf16[8,16,1024]{2,1,0:T(8,128)(2,1)} %refs_0_), channel_id=1, source_target_pairs={{0,16},{4,20},{8,24},{12,28},{16,0},{20,4},{24,8},{28,12},{1,17},{... | collective-permute-start | bytes 786440 | tf_op jit(solution)/shard_map/ppermute | solution.py:98
  4.5 0.0 collective-permute-start.2
  4.5 2.2 %shard_map.46 = (bf16[8,256,1024]{2,1,0:T(8,128)(2,1)S(1)}, f32[8,128]{1,0:T(8,128)S(1)}) custom-call(bf16[8,256,1024]{2,1,0:T(8,128)(2,1)} %int_ref.1), custom_call_target="tpu_custom_call" | custom-call | bytes 8388608 | tf_op jit(solution)/shard_map/pallas_call | solution.py:27
  6.8 2.8 %collective-permute-done.refs_2_ = bf16[8,16,1024]{2,1,0:T(8,128)(2,1)S(1)} collective-permute-done((bf16[8,16,1024]{2,1,0:T(8,128)(2,1)}, bf16[8,16,1024]{2,1,0:T(8,128)(2,1)S(1)}, u32[]{:S(2)}, u32[]{:S(2)}) %collective-permute-start) | collective-permute-done | bytes 262176 | tf_op jit(solution)/shard_map/ppermute | solution.py:98
  9.5 1.5 %collective-permute-done.1.refs_4_ = bf16[8,16,1024]{2,1,0:T(8,128)(2,1)S(1)} collective-permute-done((bf16[8,16,1024]{2,1,0:T(8,128)(2,1)}, bf16[8,16,1024]{2,1,0:T(8,128)(2,1)S(1)}, u32[]{:S(2)}, u32[]{:S(2)}) %collective-permute-start.1) | collective-permute-done | bytes 262176 | tf_op jit(solution)/shard_map/ppermute | solution.py:98
  11.0 0.5 %collective-permute-start.4 = (bf16[8,16,1024]{2,1,0:T(8,128)(2,1)S(1)}, bf16[8,16,1024]{2,1,0:T(8,128)(2,1)S(1)}, u32[]{:S(2)}, u32[]{:S(2)}) collective-permute-start(bf16[8,16,1024]{2,1,0:T(8,128)(2,1)S(1)} %collective-permute-done.1.refs_4_), channel_id=1, source_target_pairs={{0,4},{4,0},{8,12},{12,8},{16,20},{20,16},{24,28},{28,24},{1,5},{5... | collective-permute-start | bytes 786440 | tf_op jit(solution)/shard_map/ppermute | solution.py:98
  11.5 1.6 %collective-permute-start.5 = (bf16[4,16,1024]{2,1,0:T(8,128)(2,1)S(1)}, bf16[4,16,1024]{2,1,0:T(8,128)(2,1)S(1)}, u32[]{:S(2)}, u32[]{:S(2)}) collective-permute-start(bf16[4,16,1024]{2,1,0:T(8,128)(2,1)S(1)} %slice.52), channel_id=1, source_target_pairs={{0,16},{4,20},{8,24},{12,28},{16,0},{20,4},{24,8},{28,12},{1,17},{... | collective-permute-start | bytes 393224 | tf_op jit(solution)/shard_map/ppermute | solution.py:98
  13.1 0.5 %collective-permute-start.6 = (bf16[4,16,1024]{2,1,0:T(8,128)(2,1)S(1)}, bf16[4,16,1024]{2,1,0:T(8,128)(2,1)S(1)}, u32[]{:S(2)}, u32[]{:S(2)}) collective-permute-start(bf16[4,16,1024]{2,1,0:T(8,128)(2,1)S(1)} %slice.53), channel_id=1, source_target_pairs={{0,8},{4,12},{8,0},{12,4},{16,24},{20,28},{24,16},{28,20},{1,9},{5... | collective-permute-start | bytes 393224 | tf_op jit(solution)/shard_map/ppermute | solution.py:98
  13.7 0.0 collective-permute-done.2.refs_1_
  13.7 0.0 collective-permute-done.3.refs_3_
  13.7 0.0 collective-permute-done.4.refs_5_
  13.7 2.0 %shard_map.47 = (f32[4,8,24,256]{3,2,1,0:T(8,128)S(1)}, f32[8,128]{1,0:T(8,128)S(1)}) custom-call(s32[2]{0:T(128)S(1)} %pad_add_fusion.place_ref, f32[8,128]{1,0:T(8,128)S(1)} %get-tuple-element.24.seen_ref, bf16[8,16,1024]{2,1,0:T(8,128)(2,1)S(1)} %copy-done, bf16[8,16,1024]{2,1,0:T(8,128)(2,1)S(1)} %collective-permute-done.2.refs_1_, ...), custom_call_target="tpu_custom_call" | custom-call | flops 402653184 | bytes 6553600 | tf_op jit(solution)/shard_map/pallas_call | solution.py:60
  15.7 0.0 copy-start.2
  15.7 0.0 copy-start.1
  15.7 1.3 %collective-permute-done.5 = bf16[4,16,1024]{2,1,0:T(8,128)(2,1)S(1)} collective-permute-done((bf16[4,16,1024]{2,1,0:T(8,128)(2,1)S(1)}, bf16[4,16,1024]{2,1,0:T(8,128)(2,1)S(1)}, u32[]{:S(2)}, u32[]{:S(2)}) %collective-permute-start.5) | collective-permute-done | bytes 131104 | tf_op jit(solution)/shard_map/ppermute | solution.py:98
  17.0 1.2 %collective-permute-done.6 = bf16[4,16,1024]{2,1,0:T(8,128)(2,1)S(1)} collective-permute-done((bf16[4,16,1024]{2,1,0:T(8,128)(2,1)S(1)}, bf16[4,16,1024]{2,1,0:T(8,128)(2,1)S(1)}, u32[]{:S(2)}, u32[]{:S(2)}) %collective-permute-start.6) | collective-permute-done | bytes 131104 | tf_op jit(solution)/shard_map/ppermute | solution.py:98
  18.3 0.1 collective-permute-start.7
  18.4 0.1 fusion
  18.4 3.7 %collective-permute-start.10 = (f16[8,24,256]{2,1,0:T(8,128)(2,1)S(1)}, f16[8,24,256]{2,1,0:T(8,128)(2,1)S(1)}, u32[]{:S(2)}, u32[]{:S(2)}) collective-permute-start(f16[8,24,256]{2,1,0:T(8,128)(2,1)S(1)} %get-tuple-element.38), channel_id=1, source_target_pairs={{0,3},{1,2},{2,1},{3,0},{4,7},{5,6},{6,5},{7,4},{8,11},{9,10},{10,... | collective-permute-start | bytes 294920 | tf_op jit(solution)/shard_map/ppermute | solution.py:98
  22.1 0.0 collective-permute-start.8
  22.1 0.8 %collective-permute-start.9 = (f16[8,24,256]{2,1,0:T(8,128)(2,1)S(1)}, f16[8,24,256]{2,1,0:T(8,128)(2,1)S(1)}, u32[]{:S(2)}, u32[]{:S(2)}) collective-permute-start(f16[8,24,256]{2,1,0:T(8,128)(2,1)S(1)} %get-tuple-element.39), channel_id=1, source_target_pairs={{0,2},{1,3},{2,0},{3,1},{4,6},{5,7},{6,4},{7,5},{8,10},{9,11},{10,... | collective-permute-start | bytes 294920 | tf_op jit(solution)/shard_map/ppermute | solution.py:98
  22.9 0.0 collective-permute-done.7.refs_1_
  22.9 1.9 %shard_map.48 = (f32[4,8,8,256]{3,2,1,0:T(8,128)S(1)}, f32[8,128]{1,0:T(8,128)S(1)}) custom-call(s32[2]{0:T(128)S(1)} %pad_add_fusion.place_ref, f32[8,128]{1,0:T(8,128)S(1)} %get-tuple-element.30.seen_ref, bf16[8,16,1024]{2,1,0:T(8,128)(2,1)S(1)} %constant_dynamic-update-slice_fusion.refs_0_, bf16[8,16,1024]{2,1,0:T(8,128)(2,1)S(1)} %collective-permute-done.7.refs_1_, ...), custom_call_target="tpu_custom_call" | custom-call | flops 134217728 | bytes 4980736 | tf_op jit(solution)/shard_map/pallas_call | solution.py:60
  24.8 1.3 %collective-permute-start.16 = (f16[8,8,256]{2,1,0:T(8,128)(2,1)S(1)}, f16[8,8,256]{2,1,0:T(8,128)(2,1)S(1)}, u32[]{:S(2)}, u32[]{:S(2)}) collective-permute-start(f16[8,8,256]{2,1,0:T(8,128)(2,1)S(1)} %get-tuple-element.41), channel_id=1, source_target_pairs={{0,1},{1,0},{2,3},{3,2},{4,5},{5,4},{6,7},{7,6},{8,9},{9,8},{10,11... | collective-permute-start | bytes 98312 | tf_op jit(solution)/shard_map/ppermute | solution.py:98
  26.1 2.9 %collective-permute-start.17 = (f16[8,8,256]{2,1,0:T(8,128)(2,1)S(1)}, f16[8,8,256]{2,1,0:T(8,128)(2,1)S(1)}, u32[]{:S(2)}, u32[]{:S(2)}) collective-permute-start(f16[8,8,256]{2,1,0:T(8,128)(2,1)S(1)} %get-tuple-element.43), channel_id=1, source_target_pairs={{0,2},{1,3},{2,0},{3,1},{4,6},{5,7},{6,4},{7,5},{8,10},{9,11},{10,... | collective-permute-start | bytes 98312 | tf_op jit(solution)/shard_map/ppermute | solution.py:98
  29.0 0.5 %collective-permute-start.18 = (f16[8,8,256]{2,1,0:T(8,128)(2,1)S(1)}, f16[8,8,256]{2,1,0:T(8,128)(2,1)S(1)}, u32[]{:S(2)}, u32[]{:S(2)}) collective-permute-start(f16[8,8,256]{2,1,0:T(8,128)(2,1)S(1)} %get-tuple-element.42), channel_id=1, source_target_pairs={{0,3},{1,2},{2,1},{3,0},{4,7},{5,6},{6,5},{7,4},{8,11},{9,10},{10,... | collective-permute-start | bytes 98312 | tf_op jit(solution)/shard_map/ppermute | solution.py:98
  29.6 0.0 collective-permute-done.8
  29.6 2.5 %collective-permute-done.9 = f16[8,24,256]{2,1,0:T(8,128)(2,1)S(1)} collective-permute-done((f16[8,24,256]{2,1,0:T(8,128)(2,1)S(1)}, f16[8,24,256]{2,1,0:T(8,128)(2,1)S(1)}, u32[]{:S(2)}, u32[]{:S(2)}) %collective-permute-start.9) | collective-permute-done | bytes 98336 | tf_op jit(solution)/shard_map/ppermute | solution.py:98
  32.1 0.1 multiply_add_fusion.refs_0_
  32.2 0.1 collective-permute-start.11
  32.3 0.6 %collective-permute-start.12 = (f32[8,4,256]{2,1,0:T(4,128)S(1)}, f32[8,4,256]{2,1,0:T(4,128)S(1)}, u32[]{:S(2)}, u32[]{:S(2)}) collective-permute-start(f32[8,4,256]{2,1,0:T(4,128)S(1)} %get-tuple-element.47), channel_id=1, source_target_pairs={{0,8},{4,12},{8,0},{12,4},{16,24},{20,28},{24,16},{28,20},{1,9},{5... | collective-permute-start | bytes 98312 | tf_op jit(solution)/shard_map/ppermute | solution.py:98
  32.9 1.3 %collective-permute-start.13 = (f32[8,4,256]{2,1,0:T(4,128)S(1)}, f32[8,4,256]{2,1,0:T(4,128)S(1)}, u32[]{:S(2)}, u32[]{:S(2)}) collective-permute-start(f32[8,4,256]{2,1,0:T(4,128)S(1)} %get-tuple-element.46), channel_id=1, source_target_pairs={{0,12},{4,8},{8,4},{12,0},{16,28},{20,24},{24,20},{28,16},{1,13},{... | collective-permute-start | bytes 98312 | tf_op jit(solution)/shard_map/ppermute | solution.py:98
  34.2 0.0 collective-permute-done.17
  34.2 0.5 %collective-permute-start.14 = (f32[8,4,256]{2,1,0:T(4,128)S(1)}, f32[8,4,256]{2,1,0:T(4,128)S(1)}, u32[]{:S(2)}, u32[]{:S(2)}) collective-permute-start(f32[8,4,256]{2,1,0:T(4,128)S(1)} %get-tuple-element.45), channel_id=1, source_target_pairs={{0,16},{4,20},{8,24},{12,28},{16,0},{20,4},{24,8},{28,12},{1,17},{... | collective-permute-start | bytes 98312 | tf_op jit(solution)/shard_map/ppermute | solution.py:98
  34.7 0.1 collective-permute-done.18
  34.8 1.1 %collective-permute-start.15 = (f32[8,4,256]{2,1,0:T(4,128)S(1)}, f32[8,4,256]{2,1,0:T(4,128)S(1)}, u32[]{:S(2)}, u32[]{:S(2)}) collective-permute-start(f32[8,4,256]{2,1,0:T(4,128)S(1)} %get-tuple-element.44), channel_id=1, source_target_pairs={{0,20},{4,16},{8,28},{12,24},{16,4},{20,0},{24,12},{28,8},{1,21},{... | collective-permute-start | bytes 98312 | tf_op jit(solution)/shard_map/ppermute | solution.py:98
  35.9 0.5 %collective-permute-start.19 = (f32[8,4,256]{2,1,0:T(4,128)S(1)}, f32[8,4,256]{2,1,0:T(4,128)S(1)}, u32[]{:S(2)}, u32[]{:S(2)}) collective-permute-start(f32[8,4,256]{2,1,0:T(4,128)S(1)} %get-tuple-element.50), channel_id=1, source_target_pairs={{0,24},{4,28},{8,16},{12,20},{16,8},{20,12},{24,0},{28,4},{1,25},{... | collective-permute-start | bytes 98312 | tf_op jit(solution)/shard_map/ppermute | solution.py:98
  36.5 0.1 collective-permute-done.12.refs_2_
  36.6 2.1 %collective-permute-start.20 = (f32[8,4,256]{2,1,0:T(4,128)S(1)}, f32[8,4,256]{2,1,0:T(4,128)S(1)}, u32[]{:S(2)}, u32[]{:S(2)}) collective-permute-start(f32[8,4,256]{2,1,0:T(4,128)S(1)} %get-tuple-element.49), channel_id=1, source_target_pairs={{0,28},{4,24},{8,20},{12,16},{16,12},{20,8},{24,4},{28,0},{1,29},{... | collective-permute-start | bytes 98312 | tf_op jit(solution)/shard_map/ppermute | solution.py:98
  38.7 0.1 copy.5.occ_ref
  38.8 0.0 collective-permute-done.13.refs_3_
  38.8 0.0 collective-permute-done.14.refs_4_
  38.8 0.0 collective-permute-done.15.refs_5_
  38.8 2.3 %collective-permute-done.19.refs_6_ = f32[8,4,256]{2,1,0:T(4,128)S(1)} collective-permute-done((f32[8,4,256]{2,1,0:T(4,128)S(1)}, f32[8,4,256]{2,1,0:T(4,128)S(1)}, u32[]{:S(2)}, u32[]{:S(2)}) %collective-permute-start.19) | collective-permute-done | bytes 32800 | tf_op jit(solution)/shard_map/ppermute | solution.py:98
  41.1 0.1 collective-permute-done.20.refs_7_
  41.2 1.4 %shard_map.49 = f32[8,4,2048]{2,1,0:T(4,128)} custom-call(s32[2]{0:T(128)S(1)} %pad_add_fusion.place_ref, f32[8,128]{1,0:T(8,128)S(1)} %get-tuple-element.34.seen_ref, f32[8,4]{1,0:T(8,128)S(1)} %copy.5.occ_ref, f32[8,2048]{1,0:T(8,128)S(1)} %copy-done.1, f32[8,24,256]{2,1,0:T(8,128)S(1)} %multiply_add_fusion.refs_0_, ...), custom_call_target="tpu_custom_call" | custom-call | tf_op jit(solution)/shard_map/pallas_call | solution.py:88
  (16 shorter events, 0.1 us)
Async XLA Ops:
  0.0 13.7 %copy-start = (bf16[8,16,1024]{2,1,0:T(8,128)(2,1)S(1)}, bf16[8,16,1024]{2,1,0:T(8,128)(2,1)}, u32[]{:S(2)}) copy-start(bf16[8,16,1024]{2,1,0:T(8,128)(2,1)} %refs_0_) | copy-start | bytes 786436
  0.1 9.5 %collective-permute-start = (bf16[8,16,1024]{2,1,0:T(8,128)(2,1)}, bf16[8,16,1024]{2,1,0:T(8,128)(2,1)S(1)}, u32[]{:S(2)}, u32[]{:S(2)}) collective-permute-start(bf16[8,16,1024]{2,1,0:T(8,128)(2,1)} %refs_0_), channel_id=1, source_target_pairs={{0,8},{4,12},{8,0},{12,4},{16,24},{20,28},{24,16},{28,20},{1,9},{5... | collective-permute-start | bytes 786440 | tf_op jit(solution)/shard_map/ppermute | solution.py:98
  3.0 8.0 %collective-permute-start.1 = (bf16[8,16,1024]{2,1,0:T(8,128)(2,1)}, bf16[8,16,1024]{2,1,0:T(8,128)(2,1)S(1)}, u32[]{:S(2)}, u32[]{:S(2)}) collective-permute-start(bf16[8,16,1024]{2,1,0:T(8,128)(2,1)} %refs_0_), channel_id=1, source_target_pairs={{0,16},{4,20},{8,24},{12,28},{16,0},{20,4},{24,8},{28,12},{1,17},{... | collective-permute-start | bytes 786440 | tf_op jit(solution)/shard_map/ppermute | solution.py:98
  4.5 9.1 %collective-permute-start.2 = (bf16[8,16,1024]{2,1,0:T(8,128)(2,1)}, bf16[8,16,1024]{2,1,0:T(8,128)(2,1)S(1)}, u32[]{:S(2)}, u32[]{:S(2)}) collective-permute-start(bf16[8,16,1024]{2,1,0:T(8,128)(2,1)} %refs_0_), channel_id=1, source_target_pairs={{0,4},{4,0},{8,12},{12,8},{16,20},{20,16},{24,28},{28,24},{1,5},{5... | collective-permute-start | bytes 786440 | tf_op jit(solution)/shard_map/ppermute | solution.py:98
  11.0 2.7 %collective-permute-start.3 = (bf16[8,16,1024]{2,1,0:T(8,128)(2,1)S(1)}, bf16[8,16,1024]{2,1,0:T(8,128)(2,1)S(1)}, u32[]{:S(2)}, u32[]{:S(2)}) collective-permute-start(bf16[8,16,1024]{2,1,0:T(8,128)(2,1)S(1)} %collective-permute-done.refs_2_), channel_id=1, source_target_pairs={{0,4},{4,0},{8,12},{12,8},{16,20},{20,16},{24,28},{28,24},{1,5},{5... | collective-permute-start | bytes 786440 | tf_op jit(solution)/shard_map/ppermute | solution.py:98
  11.0 2.7 %collective-permute-start.4 = (bf16[8,16,1024]{2,1,0:T(8,128)(2,1)S(1)}, bf16[8,16,1024]{2,1,0:T(8,128)(2,1)S(1)}, u32[]{:S(2)}, u32[]{:S(2)}) collective-permute-start(bf16[8,16,1024]{2,1,0:T(8,128)(2,1)S(1)} %collective-permute-done.1.refs_4_), channel_id=1, source_target_pairs={{0,4},{4,0},{8,12},{12,8},{16,20},{20,16},{24,28},{28,24},{1,5},{5... | collective-permute-start | bytes 786440 | tf_op jit(solution)/shard_map/ppermute | solution.py:98
  11.5 5.5 %collective-permute-start.5 = (bf16[4,16,1024]{2,1,0:T(8,128)(2,1)S(1)}, bf16[4,16,1024]{2,1,0:T(8,128)(2,1)S(1)}, u32[]{:S(2)}, u32[]{:S(2)}) collective-permute-start(bf16[4,16,1024]{2,1,0:T(8,128)(2,1)S(1)} %slice.52), channel_id=1, source_target_pairs={{0,16},{4,20},{8,24},{12,28},{16,0},{20,4},{24,8},{28,12},{1,17},{... | collective-permute-start | bytes 393224 | tf_op jit(solution)/shard_map/ppermute | solution.py:98
  13.1 5.1 %collective-permute-start.6 = (bf16[4,16,1024]{2,1,0:T(8,128)(2,1)S(1)}, bf16[4,16,1024]{2,1,0:T(8,128)(2,1)S(1)}, u32[]{:S(2)}, u32[]{:S(2)}) collective-permute-start(bf16[4,16,1024]{2,1,0:T(8,128)(2,1)S(1)} %slice.53), channel_id=1, source_target_pairs={{0,8},{4,12},{8,0},{12,4},{16,24},{20,28},{24,16},{28,20},{1,9},{5... | collective-permute-start | bytes 393224 | tf_op jit(solution)/shard_map/ppermute | solution.py:98
  15.7 23.0 %copy-start.2 = (f32[8,4]{0,1:T(4,128)S(1)}, f32[8,4]{0,1:T(4,128)}, u32[]{:S(2)}) copy-start(f32[8,4]{0,1:T(4,128)} %param.6) | copy-start | bytes 388
  15.7 25.5 %copy-start.1 = (f32[8,2048]{1,0:T(8,128)S(1)}, f32[8,2048]{1,0:T(8,128)}, u32[]{:S(2)}) copy-start(f32[8,2048]{1,0:T(8,128)} %vir_ref.1) | copy-start | bytes 196612
  18.3 4.6 %collective-permute-start.7 = (bf16[8,16,1024]{2,1,0:T(8,128)(2,1)S(1)}, bf16[8,16,1024]{2,1,0:T(8,128)(2,1)S(1)}, u32[]{:S(2)}, u32[]{:S(2)}) collective-permute-start(bf16[8,16,1024]{2,1,0:T(8,128)(2,1)S(1)} %constant_dynamic-update-slice_fusion.refs_0_), channel_id=1, source_target_pairs={{0,4},{4,0},{8,12},{12,8},{16,20},{20,16},{24,28},{28,24},{1,5},{5... | collective-permute-start | bytes 786440 | tf_op jit(solution)/shard_map/ppermute | solution.py:98
  18.4 10.6 %collective-permute-start.10 = (f16[8,24,256]{2,1,0:T(8,128)(2,1)S(1)}, f16[8,24,256]{2,1,0:T(8,128)(2,1)S(1)}, u32[]{:S(2)}, u32[]{:S(2)}) collective-permute-start(f16[8,24,256]{2,1,0:T(8,128)(2,1)S(1)} %get-tuple-element.38), channel_id=1, source_target_pairs={{0,3},{1,2},{2,1},{3,0},{4,7},{5,6},{6,5},{7,4},{8,11},{9,10},{10,... | collective-permute-start | bytes 294920 | tf_op jit(solution)/shard_map/ppermute | solution.py:98
  22.1 7.5 %collective-permute-start.8 = (f16[8,24,256]{2,1,0:T(8,128)(2,1)S(1)}, f16[8,24,256]{2,1,0:T(8,128)(2,1)S(1)}, u32[]{:S(2)}, u32[]{:S(2)}) collective-permute-start(f16[8,24,256]{2,1,0:T(8,128)(2,1)S(1)} %get-tuple-element.37), channel_id=1, source_target_pairs={{0,1},{1,0},{2,3},{3,2},{4,5},{5,4},{6,7},{7,6},{8,9},{9,8},{10,11... | collective-permute-start | bytes 294920 | tf_op jit(solution)/shard_map/ppermute | solution.py:98
  22.1 10.0 %collective-permute-start.9 = (f16[8,24,256]{2,1,0:T(8,128)(2,1)S(1)}, f16[8,24,256]{2,1,0:T(8,128)(2,1)S(1)}, u32[]{:S(2)}, u32[]{:S(2)}) collective-permute-start(f16[8,24,256]{2,1,0:T(8,128)(2,1)S(1)} %get-tuple-element.39), channel_id=1, source_target_pairs={{0,2},{1,3},{2,0},{3,1},{4,6},{5,7},{6,4},{7,5},{8,10},{9,11},{10,... | collective-permute-start | bytes 294920 | tf_op jit(solution)/shard_map/ppermute | solution.py:98
  24.8 8.1 %collective-permute-start.16 = (f16[8,8,256]{2,1,0:T(8,128)(2,1)S(1)}, f16[8,8,256]{2,1,0:T(8,128)(2,1)S(1)}, u32[]{:S(2)}, u32[]{:S(2)}) collective-permute-start(f16[8,8,256]{2,1,0:T(8,128)(2,1)S(1)} %get-tuple-element.41), channel_id=1, source_target_pairs={{0,1},{1,0},{2,3},{3,2},{4,5},{5,4},{6,7},{7,6},{8,9},{9,8},{10,11... | collective-permute-start | bytes 98312 | tf_op jit(solution)/shard_map/ppermute | solution.py:98
  26.1 8.1 %collective-permute-start.17 = (f16[8,8,256]{2,1,0:T(8,128)(2,1)S(1)}, f16[8,8,256]{2,1,0:T(8,128)(2,1)S(1)}, u32[]{:S(2)}, u32[]{:S(2)}) collective-permute-start(f16[8,8,256]{2,1,0:T(8,128)(2,1)S(1)} %get-tuple-element.43), channel_id=1, source_target_pairs={{0,2},{1,3},{2,0},{3,1},{4,6},{5,7},{6,4},{7,5},{8,10},{9,11},{10,... | collective-permute-start | bytes 98312 | tf_op jit(solution)/shard_map/ppermute | solution.py:98
  29.0 5.7 %collective-permute-start.18 = (f16[8,8,256]{2,1,0:T(8,128)(2,1)S(1)}, f16[8,8,256]{2,1,0:T(8,128)(2,1)S(1)}, u32[]{:S(2)}, u32[]{:S(2)}) collective-permute-start(f16[8,8,256]{2,1,0:T(8,128)(2,1)S(1)} %get-tuple-element.42), channel_id=1, source_target_pairs={{0,3},{1,2},{2,1},{3,0},{4,7},{5,6},{6,5},{7,4},{8,11},{9,10},{10,... | collective-permute-start | bytes 98312 | tf_op jit(solution)/shard_map/ppermute | solution.py:98
  32.2 3.7 %collective-permute-start.11 = (f32[8,4,256]{2,1,0:T(4,128)S(1)}, f32[8,4,256]{2,1,0:T(4,128)S(1)}, u32[]{:S(2)}, u32[]{:S(2)}) collective-permute-start(f32[8,4,256]{2,1,0:T(4,128)S(1)} %get-tuple-element.48), channel_id=1, source_target_pairs={{0,4},{4,0},{8,12},{12,8},{16,20},{20,16},{24,28},{28,24},{1,5},{5... | collective-permute-start | bytes 98312 | tf_op jit(solution)/shard_map/ppermute | solution.py:98
  32.3 4.3 %collective-permute-start.12 = (f32[8,4,256]{2,1,0:T(4,128)S(1)}, f32[8,4,256]{2,1,0:T(4,128)S(1)}, u32[]{:S(2)}, u32[]{:S(2)}) collective-permute-start(f32[8,4,256]{2,1,0:T(4,128)S(1)} %get-tuple-element.47), channel_id=1, source_target_pairs={{0,8},{4,12},{8,0},{12,4},{16,24},{20,28},{24,16},{28,20},{1,9},{5... | collective-permute-start | bytes 98312 | tf_op jit(solution)/shard_map/ppermute | solution.py:98
  32.9 5.9 %collective-permute-start.13 = (f32[8,4,256]{2,1,0:T(4,128)S(1)}, f32[8,4,256]{2,1,0:T(4,128)S(1)}, u32[]{:S(2)}, u32[]{:S(2)}) collective-permute-start(f32[8,4,256]{2,1,0:T(4,128)S(1)} %get-tuple-element.46), channel_id=1, source_target_pairs={{0,12},{4,8},{8,4},{12,0},{16,28},{20,24},{24,20},{28,16},{1,13},{... | collective-permute-start | bytes 98312 | tf_op jit(solution)/shard_map/ppermute | solution.py:98
  34.2 4.6 %collective-permute-start.14 = (f32[8,4,256]{2,1,0:T(4,128)S(1)}, f32[8,4,256]{2,1,0:T(4,128)S(1)}, u32[]{:S(2)}, u32[]{:S(2)}) collective-permute-start(f32[8,4,256]{2,1,0:T(4,128)S(1)} %get-tuple-element.45), channel_id=1, source_target_pairs={{0,16},{4,20},{8,24},{12,28},{16,0},{20,4},{24,8},{28,12},{1,17},{... | collective-permute-start | bytes 98312 | tf_op jit(solution)/shard_map/ppermute | solution.py:98
  34.8 4.0 %collective-permute-start.15 = (f32[8,4,256]{2,1,0:T(4,128)S(1)}, f32[8,4,256]{2,1,0:T(4,128)S(1)}, u32[]{:S(2)}, u32[]{:S(2)}) collective-permute-start(f32[8,4,256]{2,1,0:T(4,128)S(1)} %get-tuple-element.44), channel_id=1, source_target_pairs={{0,20},{4,16},{8,28},{12,24},{16,4},{20,0},{24,12},{28,8},{1,21},{... | collective-permute-start | bytes 98312 | tf_op jit(solution)/shard_map/ppermute | solution.py:98
  35.9 5.2 %collective-permute-start.19 = (f32[8,4,256]{2,1,0:T(4,128)S(1)}, f32[8,4,256]{2,1,0:T(4,128)S(1)}, u32[]{:S(2)}, u32[]{:S(2)}) collective-permute-start(f32[8,4,256]{2,1,0:T(4,128)S(1)} %get-tuple-element.50), channel_id=1, source_target_pairs={{0,24},{4,28},{8,16},{12,20},{16,8},{20,12},{24,0},{28,4},{1,25},{... | collective-permute-start | bytes 98312 | tf_op jit(solution)/shard_map/ppermute | solution.py:98
  36.6 4.6 %collective-permute-start.20 = (f32[8,4,256]{2,1,0:T(4,128)S(1)}, f32[8,4,256]{2,1,0:T(4,128)S(1)}, u32[]{:S(2)}, u32[]{:S(2)}) collective-permute-start(f32[8,4,256]{2,1,0:T(4,128)S(1)} %get-tuple-element.49), channel_id=1, source_target_pairs={{0,28},{4,24},{8,20},{12,16},{16,12},{20,8},{24,4},{28,0},{1,29},{... | collective-permute-start | bytes 98312 | tf_op jit(solution)/shard_map/ppermute | solution.py:98

commit v3 on v2

--- a/solution.py
+++ b/solution.py
@@ -35,17 +35,20 @@
     )(pltpu.with_memory_space_constraint(integrals, pltpu.HBM))
 
 
-def contract_kernel(blocks, place_ref, seen_ref, *refs):
-    amp_refs, int_ref, out_ref, mark_ref = refs[:blocks], refs[blocks], refs[blocks + 1], refs[blocks + 2]
+def contract_kernel(parts, blocks, place_ref, seen_ref, *refs):
+    amp_refs, int_ref, out_ref, mark_ref = refs[: parts * blocks], refs[-3], refs[-2], refs[-1]
     mark_ref[...] = jnp.zeros_like(mark_ref)
     vir = place_ref[0]
     upper = lax.broadcasted_iota(jnp.int32, (8, int_ref.shape[1]), 0) < 4
+    irreps = int_ref.shape[0] // parts
     for g in range(int_ref.shape[0]):
-        rows = jnp.concatenate([a[g] for a in amp_refs], axis=0)
+        held = amp_refs[g // irreps * blocks : (g // irreps + 1) * blocks]
+        rows = [a[g % irreps] for a in held]
+        rows = jnp.concatenate(rows, axis=0) if blocks > 1 else rows[0]
         sums = lax.dot_general(
             rows, int_ref[g], (((1,), (1,)), ((), ())), preferred_element_type=jnp.float32
         )
-        for pair in range(blocks // 2):
+        for pair in range(rows.shape[0] // 32):
             for half in range(2):
                 low = sums[32 * pair + 8 * half : 32 * pair + 8 * half + 8]
                 high = sums[32 * pair + 16 + 8 * half : 32 * pair + 24 + 8 * half]
@@ -54,11 +57,12 @@
                 out_ref[(2 * half + 1) ^ vir, g, at, :] = jnp.where(upper, pltpu.roll(low, 4, 0), high)
 
 
-def contract(place, seen, pieces, integrals):
+def contract(place, seen, pieces, integrals, parts=1):
     irreps, width, depth = integrals.shape
-    rows = 4 * len(pieces)
+    blocks = len(pieces) // parts
+    rows = sum(piece.shape[1] for piece in pieces[:blocks]) // 4
     return pl.pallas_call(
-        functools.partial(contract_kernel, len(pieces)),
+        functools.partial(contract_kernel, parts, blocks),
         out_shape=(jax.ShapeDtypeStruct((4, irreps, rows, width), jnp.float32), MARK),
         in_specs=[SMEM] + [VMEM] * (len(pieces) + 2),
         out_specs=(VMEM, VMEM),
@@ -99,7 +103,7 @@
 
 
 def reduced(own, sums, size):
-    pieces = [swap((sums[j] * SCALE).astype(jnp.float16), "vir", j) for j in range(1, size)]
+    pieces = [swap((sums[j] * SCALE).astype(jnp.float16), "vir", j) for j in (3, 1, 2)]
     total = pieces[0].astype(jnp.float32)
     for piece in pieces[1:]:
         total = total + piece.astype(jnp.float32)
@@ -115,24 +119,24 @@
     x = swap(amplitudes, "occ", 2)
     y = swap(amplitudes, "occ", 4)
     slab, mark = load(integrals)
-    source = amplitudes
-    x, y, mark = lax.optimization_barrier((x, y, mark))
-    d_low, d_high = swap(x[:half], "occ", 4), swap(y[half:], "occ", 2)
+    x, y, sib, mark = lax.optimization_barrier((x, y, sib, mark))
     x_sib, y_sib = swap(x, "occ", 1), swap(y, "occ", 1)
+    d_low = swap(jnp.concatenate([x[:half], x_sib[:half]], axis=1), "occ", 4)
+    d_high = swap(jnp.concatenate([y[half:], y_sib[half:]], axis=1), "occ", 2)
+    pieces, nd = [d_low, d_high], 2
     sums_b, mark = contract(place, mark, [amplitudes, sib, x, x_sib, y, y_sib], slab)
-    d_low, d_high, mark = lax.optimization_barrier((d_low, d_high, mark))
-    d = jnp.concatenate([d_low, d_high], axis=0)
-    d_sib = swap(d, "occ", 1)
-    sums_c, mark = contract(place, mark, [d, d_sib], slab)
+    *pieces, mark = lax.optimization_barrier((*pieces, mark))
+    sums_c, mark = contract(place, mark, pieces, slab, 2)
     own, mark = lax.optimization_barrier((sums_b[0], mark))
     total_b = reduced(own, sums_b, size)
+    back_x, back_y = swap(total_b[:, 8:16], "occ", 2), swap(total_b[:, 16:], "occ", 4)
     own_c = sums_c[0]
-    parts_c = [swap((sums_c[j] * SCALE).astype(jnp.float16), "vir", j) for j in range(1, size)]
-    b = [swap(p, "occ", k) for k, p in ((1, total_b[:, 4:8]), (2, total_b[:, 8:12]), (3, total_b[:, 12:16]), (4, total_b[:, 16:20]), (5, total_b[:, 20:24]))]
-    total_c = parts_c[0].astype(jnp.float32) + parts_c[1].astype(jnp.float32) + parts_c[2].astype(jnp.float32)
-    total_c = own_c + total_c * (1 / SCALE)
-    b += [swap(total_c[:, :4], "occ", 6), swap(total_c[:, 4:], "occ", 7)]
-    return update(place, mark, occ_energy, vir_energy, [(k, k, 0) for k in range(8)], [total_b] + b)
+    total_c = reduced(own_c, sums_c, size)
+    back_d = swap(total_c, "occ", 6)
+    odd = swap(jnp.concatenate([total_b[:, 4:8], back_x[:, 4:], back_y[:, 4:]], axis=1), "occ", 1)
+    odd_d = swap(back_d[:, 4:], "occ", 1)
+    masks = [(0, 0, 0), (1, 4, 0), (2, 1, 0), (3, 4, 4), (4, 2, 0), (5, 4, 8), (6, 3, 0), (7, 5, 0)]
+    return update(place, mark, occ_energy, vir_energy, masks, [total_b, back_x, back_y, back_d, odd, odd_d])
 
 
 def plain(amplitudes, integrals, occ_energy, vir_energy):

time: 42.7 us -> 39.8 us (0.932)
  starting transfers between devices: 22.6 us -> 20.3 us
  waiting for transfers between devices: 12 us -> 11.3 us
    ppermute x21 -> x18, starting transfers between devices: 22.6 us -> 20.3 us  [swap(): lax.ppermute(x, axis, [(i, i ^ mask) for i in range(lax.axis_size(axis))])]
    ppermute x21 -> x18, waiting for transfers between devices: 12 us -> 11.3 us  [swap(): lax.ppermute(x, axis, [(i, i ^ mask) for i in range(lax.axis_size(axis))])]
  transfers between devices with their start and end apart: 21 -> 18, of which waited for: 9 -> 9; matrix products, arithmetic and copies ran while one was open for 1% -> 1% of each run, Pallas kernels for 14% -> 15%
where the time goes in v3:
time: 39.8 us; the launch traced here: 39.7 us
  starting transfers between devices  20.3 us (51%)
  waiting for transfers between devices  11.3 us (28%)
  Pallas kernels  7.47 us (19%)
    ppermute x18, starting transfers between devices, swap(): lax.ppermute(x, axis, [(i, i ^ mask) for i in range(lax.axis_size(axis))])  20.3 us
    ppermute x18, waiting for transfers between devices, swap(): lax.ppermute(x, axis, [(i, i ^ mask) for i in range(lax.axis_size(axis))])  11.3 us
    pallas_call x2, Pallas kernels, contract(): pl.pallas_call(functools.partial(contract_kernel, parts, blocks), out_sha...  3.87 us
    pallas_call x1, Pallas kernels, load(): pl.pallas_call(load_kernel, out_shape=(jax.ShapeDtypeStruct(integrals.sha...  2.21 us
    pallas_call x1, Pallas kernels, update(): pl.pallas_call(functools.partial(update_kernel, masks), out_shape=jax.Sha...  1.39 us
  transfers between devices with their start and end apart: 18, of which 9 were waited for; matrix products, arithmetic and copies ran while one was open for 1% of the time, Pallas kernels for 15%

profile of v3, /device:TPU:0, one launch (start us, length us, event | category | flops | bytes accessed | tf_op | source)
XLA Modules:
  0.0 39.7 jit_solution(13611944280899774887)
XLA Ops:
  0.0 0.1 pad_add_fusion.place_ref
  0.1 2.9 %collective-permute-start = (bf16[8,16,1024]{2,1,0:T(8,128)(2,1)}, bf16[8,16,1024]{2,1,0:T(8,128)(2,1)S(1)}, u32[]{:S(2)}, u32[]{:S(2)}) collective-permute-start(bf16[8,16,1024]{2,1,0:T(8,128)(2,1)} %refs_0_), channel_id=1, source_target_pairs={{0,8},{4,12},{8,0},{12,4},{16,24},{20,28},{24,16},{28,20},{1,9},{5... | collective-permute-start | bytes 786440 | tf_op jit(solution)/shard_map/ppermute | solution.py:102
  3.0 1.5 %collective-permute-start.1 = (bf16[8,16,1024]{2,1,0:T(8,128)(2,1)}, bf16[8,16,1024]{2,1,0:T(8,128)(2,1)S(1)}, u32[]{:S(2)}, u32[]{:S(2)}) collective-permute-start(bf16[8,16,1024]{2,1,0:T(8,128)(2,1)} %refs_0_), channel_id=1, source_target_pairs={{0,16},{4,20},{8,24},{12,28},{16,0},{20,4},{24,8},{28,12},{1,17},{... | collective-permute-start | bytes 786440 | tf_op jit(solution)/shard_map/ppermute | solution.py:102
  4.5 0.0 collective-permute-start.2
  4.5 2.2 %shard_map.46 = (bf16[8,256,1024]{2,1,0:T(8,128)(2,1)S(1)}, f32[8,128]{1,0:T(8,128)S(1)}) custom-call(bf16[8,256,1024]{2,1,0:T(8,128)(2,1)} %int_ref.1), custom_call_target="tpu_custom_call" | custom-call | bytes 8388608 | tf_op jit(solution)/shard_map/pallas_call | solution.py:27
  6.8 2.8 %collective-permute-done.refs_2_ = bf16[8,16,1024]{2,1,0:T(8,128)(2,1)S(1)} collective-permute-done((bf16[8,16,1024]{2,1,0:T(8,128)(2,1)}, bf16[8,16,1024]{2,1,0:T(8,128)(2,1)S(1)}, u32[]{:S(2)}, u32[]{:S(2)}) %collective-permute-start) | collective-permute-done | bytes 262176 | tf_op jit(solution)/shard_map/ppermute | solution.py:102
  9.5 1.5 %collective-permute-done.1.refs_4_ = bf16[8,16,1024]{2,1,0:T(8,128)(2,1)S(1)} collective-permute-done((bf16[8,16,1024]{2,1,0:T(8,128)(2,1)}, bf16[8,16,1024]{2,1,0:T(8,128)(2,1)S(1)}, u32[]{:S(2)}, u32[]{:S(2)}) %collective-permute-start.1) | collective-permute-done | bytes 262176 | tf_op jit(solution)/shard_map/ppermute | solution.py:102
  11.0 0.0 collective-permute-done.2.refs_1_
  11.0 0.0 collective-permute-start.4
  11.0 0.5 %collective-permute-start.3 = (bf16[8,16,1024]{2,1,0:T(8,128)(2,1)S(1)}, bf16[8,16,1024]{2,1,0:T(8,128)(2,1)S(1)}, u32[]{:S(2)}, u32[]{:S(2)}) collective-permute-start(bf16[8,16,1024]{2,1,0:T(8,128)(2,1)S(1)} %collective-permute-done.refs_2_), channel_id=1, source_target_pairs={{0,4},{4,0},{8,12},{12,8},{16,20},{20,16},{24,28},{28,24},{1,5},{5... | collective-permute-start | bytes 786440 | tf_op jit(solution)/shard_map/ppermute | solution.py:102
  11.5 1.0 %collective-permute-done.4.refs_5_ = bf16[8,16,1024]{2,1,0:T(8,128)(2,1)S(1)} collective-permute-done((bf16[8,16,1024]{2,1,0:T(8,128)(2,1)S(1)}, bf16[8,16,1024]{2,1,0:T(8,128)(2,1)S(1)}, u32[]{:S(2)}, u32[]{:S(2)}) %collective-permute-start.4) | collective-permute-done | bytes 262176 | tf_op jit(solution)/shard_map/ppermute | solution.py:102
  12.6 0.4 %collective-permute-start.6 = (bf16[4,32,1024]{2,1,0:T(8,128)(2,1)S(1)}, bf16[4,32,1024]{2,1,0:T(8,128)(2,1)S(1)}, u32[]{:S(2)}, u32[]{:S(2)}) collective-permute-start(bf16[4,32,1024]{2,1,0:T(8,128)(2,1)S(1)} %pad_maximum_fusion.1), channel_id=1, source_target_pairs={{0,8},{4,12},{8,0},{12,4},{16,24},{20,28},{24,16},{28,20},{1,9},{5... | collective-permute-start | bytes 786440 | tf_op jit(solution)/shard_map/ppermute | solution.py:102
  13.0 0.0 collective-permute-done.3.refs_3_
  13.1 1.7 %collective-permute-start.5 = (bf16[4,32,1024]{2,1,0:T(8,128)(2,1)S(1)}, bf16[4,32,1024]{2,1,0:T(8,128)(2,1)S(1)}, u32[]{:S(2)}, u32[]{:S(2)}) collective-permute-start(bf16[4,32,1024]{2,1,0:T(8,128)(2,1)S(1)} %pad_maximum_fusion), channel_id=1, source_target_pairs={{0,16},{4,20},{8,24},{12,28},{16,0},{20,4},{24,8},{28,12},{1,17},{... | collective-permute-start | bytes 786440 | tf_op jit(solution)/shard_map/ppermute | solution.py:102
  14.8 0.0 copy-done
  14.8 2.0 %shard_map.47 = (f32[4,8,24,256]{3,2,1,0:T(8,128)S(1)}, f32[8,128]{1,0:T(8,128)S(1)}) custom-call(s32[2]{0:T(128)S(1)} %pad_add_fusion.place_ref, f32[8,128]{1,0:T(8,128)S(1)} %get-tuple-element.25.seen_ref, bf16[8,16,1024]{2,1,0:T(8,128)(2,1)S(1)} %copy-done, bf16[8,16,1024]{2,1,0:T(8,128)(2,1)S(1)} %collective-permute-done.2.refs_1_, ...), custom_call_target="tpu_custom_call" | custom-call | flops 402653184 | bytes 6553600 | tf_op jit(solution)/shard_map/pallas_call | solution.py:64
  16.8 0.0 copy-start.2
  16.8 0.0 copy-start.1
  16.8 0.1 fusion
  16.9 3.7 %collective-permute-start.7 = (f16[8,24,256]{2,1,0:T(8,128)(2,1)S(1)}, f16[8,24,256]{2,1,0:T(8,128)(2,1)S(1)}, u32[]{:S(2)}, u32[]{:S(2)}) collective-permute-start(f16[8,24,256]{2,1,0:T(8,128)(2,1)S(1)} %get-tuple-element.39), channel_id=1, source_target_pairs={{0,3},{1,2},{2,1},{3,0},{4,7},{5,6},{6,5},{7,4},{8,11},{9,10},{10,... | collective-permute-start | bytes 294920 | tf_op jit(solution)/shard_map/ppermute | solution.py:102
  20.6 0.0 collective-permute-start.8
  20.6 0.8 %collective-permute-start.9 = (f16[8,24,256]{2,1,0:T(8,128)(2,1)S(1)}, f16[8,24,256]{2,1,0:T(8,128)(2,1)S(1)}, u32[]{:S(2)}, u32[]{:S(2)}) collective-permute-start(f16[8,24,256]{2,1,0:T(8,128)(2,1)S(1)} %get-tuple-element.40), channel_id=1, source_target_pairs={{0,2},{1,3},{2,0},{3,1},{4,6},{5,7},{6,4},{7,5},{8,10},{9,11},{10,... | collective-permute-start | bytes 294920 | tf_op jit(solution)/shard_map/ppermute | solution.py:102
  21.4 0.0 collective-permute-done.6.refs_1_
  21.4 0.0 collective-permute-done.5.refs_0_
  21.4 1.9 %shard_map.48 = (f32[4,8,8,256]{3,2,1,0:T(8,128)S(1)}, f32[8,128]{1,0:T(8,128)S(1)}) custom-call(s32[2]{0:T(128)S(1)} %pad_add_fusion.place_ref, f32[8,128]{1,0:T(8,128)S(1)} %get-tuple-element.32.seen_ref, bf16[4,32,1024]{2,1,0:T(8,128)(2,1)S(1)} %collective-permute-done.5.refs_0_, bf16[4,32,1024]{2,1,0:T(8,128)(2,1)S(1)} %collective-permute-done.6.refs_1_, ...), custom_call_target="tpu_custom_call" | custom-call | flops 134217728 | bytes 4980736 | tf_op jit(solution)/shard_map/pallas_call | solution.py:64
  23.3 3.7 %collective-permute-start.12 = (f16[8,8,256]{2,1,0:T(8,128)(2,1)S(1)}, f16[8,8,256]{2,1,0:T(8,128)(2,1)S(1)}, u32[]{:S(2)}, u32[]{:S(2)}) collective-permute-start(f16[8,8,256]{2,1,0:T(8,128)(2,1)S(1)} %get-tuple-element.43), channel_id=1, source_target_pairs={{0,3},{1,2},{2,1},{3,0},{4,7},{5,6},{6,5},{7,4},{8,11},{9,10},{10,... | collective-permute-start | bytes 98312 | tf_op jit(solution)/shard_map/ppermute | solution.py:102
  27.0 0.0 collective-permute-start.13
  27.0 0.0 collective-permute-done.7
  27.0 0.8 %collective-permute-start.14 = (f16[8,8,256]{2,1,0:T(8,128)(2,1)S(1)}, f16[8,8,256]{2,1,0:T(8,128)(2,1)S(1)}, u32[]{:S(2)}, u32[]{:S(2)}) collective-permute-start(f16[8,8,256]{2,1,0:T(8,128)(2,1)S(1)} %get-tuple-element.44), channel_id=1, source_target_pairs={{0,2},{1,3},{2,0},{3,1},{4,6},{5,7},{6,4},{7,5},{8,10},{9,11},{10,... | collective-permute-start | bytes 98312 | tf_op jit(solution)/shard_map/ppermute | solution.py:102
  27.7 0.0 collective-permute-done.8
  27.7 2.1 %collective-permute-done.9 = f16[8,24,256]{2,1,0:T(8,128)(2,1)S(1)} collective-permute-done((f16[8,24,256]{2,1,0:T(8,128)(2,1)S(1)}, f16[8,24,256]{2,1,0:T(8,128)(2,1)S(1)}, u32[]{:S(2)}, u32[]{:S(2)}) %collective-permute-start.9) | collective-permute-done | bytes 98336 | tf_op jit(solution)/shard_map/ppermute | solution.py:102
  29.9 1.5 %collective-permute-start.10 = (f32[8,8,256]{2,1,0:T(8,128)S(1)}, f32[8,8,256]{2,1,0:T(8,128)S(1)}, u32[]{:S(2)}, u32[]{:S(2)}) collective-permute-start(f32[8,8,256]{2,1,0:T(8,128)S(1)} %get-tuple-element.47), channel_id=1, source_target_pairs={{0,8},{4,12},{8,0},{12,4},{16,24},{20,28},{24,16},{28,20},{1,9},{5... | collective-permute-start | bytes 196616 | tf_op jit(solution)/shard_map/ppermute | solution.py:102
  31.4 0.0 collective-permute-start.11
  31.4 0.0 collective-permute-done.12
  31.4 0.0 collective-permute-done.13
  31.4 0.3 collective-permute-done.14
  31.8 2.5 %collective-permute-start.15 = (f32[8,8,256]{2,1,0:T(8,128)S(1)}, f32[8,8,256]{2,1,0:T(8,128)S(1)}, u32[]{:S(2)}, u32[]{:S(2)}) collective-permute-start(f32[8,8,256]{2,1,0:T(8,128)S(1)} %bitcast_add_fusion), channel_id=1, source_target_pairs={{0,24},{4,28},{8,16},{12,20},{16,8},{20,12},{24,0},{28,4},{1,25},{... | collective-permute-start | bytes 196616 | tf_op jit(solution)/shard_map/ppermute | solution.py:102
  34.3 0.4 collective-permute-done.10.refs_1_
  34.7 1.0 %collective-permute-done.11.refs_2_ = f32[8,8,256]{2,1,0:T(8,128)S(1)} collective-permute-done((f32[8,8,256]{2,1,0:T(8,128)S(1)}, f32[8,8,256]{2,1,0:T(8,128)S(1)}, u32[]{:S(2)}, u32[]{:S(2)}) %collective-permute-start.11) | collective-permute-done | bytes 65568 | tf_op jit(solution)/shard_map/ppermute | solution.py:102
  35.7 0.1 collective-permute-start.16
  35.8 1.2 %collective-permute-done.15.refs_3_ = f32[8,8,256]{2,1,0:T(8,128)S(1)} collective-permute-done((f32[8,8,256]{2,1,0:T(8,128)S(1)}, f32[8,8,256]{2,1,0:T(8,128)S(1)}, u32[]{:S(2)}, u32[]{:S(2)}) %collective-permute-start.15) | collective-permute-done | bytes 65568 | tf_op jit(solution)/shard_map/ppermute | solution.py:102
  37.0 0.1 collective-permute-start.17
  37.1 0.0 copy-done.2
  37.1 0.1 copy.5.occ_ref
  37.2 1.1 %collective-permute-done.17.refs_5_ = f32[8,4,256]{2,1,0:T(4,128)S(1)} collective-permute-done((f32[8,4,256]{2,1,0:T(4,128)S(1)}, f32[8,4,256]{2,1,0:T(4,128)S(1)}, u32[]{:S(2)}, u32[]{:S(2)}) %collective-permute-start.17) | collective-permute-done | bytes 32800 | tf_op jit(solution)/shard_map/ppermute | solution.py:102
  38.3 0.0 collective-permute-done.16.refs_4_
  38.3 0.0 copy-done.1
  38.3 1.4 %shard_map.49 = f32[8,4,2048]{2,1,0:T(4,128)} custom-call(s32[2]{0:T(128)S(1)} %pad_add_fusion.place_ref, f32[8,128]{1,0:T(8,128)S(1)} %get-tuple-element.36.seen_ref, f32[8,4]{1,0:T(8,128)S(1)} %copy.5.occ_ref, f32[8,2048]{1,0:T(8,128)S(1)} %copy-done.1, f32[8,24,256]{2,1,0:T(8,128)S(1)} %multiply_add_fusion.refs_0_, ...), custom_call_target="tpu_custom_call" | custom-call | tf_op jit(solution)/shard_map/pallas_call | solution.py:92
  (16 shorter events, 0.2 us)
Async XLA Ops:
  0.0 14.8 %copy-start = (bf16[8,16,1024]{2,1,0:T(8,128)(2,1)S(1)}, bf16[8,16,1024]{2,1,0:T(8,128)(2,1)}, u32[]{:S(2)}) copy-start(bf16[8,16,1024]{2,1,0:T(8,128)(2,1)} %refs_0_) | copy-start | bytes 786436
  0.1 9.5 %collective-permute-start = (bf16[8,16,1024]{2,1,0:T(8,128)(2,1)}, bf16[8,16,1024]{2,1,0:T(8,128)(2,1)S(1)}, u32[]{:S(2)}, u32[]{:S(2)}) collective-permute-start(bf16[8,16,1024]{2,1,0:T(8,128)(2,1)} %refs_0_), channel_id=1, source_target_pairs={{0,8},{4,12},{8,0},{12,4},{16,24},{20,28},{24,16},{28,20},{1,9},{5... | collective-permute-start | bytes 786440 | tf_op jit(solution)/shard_map/ppermute | solution.py:102
  3.0 8.0 %collective-permute-start.1 = (bf16[8,16,1024]{2,1,0:T(8,128)(2,1)}, bf16[8,16,1024]{2,1,0:T(8,128)(2,1)S(1)}, u32[]{:S(2)}, u32[]{:S(2)}) collective-permute-start(bf16[8,16,1024]{2,1,0:T(8,128)(2,1)} %refs_0_), channel_id=1, source_target_pairs={{0,16},{4,20},{8,24},{12,28},{16,0},{20,4},{24,8},{28,12},{1,17},{... | collective-permute-start | bytes 786440 | tf_op jit(solution)/shard_map/ppermute | solution.py:102
  4.5 6.5 %collective-permute-start.2 = (bf16[8,16,1024]{2,1,0:T(8,128)(2,1)}, bf16[8,16,1024]{2,1,0:T(8,128)(2,1)S(1)}, u32[]{:S(2)}, u32[]{:S(2)}) collective-permute-start(bf16[8,16,1024]{2,1,0:T(8,128)(2,1)} %refs_0_), channel_id=1, source_target_pairs={{0,4},{4,0},{8,12},{12,8},{16,20},{20,16},{24,28},{28,24},{1,5},{5... | collective-permute-start | bytes 786440 | tf_op jit(solution)/shard_map/ppermute | solution.py:102
  11.0 1.5 %collective-permute-start.4 = (bf16[8,16,1024]{2,1,0:T(8,128)(2,1)S(1)}, bf16[8,16,1024]{2,1,0:T(8,128)(2,1)S(1)}, u32[]{:S(2)}, u32[]{:S(2)}) collective-permute-start(bf16[8,16,1024]{2,1,0:T(8,128)(2,1)S(1)} %collective-permute-done.1.refs_4_), channel_id=1, source_target_pairs={{0,4},{4,0},{8,12},{12,8},{16,20},{20,16},{24,28},{28,24},{1,5},{5... | collective-permute-start | bytes 786440 | tf_op jit(solution)/shard_map/ppermute | solution.py:102
  11.0 2.0 %collective-permute-start.3 = (bf16[8,16,1024]{2,1,0:T(8,128)(2,1)S(1)}, bf16[8,16,1024]{2,1,0:T(8,128)(2,1)S(1)}, u32[]{:S(2)}, u32[]{:S(2)}) collective-permute-start(bf16[8,16,1024]{2,1,0:T(8,128)(2,1)S(1)} %collective-permute-done.refs_2_), channel_id=1, source_target_pairs={{0,4},{4,0},{8,12},{12,8},{16,20},{20,16},{24,28},{28,24},{1,5},{5... | collective-permute-start | bytes 786440 | tf_op jit(solution)/shard_map/ppermute | solution.py:102
  12.6 8.8 %collective-permute-start.6 = (bf16[4,32,1024]{2,1,0:T(8,128)(2,1)S(1)}, bf16[4,32,1024]{2,1,0:T(8,128)(2,1)S(1)}, u32[]{:S(2)}, u32[]{:S(2)}) collective-permute-start(bf16[4,32,1024]{2,1,0:T(8,128)(2,1)S(1)} %pad_maximum_fusion.1), channel_id=1, source_target_pairs={{0,8},{4,12},{8,0},{12,4},{16,24},{20,28},{24,16},{28,20},{1,9},{5... | collective-permute-start | bytes 786440 | tf_op jit(solution)/shard_map/ppermute | solution.py:102
  13.1 8.3 %collective-permute-start.5 = (bf16[4,32,1024]{2,1,0:T(8,128)(2,1)S(1)}, bf16[4,32,1024]{2,1,0:T(8,128)(2,1)S(1)}, u32[]{:S(2)}, u32[]{:S(2)}) collective-permute-start(bf16[4,32,1024]{2,1,0:T(8,128)(2,1)S(1)} %pad_maximum_fusion), channel_id=1, source_target_pairs={{0,16},{4,20},{8,24},{12,28},{16,0},{20,4},{24,8},{28,12},{1,17},{... | collective-permute-start | bytes 786440 | tf_op jit(solution)/shard_map/ppermute | solution.py:102
  16.8 20.3 %copy-start.2 = (f32[8,4]{0,1:T(4,128)S(1)}, f32[8,4]{0,1:T(4,128)}, u32[]{:S(2)}) copy-start(f32[8,4]{0,1:T(4,128)} %param.6) | copy-start | bytes 388
  16.8 21.5 %copy-start.1 = (f32[8,2048]{1,0:T(8,128)S(1)}, f32[8,2048]{1,0:T(8,128)}, u32[]{:S(2)}) copy-start(f32[8,2048]{1,0:T(8,128)} %vir_ref.1) | copy-start | bytes 196612
  16.9 10.1 %collective-permute-start.7 = (f16[8,24,256]{2,1,0:T(8,128)(2,1)S(1)}, f16[8,24,256]{2,1,0:T(8,128)(2,1)S(1)}, u32[]{:S(2)}, u32[]{:S(2)}) collective-permute-start(f16[8,24,256]{2,1,0:T(8,128)(2,1)S(1)} %get-tuple-element.39), channel_id=1, source_target_pairs={{0,3},{1,2},{2,1},{3,0},{4,7},{5,6},{6,5},{7,4},{8,11},{9,10},{10,... | collective-permute-start | bytes 294920 | tf_op jit(solution)/shard_map/ppermute | solution.py:102
  20.6 7.2 %collective-permute-start.8 = (f16[8,24,256]{2,1,0:T(8,128)(2,1)S(1)}, f16[8,24,256]{2,1,0:T(8,128)(2,1)S(1)}, u32[]{:S(2)}, u32[]{:S(2)}) collective-permute-start(f16[8,24,256]{2,1,0:T(8,128)(2,1)S(1)} %get-tuple-element.41), channel_id=1, source_target_pairs={{0,1},{1,0},{2,3},{3,2},{4,5},{5,4},{6,7},{7,6},{8,9},{9,8},{10,11... | collective-permute-start | bytes 294920 | tf_op jit(solution)/shard_map/ppermute | solution.py:102
  20.6 9.2 %collective-permute-start.9 = (f16[8,24,256]{2,1,0:T(8,128)(2,1)S(1)}, f16[8,24,256]{2,1,0:T(8,128)(2,1)S(1)}, u32[]{:S(2)}, u32[]{:S(2)}) collective-permute-start(f16[8,24,256]{2,1,0:T(8,128)(2,1)S(1)} %get-tuple-element.40), channel_id=1, source_target_pairs={{0,2},{1,3},{2,0},{3,1},{4,6},{5,7},{6,4},{7,5},{8,10},{9,11},{10,... | collective-permute-start | bytes 294920 | tf_op jit(solution)/shard_map/ppermute | solution.py:102
  23.3 8.2 %collective-permute-start.12 = (f16[8,8,256]{2,1,0:T(8,128)(2,1)S(1)}, f16[8,8,256]{2,1,0:T(8,128)(2,1)S(1)}, u32[]{:S(2)}, u32[]{:S(2)}) collective-permute-start(f16[8,8,256]{2,1,0:T(8,128)(2,1)S(1)} %get-tuple-element.43), channel_id=1, source_target_pairs={{0,3},{1,2},{2,1},{3,0},{4,7},{5,6},{6,5},{7,4},{8,11},{9,10},{10,... | collective-permute-start | bytes 98312 | tf_op jit(solution)/shard_map/ppermute | solution.py:102
  27.0 4.5 %collective-permute-start.13 = (f16[8,8,256]{2,1,0:T(8,128)(2,1)S(1)}, f16[8,8,256]{2,1,0:T(8,128)(2,1)S(1)}, u32[]{:S(2)}, u32[]{:S(2)}) collective-permute-start(f16[8,8,256]{2,1,0:T(8,128)(2,1)S(1)} %get-tuple-element.45), channel_id=1, source_target_pairs={{0,1},{1,0},{2,3},{3,2},{4,5},{5,4},{6,7},{7,6},{8,9},{9,8},{10,11... | collective-permute-start | bytes 98312 | tf_op jit(solution)/shard_map/ppermute | solution.py:102
  27.0 4.8 %collective-permute-start.14 = (f16[8,8,256]{2,1,0:T(8,128)(2,1)S(1)}, f16[8,8,256]{2,1,0:T(8,128)(2,1)S(1)}, u32[]{:S(2)}, u32[]{:S(2)}) collective-permute-start(f16[8,8,256]{2,1,0:T(8,128)(2,1)S(1)} %get-tuple-element.44), channel_id=1, source_target_pairs={{0,2},{1,3},{2,0},{3,1},{4,6},{5,7},{6,4},{7,5},{8,10},{9,11},{10,... | collective-permute-start | bytes 98312 | tf_op jit(solution)/shard_map/ppermute | solution.py:102
  29.9 4.8 %collective-permute-start.10 = (f32[8,8,256]{2,1,0:T(8,128)S(1)}, f32[8,8,256]{2,1,0:T(8,128)S(1)}, u32[]{:S(2)}, u32[]{:S(2)}) collective-permute-start(f32[8,8,256]{2,1,0:T(8,128)S(1)} %get-tuple-element.47), channel_id=1, source_target_pairs={{0,8},{4,12},{8,0},{12,4},{16,24},{20,28},{24,16},{28,20},{1,9},{5... | collective-permute-start | bytes 196616 | tf_op jit(solution)/shard_map/ppermute | solution.py:102
  31.4 4.3 %collective-permute-start.11 = (f32[8,8,256]{2,1,0:T(8,128)S(1)}, f32[8,8,256]{2,1,0:T(8,128)S(1)}, u32[]{:S(2)}, u32[]{:S(2)}) collective-permute-start(f32[8,8,256]{2,1,0:T(8,128)S(1)} %get-tuple-element.46), channel_id=1, source_target_pairs={{0,16},{4,20},{8,24},{12,28},{16,0},{20,4},{24,8},{28,12},{1,17},{... | collective-permute-start | bytes 196616 | tf_op jit(solution)/shard_map/ppermute | solution.py:102
  31.8 5.2 %collective-permute-start.15 = (f32[8,8,256]{2,1,0:T(8,128)S(1)}, f32[8,8,256]{2,1,0:T(8,128)S(1)}, u32[]{:S(2)}, u32[]{:S(2)}) collective-permute-start(f32[8,8,256]{2,1,0:T(8,128)S(1)} %bitcast_add_fusion), channel_id=1, source_target_pairs={{0,24},{4,28},{8,16},{12,20},{16,8},{20,12},{24,0},{28,4},{1,25},{... | collective-permute-start | bytes 196616 | tf_op jit(solution)/shard_map/ppermute | solution.py:102
  35.7 2.6 %collective-permute-start.16 = (f32[8,12,256]{2,1,0:T(8,128)S(1)}, f32[8,12,256]{2,1,0:T(8,128)S(1)}, u32[]{:S(2)}, u32[]{:S(2)}) collective-permute-start(f32[8,12,256]{2,1,0:T(8,128)S(1)} %pad_maximum_fusion.2), channel_id=1, source_target_pairs={{0,4},{4,0},{8,12},{12,8},{16,20},{20,16},{24,28},{28,24},{1,5},{5... | collective-permute-start | bytes 294920 | tf_op jit(solution)/shard_map/ppermute | solution.py:102
  37.0 1.3 %collective-permute-start.17 = (f32[8,4,256]{2,1,0:T(4,128)S(1)}, f32[8,4,256]{2,1,0:T(4,128)S(1)}, u32[]{:S(2)}, u32[]{:S(2)}) collective-permute-start(f32[8,4,256]{2,1,0:T(4,128)S(1)} %slice.79), channel_id=1, source_target_pairs={{0,4},{4,0},{8,12},{12,8},{16,20},{20,16},{24,28},{28,24},{1,5},{5... | collective-permute-start | bytes 98312 | tf_op jit(solution)/shard_map/ppermute | solution.py:102

commit v4 on v2

v4 whole, which is shorter than its diff:
```python
import functools

import jax
import jax.numpy as jnp
from jax import lax
from jax.experimental import pallas as pl
from jax.experimental.pallas import tpu as pltpu
from jax.sharding import PartitionSpec as P

VMEM = pl.BlockSpec(memory_space=pltpu.VMEM)
SCALE = 64.0
SUMS = 16.0
MARK = jax.ShapeDtypeStruct((8, 128), jnp.float32)
PARAMS = pltpu.CompilerParams(vmem_limit_bytes=16 << 20)


def load_kernel(int_ref, slab_ref, mark_ref, sems):
    copies = [pltpu.make_async_copy(int_ref.at[g], slab_ref.at[g], sems.at[g]) for g in range(int_ref.shape[0])]
    for copy in copies:
        copy.start()
    for copy in copies:
        copy.wait()
    mark_ref[...] = jnp.zeros_like(mark_ref)


def load(integrals):
    return pl.pallas_call(
        load_kernel,
        out_shape=(jax.ShapeDtypeStruct(integrals.shape, integrals.dtype), MARK),
        in_specs=[pl.BlockSpec(memory_space=pl.ANY)],
        out_specs=(VMEM, VMEM),
        scratch_shapes=[pltpu.SemaphoreType.DMA((integrals.shape[0],))],
        compiler_params=PARAMS,
        cost_estimate=pl.CostEstimate(flops=0, bytes_accessed=4 * integrals.size, transcendentals=0),
    )(pltpu.with_memory_space_constraint(integrals, pltpu.HBM))


def contract_kernel(groups, seen_ref, *refs):
    int_ref, out_ref, mark_ref = refs[-3:]
    mark_ref[...] = jnp.zeros_like(mark_ref)
    irreps, width = int_ref.shape[:2]
    vir = lax.axis_index("vir")
    upper = lax.broadcasted_iota(jnp.int32, (8, width), 0) < 4
    for g in range(irreps):
        held = [refs[n] for n in groups[g * len(groups) // irreps]]
        rows = jnp.concatenate([a[g % a.shape[0]] for a in held], axis=0)
        sums = lax.dot_general(
            rows, int_ref[g], (((1,), (1,)), ((), ())), preferred_element_type=jnp.float32
        )
        for pair in range(rows.shape[0] // 32):
            for half in range(2):
                low = sums[32 * pair + 8 * half : 32 * pair + 8 * half + 8]
                high = sums[32 * pair + 16 + 8 * half : 32 * pair + 24 + 8 * half]
                at = pl.ds(8 * pair, 8)
                out_ref[(2 * half) ^ vir, g, at, :] = jnp.where(upper, low, pltpu.roll(high, 4, 0))
                out_ref[(2 * half + 1) ^ vir, g, at, :] = jnp.where(upper, pltpu.roll(low, 4, 0), high)


def contract(seen, pieces, integrals, groups):
    irreps, width, depth = integrals.shape
    rows = sum(pieces[n].shape[1] for n in groups[0]) // 4
    return pl.pallas_call(
        functools.partial(contract_kernel, groups),
        out_shape=(jax.ShapeDtypeStruct((4, irreps, rows, width), jnp.float32), MARK),
        in_specs=[VMEM] * (len(pieces) + 2),
        out_specs=(VMEM, VMEM),
        compiler_params=PARAMS,
        cost_estimate=pl.CostEstimate(
            flops=2 * irreps * 4 * rows * depth * width,
            bytes_accessed=2 * irreps * depth * (width + 4 * rows) + 16 * irreps * rows * width,
            transcendentals=0,
        ),
    )(seen, *pieces, integrals)


def update_kernel(slabs, seen_ref, occ_ref, vir_ref, *refs):
    out_ref = refs[-1]
    width = refs[0].shape[2]
    share = out_ref.shape[1]
    occ = lax.axis_index("occ")
    y, x, core = occ // 4, occ // 2 % 2, occ % 2
    chips = {"own": 2 * y + x, "next": 2 * x + 1 - y, "last": 2 * (1 - x) + y, "far": 3 - 2 * y - x}
    for chip, flip, n, first in slabs:
        owner = 2 * chips[chip] + (1 - core if flip else core)
        at = pl.ds(pl.multiple_of(owner * width, width), width)
        for g in range(out_ref.shape[0]):
            levels = occ_ref[g][:, None] + vir_ref[g, at][None, :]
            out_ref[g, :, at] = refs[n][g, first : first + share, :] / levels


def update(seen, occ_energy, vir_energy, slabs, pieces):
    irreps, share = occ_energy.shape
    return pl.pallas_call(
        functools.partial(update_kernel, slabs),
        out_shape=jax.ShapeDtypeStruct((irreps, share, vir_energy.shape[1]), jnp.float32),
        in_specs=[VMEM] * (3 + len(pieces)),
        out_specs=VMEM,
        compiler_params=PARAMS,
    )(seen, occ_energy, vir_energy, *pieces)


def swap(x, axis, mask):
    return lax.ppermute(x, axis, [(i, i ^ mask) for i in range(lax.axis_size(axis))])


def turn(x, step):
    ring = (0, 1, 3, 2)
    return lax.ppermute(
        x,
        "occ",
        [(2 * ring[r] + core, 2 * ring[(r + step) % 4] + core) for r in range(4) for core in range(2)],
    )


def reduced(own, sums, order):
    pieces = [swap((sums[j] * SCALE).astype(jnp.float16), "vir", j) for j in order]
    total = pieces[0].astype(jnp.float32)
    for piece in pieces[1:]:
        total = total + piece.astype(jnp.float32)
    return own + total * (1 / SCALE)


def paired(amplitudes, integrals, occ_energy, vir_energy):
    half = amplitudes.shape[0] // 2
    sib = swap(amplitudes, "occ", 1)
    last = turn(amplitudes, 1)
    nxt = turn(amplitudes, -1)
    slab, mark = load(integrals)
    last, nxt, sib, mark = lax.optimization_barrier((last, nxt, sib, mark))
    last_sib, nxt_sib = swap(last, "occ", 1), swap(nxt, "occ", 1)
    low = turn(jnp.concatenate([last[:half], last_sib[:half]], axis=1), 1)
    high = turn(jnp.concatenate([nxt[half:], nxt_sib[half:]], axis=1), -1)
    sums_b, mark = contract(mark, [amplitudes, sib, last, last_sib, nxt, nxt_sib], slab, [(0, 1, 2, 3, 4, 5)])
    low, high, mark = lax.optimization_barrier((low, high, mark))
    sums_c, mark = contract(mark, [low, high], slab, [(0,), (1,)])
    own, mark = lax.optimization_barrier((sums_b[0], mark))
    total_b = reduced(own, sums_b, (2, 3, 1))
    from_next = turn(total_b[:, 8:16], -1)
    from_last = turn(total_b[:, 16:24], 1)
    total_c = reduced(sums_c[0], sums_c, (2, 3, 1))
    from_far = swap((total_c * SUMS).astype(jnp.float16), "occ", 6).astype(jnp.float32) * (1 / SUMS)
    odd = swap(jnp.concatenate([total_b[:, 4:8], from_next[:, 4:], from_last[:, 4:]], axis=1), "occ", 1)
    odd_far = swap(from_far[:, 4:], "occ", 1)
    slabs = [("own", 0, 0, 0), ("own", 1, 4, 0), ("next", 0, 1, 0), ("next", 1, 4, 4), ("last", 0, 2, 0), ("last", 1, 4, 8), ("far", 0, 3, 0), ("far", 1, 5, 0)]
    return update(mark, occ_energy, vir_energy, slabs, [total_b, from_next, from_last, from_far, odd, odd_far])


def plain(amplitudes, integrals, occ_energy, vir_energy):
    n_occ = lax.axis_size("occ")
    n_vir = lax.axis_size("vir")
    irreps, rows_dev = amplitudes.shape[:2]
    share = rows_dev // n_vir
    held = lax.all_gather(amplitudes, "occ", axis=1, tiled=True)
    ladder = jnp.einsum("gic,gac->gia", held, integrals, preferred_element_type=jnp.float32)
    partial_cols = lax.psum_scatter(ladder, "vir", scatter_dimension=2, tiled=True)
    width = partial_cols.shape[2]
    moved = lax.all_to_all(partial_cols, "occ", split_axis=1, concat_axis=2, tiled=True)
    moved = lax.all_to_all(moved, "vir", split_axis=1, concat_axis=2, tiled=True)
    moved = moved.reshape(irreps, share, n_vir, n_occ, width)
    moved = jnp.transpose(moved, (0, 1, 3, 2, 4)).reshape(irreps, share, n_occ * n_vir * width)
    return moved / (occ_energy[:, :, None] + vir_energy[:, None, :])


def local(amplitudes, integrals, occ_energy, vir_energy):
    fits = lax.axis_size("occ") == 8 and lax.axis_size("vir") == 4 and amplitudes.shape[1] == 16
    if not fits:
        return plain(amplitudes, integrals, occ_energy, vir_energy)
    return paired(amplitudes, integrals, occ_energy, vir_energy)


def solution(mesh):
    placed = (P(None, "occ", "vir"), P(None, "occ", "vir"), P(None, ("occ", "vir")), P())
    return jax.shard_map(
        local, mesh=mesh, in_specs=placed, out_specs=P(None, ("occ", "vir"), None), check_vma=False
    )
```

time: 42.7 us -> 38.4 us (0.90)
  starting transfers between devices: 22.6 us -> 18.6 us
  Pallas kernels: 7.48 us -> 5.86 us
  waiting for transfers between devices: 12 us -> 13.2 us
    ppermute x21 -> x12, starting transfers between devices: 22.6 us -> 11.4 us  [swap(): lax.ppermute(x, axis, [(i, i ^ mask) for i in range(lax.axis_size(axis))])]
    ppermute x0 -> x6, starting transfers between devices: none -> 7.22 us  [turn(): lax.ppermute(x, 'occ', [(2 * ring[r] + core, 2 * ring[(r + step) % 4] + c...]
    ppermute x0 -> x6, waiting for transfers between devices: none -> 6.49 us  [turn(): lax.ppermute(x, 'occ', [(2 * ring[r] + core, 2 * ring[(r + step) % 4] + c...]
    ppermute x21 -> x12, waiting for transfers between devices: 12 us -> 6.7 us  [swap(): lax.ppermute(x, axis, [(i, i ^ mask) for i in range(lax.axis_size(axis))])]
    pallas_call x3, Pallas kernels: 5.26 us -> 3.64 us  [the longest x2 2.79 us: contract(): pl.pallas_call(functools.partial(contract_kernel, groups), out_shape=(jax...]
  transfers between devices with their start and end apart: 21 -> 18, of which waited for: 9 -> 10; matrix products, arithmetic and copies ran while one was open for 1% -> 1% of each run, Pallas kernels for 14% -> 13%
where the time goes in v4:
time: 38.4 us; the launch traced here: 38.3 us
  starting transfers between devices  18.6 us (48%)
  waiting for transfers between devices  13.2 us (34%)
  Pallas kernels  5.86 us (15%)
    ppermute x12, starting transfers between devices, swap(): lax.ppermute(x, axis, [(i, i ^ mask) for i in range(lax.axis_size(axis))])  11.4 us
    ppermute x6, starting transfers between devices, turn(): lax.ppermute(x, 'occ', [(2 * ring[r] + core, 2 * ring[(r + step) % 4] + c...  7.22 us
    ppermute x12, waiting for transfers between devices, swap(): lax.ppermute(x, axis, [(i, i ^ mask) for i in range(lax.axis_size(axis))])  6.7 us
    ppermute x6, waiting for transfers between devices, turn(): lax.ppermute(x, 'occ', [(2 * ring[r] + core, 2 * ring[(r + step) % 4] + c...  6.49 us
    pallas_call x2, Pallas kernels, contract(): pl.pallas_call(functools.partial(contract_kernel, groups), out_shape=(jax...  2.79 us
    pallas_call x1, Pallas kernels, load(): pl.pallas_call(load_kernel, out_shape=(jax.ShapeDtypeStruct(integrals.sha...  2.21 us
    pallas_call x1, Pallas kernels, update(): pl.pallas_call(functools.partial(update_kernel, slabs), out_shape=jax.Sha...  0.85 us
  transfers between devices with their start and end apart: 18, of which 10 were waited for; matrix products, arithmetic and copies ran while one was open for 1% of the time, Pallas kernels for 13%

profile of v4, /device:TPU:0, one launch (start us, length us, event | category | flops | bytes accessed | tf_op | source)
XLA Modules:
  0.0 38.3 jit_solution(3548132710951726900)
XLA Ops:
  0.0 0.0 copy-start
  0.0 2.9 %collective-permute-start = (bf16[8,16,1024]{2,1,0:T(8,128)(2,1)}, bf16[8,16,1024]{2,1,0:T(8,128)(2,1)S(1)}, u32[]{:S(2)}, u32[]{:S(2)}) collective-permute-start(bf16[8,16,1024]{2,1,0:T(8,128)(2,1)} %refs_0_.1), channel_id=1, source_target_pairs={{0,8},{4,12},{8,24},{12,28},{24,16},{28,20},{16,0},{20,4},{1,9},{5... | collective-permute-start | bytes 786440 | tf_op jit(solution)/shard_map/ppermute | solution.py:108
  2.9 0.1 collective-permute-start.1
  3.0 0.0 collective-permute-start.2
  3.0 2.2 %shard_map.46 = (bf16[8,256,1024]{2,1,0:T(8,128)(2,1)S(1)}, f32[8,128]{1,0:T(8,128)S(1)}) custom-call(bf16[8,256,1024]{2,1,0:T(8,128)(2,1)} %int_ref.1), custom_call_target="tpu_custom_call" | custom-call | bytes 8388608 | tf_op jit(solution)/shard_map/pallas_call | solution.py:27
  5.2 4.3 %collective-permute-done.refs_2_ = bf16[8,16,1024]{2,1,0:T(8,128)(2,1)S(1)} collective-permute-done((bf16[8,16,1024]{2,1,0:T(8,128)(2,1)}, bf16[8,16,1024]{2,1,0:T(8,128)(2,1)S(1)}, u32[]{:S(2)}, u32[]{:S(2)}) %collective-permute-start) | collective-permute-done | bytes 262176 | tf_op jit(solution)/shard_map/ppermute | solution.py:108
  9.6 1.4 %collective-permute-done.1.refs_4_ = bf16[8,16,1024]{2,1,0:T(8,128)(2,1)S(1)} collective-permute-done((bf16[8,16,1024]{2,1,0:T(8,128)(2,1)}, bf16[8,16,1024]{2,1,0:T(8,128)(2,1)S(1)}, u32[]{:S(2)}, u32[]{:S(2)}) %collective-permute-start.1) | collective-permute-done | bytes 262176 | tf_op jit(solution)/shard_map/ppermute | solution.py:108
  10.9 0.0 collective-permute-done.2.refs_1_
  10.9 0.0 collective-permute-start.4
  10.9 0.5 %collective-permute-start.3 = (bf16[8,16,1024]{2,1,0:T(8,128)(2,1)S(1)}, bf16[8,16,1024]{2,1,0:T(8,128)(2,1)S(1)}, u32[]{:S(2)}, u32[]{:S(2)}) collective-permute-start(bf16[8,16,1024]{2,1,0:T(8,128)(2,1)S(1)} %collective-permute-done.refs_2_), channel_id=1, source_target_pairs={{0,4},{4,0},{8,12},{12,8},{16,20},{20,16},{24,28},{28,24},{1,5},{5... | collective-permute-start | bytes 786440 | tf_op jit(solution)/shard_map/ppermute | solution.py:103
  11.5 1.0 %collective-permute-done.4.refs_5_ = bf16[8,16,1024]{2,1,0:T(8,128)(2,1)S(1)} collective-permute-done((bf16[8,16,1024]{2,1,0:T(8,128)(2,1)S(1)}, bf16[8,16,1024]{2,1,0:T(8,128)(2,1)S(1)}, u32[]{:S(2)}, u32[]{:S(2)}) %collective-permute-start.4) | collective-permute-done | bytes 262176 | tf_op jit(solution)/shard_map/ppermute | solution.py:103
  12.5 0.4 %collective-permute-start.6 = (bf16[4,32,1024]{2,1,0:T(8,128)(2,1)S(1)}, bf16[4,32,1024]{2,1,0:T(8,128)(2,1)S(1)}, u32[]{:S(2)}, u32[]{:S(2)}) collective-permute-start(bf16[4,32,1024]{2,1,0:T(8,128)(2,1)S(1)} %pad_maximum_fusion.1), channel_id=1, source_target_pairs={{0,16},{4,20},{8,0},{12,4},{24,8},{28,12},{16,24},{20,28},{1,17},{... | collective-permute-start | bytes 786440 | tf_op jit(solution)/shard_map/ppermute | solution.py:108
  12.9 0.0 collective-permute-done.3.refs_3_
  13.0 1.7 %collective-permute-start.5 = (bf16[4,32,1024]{2,1,0:T(8,128)(2,1)S(1)}, bf16[4,32,1024]{2,1,0:T(8,128)(2,1)S(1)}, u32[]{:S(2)}, u32[]{:S(2)}) collective-permute-start(bf16[4,32,1024]{2,1,0:T(8,128)(2,1)S(1)} %pad_maximum_fusion), channel_id=1, source_target_pairs={{0,8},{4,12},{8,24},{12,28},{24,16},{28,20},{16,0},{20,4},{1,9},{5... | collective-permute-start | bytes 786440 | tf_op jit(solution)/shard_map/ppermute | solution.py:108
  14.7 0.0 copy-done
  14.7 1.4 %shard_map.47 = (f32[4,8,24,256]{3,2,1,0:T(8,128)S(1)}, f32[8,128]{1,0:T(8,128)S(1)}) custom-call(f32[8,128]{1,0:T(8,128)S(1)} %get-tuple-element.21.seen_ref, bf16[8,16,1024]{2,1,0:T(8,128)(2,1)S(1)} %copy-done, bf16[8,16,1024]{2,1,0:T(8,128)(2,1)S(1)} %collective-permute-done.2.refs_1_, bf16[8,16,1024]{2,1,0:T(8,128)(2,1)S(1)} %collective-permute-done.refs_2_, ...), custom_call_target="tpu_custom_call" | custom-call | flops 402653184 | bytes 6553600 | tf_op jit(solution)/shard_map/pallas_call | solution.py:62
  16.1 0.0 copy-start.2
  16.1 0.0 copy-start.1
  16.2 0.1 fusion
  16.2 2.7 %collective-permute-start.7 = (f16[8,24,256]{2,1,0:T(8,128)(2,1)S(1)}, f16[8,24,256]{2,1,0:T(8,128)(2,1)S(1)}, u32[]{:S(2)}, u32[]{:S(2)}) collective-permute-start(f16[8,24,256]{2,1,0:T(8,128)(2,1)S(1)} %get-tuple-element.35), channel_id=1, source_target_pairs={{0,2},{1,3},{2,0},{3,1},{4,6},{5,7},{6,4},{7,5},{8,10},{9,11},{10,... | collective-permute-start | bytes 294920 | tf_op jit(solution)/shard_map/ppermute | solution.py:103
  18.9 1.3 %collective-permute-start.8 = (f16[8,24,256]{2,1,0:T(8,128)(2,1)S(1)}, f16[8,24,256]{2,1,0:T(8,128)(2,1)S(1)}, u32[]{:S(2)}, u32[]{:S(2)}) collective-permute-start(f16[8,24,256]{2,1,0:T(8,128)(2,1)S(1)} %get-tuple-element.37), channel_id=1, source_target_pairs={{0,3},{1,2},{2,1},{3,0},{4,7},{5,6},{6,5},{7,4},{8,11},{9,10},{10,... | collective-permute-start | bytes 294920 | tf_op jit(solution)/shard_map/ppermute | solution.py:103
  20.2 0.2 collective-permute-start.9
  20.5 0.4 %collective-permute-done.6.refs_1_ = bf16[4,32,1024]{2,1,0:T(8,128)(2,1)S(1)} collective-permute-done((bf16[4,32,1024]{2,1,0:T(8,128)(2,1)S(1)}, bf16[4,32,1024]{2,1,0:T(8,128)(2,1)S(1)}, u32[]{:S(2)}, u32[]{:S(2)}) %collective-permute-start.6) | collective-permute-done | bytes 262176 | tf_op jit(solution)/shard_map/ppermute | solution.py:108
  20.9 0.4 collective-permute-done.5.refs_0_
  21.3 1.3 %shard_map.48 = (f32[4,8,8,256]{3,2,1,0:T(8,128)S(1)}, f32[8,128]{1,0:T(8,128)S(1)}) custom-call(f32[8,128]{1,0:T(8,128)S(1)} %get-tuple-element.28.seen_ref, bf16[4,32,1024]{2,1,0:T(8,128)(2,1)S(1)} %collective-permute-done.5.refs_0_, bf16[4,32,1024]{2,1,0:T(8,128)(2,1)S(1)} %collective-permute-done.6.refs_1_, ...), custom_call_target="tpu_custom_call" | custom-call | flops 134217728 | bytes 4980736 | tf_op jit(solution)/shard_map/pallas_call | solution.py:62
  22.7 2.7 %collective-permute-start.12 = (f16[8,8,256]{2,1,0:T(8,128)(2,1)S(1)}, f16[8,8,256]{2,1,0:T(8,128)(2,1)S(1)}, u32[]{:S(2)}, u32[]{:S(2)}) collective-permute-start(f16[8,8,256]{2,1,0:T(8,128)(2,1)S(1)} %get-tuple-element.39), channel_id=1, source_target_pairs={{0,2},{1,3},{2,0},{3,1},{4,6},{5,7},{6,4},{7,5},{8,10},{9,11},{10,... | collective-permute-start | bytes 98312 | tf_op jit(solution)/shard_map/ppermute | solution.py:103
  25.3 1.3 %collective-permute-start.13 = (f16[8,8,256]{2,1,0:T(8,128)(2,1)S(1)}, f16[8,8,256]{2,1,0:T(8,128)(2,1)S(1)}, u32[]{:S(2)}, u32[]{:S(2)}) collective-permute-start(f16[8,8,256]{2,1,0:T(8,128)(2,1)S(1)} %get-tuple-element.41), channel_id=1, source_target_pairs={{0,3},{1,2},{2,1},{3,0},{4,7},{5,6},{6,5},{7,4},{8,11},{9,10},{10,... | collective-permute-start | bytes 98312 | tf_op jit(solution)/shard_map/ppermute | solution.py:103
  26.7 0.1 collective-permute-done.7
  26.8 0.1 collective-permute-start.14
  26.9 0.0 collective-permute-done.8
  26.9 0.0 collective-permute-done.9
  27.0 1.5 %collective-permute-start.10 = (f32[8,8,256]{2,1,0:T(8,128)S(1)}, f32[8,8,256]{2,1,0:T(8,128)S(1)}, u32[]{:S(2)}, u32[]{:S(2)}) collective-permute-start(f32[8,8,256]{2,1,0:T(8,128)S(1)} %get-tuple-element.43), channel_id=1, source_target_pairs={{0,16},{4,20},{8,0},{12,4},{24,8},{28,12},{16,24},{20,28},{1,17},{... | collective-permute-start | bytes 196616 | tf_op jit(solution)/shard_map/ppermute | solution.py:108
  28.5 0.6 %collective-permute-start.11 = (f32[8,8,256]{2,1,0:T(8,128)S(1)}, f32[8,8,256]{2,1,0:T(8,128)S(1)}, u32[]{:S(2)}, u32[]{:S(2)}) collective-permute-start(f32[8,8,256]{2,1,0:T(8,128)S(1)} %get-tuple-element.42), channel_id=1, source_target_pairs={{0,8},{4,12},{8,24},{12,28},{24,16},{28,20},{16,0},{20,4},{1,9},{5... | collective-permute-start | bytes 196616 | tf_op jit(solution)/shard_map/ppermute | solution.py:108
  29.1 0.8 %collective-permute-done.12 = f16[8,8,256]{2,1,0:T(8,128)(2,1)S(1)} collective-permute-done((f16[8,8,256]{2,1,0:T(8,128)(2,1)S(1)}, f16[8,8,256]{2,1,0:T(8,128)(2,1)S(1)}, u32[]{:S(2)}, u32[]{:S(2)}) %collective-permute-start.12) | collective-permute-done | bytes 32800 | tf_op jit(solution)/shard_map/ppermute | solution.py:103
  29.9 1.2 %collective-permute-done.13 = f16[8,8,256]{2,1,0:T(8,128)(2,1)S(1)} collective-permute-done((f16[8,8,256]{2,1,0:T(8,128)(2,1)S(1)}, f16[8,8,256]{2,1,0:T(8,128)(2,1)S(1)}, u32[]{:S(2)}, u32[]{:S(2)}) %collective-permute-start.13) | collective-permute-done | bytes 32800 | tf_op jit(solution)/shard_map/ppermute | solution.py:103
  31.2 0.0 collective-permute-done.14
  31.2 2.3 %collective-permute-start.15 = (f16[8,8,256]{2,1,0:T(8,128)(2,1)S(1)}, f16[8,8,256]{2,1,0:T(8,128)(2,1)S(1)}, u32[]{:S(2)}, u32[]{:S(2)}) collective-permute-start(f16[8,8,256]{2,1,0:T(8,128)(2,1)S(1)} %fusion.4), channel_id=1, source_target_pairs={{0,24},{4,28},{8,16},{12,20},{16,8},{20,12},{24,0},{28,4},{1,25},{... | collective-permute-start | bytes 98312 | tf_op jit(solution)/shard_map/ppermute | solution.py:103
  33.6 0.0 collective-permute-done.10.refs_1_
  33.6 0.0 collective-permute-done.11.refs_2_
  33.6 0.1 collective-permute-start.16
  33.7 2.4 %collective-permute-done.15 = f16[8,8,256]{2,1,0:T(8,128)(2,1)S(1)} collective-permute-done((f16[8,8,256]{2,1,0:T(8,128)(2,1)S(1)}, f16[8,8,256]{2,1,0:T(8,128)(2,1)S(1)}, u32[]{:S(2)}, u32[]{:S(2)}) %collective-permute-start.15) | collective-permute-done | bytes 32800 | tf_op jit(solution)/shard_map/ppermute | solution.py:103
  36.1 0.1 collective-permute-start.17
  36.2 0.0 copy-done.2
  36.2 0.1 copy.5.occ_ref
  36.3 1.1 %collective-permute-done.17.refs_5_ = f32[8,4,256]{2,1,0:T(4,128)S(1)} collective-permute-done((f32[8,4,256]{2,1,0:T(4,128)S(1)}, f32[8,4,256]{2,1,0:T(4,128)S(1)}, u32[]{:S(2)}, u32[]{:S(2)}) %collective-permute-start.17) | collective-permute-done | bytes 32800 | tf_op jit(solution)/shard_map/ppermute | solution.py:103
  37.4 0.0 collective-permute-done.16.refs_4_
  37.4 0.0 copy-done.1
  37.4 0.8 %shard_map.49 = f32[8,4,2048]{2,1,0:T(4,128)} custom-call(f32[8,128]{1,0:T(8,128)S(1)} %get-tuple-element.32.seen_ref, f32[8,4]{1,0:T(8,128)S(1)} %copy.5.occ_ref, f32[8,2048]{1,0:T(8,128)S(1)} %copy-done.1, f32[8,24,256]{2,1,0:T(8,128)S(1)} %multiply_add_fusion.refs_0_, f32[8,8,256]{2,1,0:T(8,128)S(1)} %collective-permute-done.10.refs_1_, ...), custom_call_target="tpu_custom_call" | custom-call | tf_op jit(solution)/shard_map/pallas_call | solution.py:93
  (16 shorter events, 0.3 us)
Async XLA Ops:
  0.0 14.7 %copy-start = (bf16[8,16,1024]{2,1,0:T(8,128)(2,1)S(1)}, bf16[8,16,1024]{2,1,0:T(8,128)(2,1)}, u32[]{:S(2)}) copy-start(bf16[8,16,1024]{2,1,0:T(8,128)(2,1)} %refs_0_.1) | copy-start | bytes 786436
  0.0 9.6 %collective-permute-start = (bf16[8,16,1024]{2,1,0:T(8,128)(2,1)}, bf16[8,16,1024]{2,1,0:T(8,128)(2,1)S(1)}, u32[]{:S(2)}, u32[]{:S(2)}) collective-permute-start(bf16[8,16,1024]{2,1,0:T(8,128)(2,1)} %refs_0_.1), channel_id=1, source_target_pairs={{0,8},{4,12},{8,24},{12,28},{24,16},{28,20},{16,0},{20,4},{1,9},{5... | collective-permute-start | bytes 786440 | tf_op jit(solution)/shard_map/ppermute | solution.py:108
  2.9 8.0 %collective-permute-start.1 = (bf16[8,16,1024]{2,1,0:T(8,128)(2,1)}, bf16[8,16,1024]{2,1,0:T(8,128)(2,1)S(1)}, u32[]{:S(2)}, u32[]{:S(2)}) collective-permute-start(bf16[8,16,1024]{2,1,0:T(8,128)(2,1)} %refs_0_.1), channel_id=1, source_target_pairs={{0,16},{4,20},{8,0},{12,4},{24,8},{28,12},{16,24},{20,28},{1,17},{... | collective-permute-start | bytes 786440 | tf_op jit(solution)/shard_map/ppermute | solution.py:108
  3.0 7.9 %collective-permute-start.2 = (bf16[8,16,1024]{2,1,0:T(8,128)(2,1)}, bf16[8,16,1024]{2,1,0:T(8,128)(2,1)S(1)}, u32[]{:S(2)}, u32[]{:S(2)}) collective-permute-start(bf16[8,16,1024]{2,1,0:T(8,128)(2,1)} %refs_0_.1), channel_id=1, source_target_pairs={{0,4},{4,0},{8,12},{12,8},{16,20},{20,16},{24,28},{28,24},{1,5},{5... | collective-permute-start | bytes 786440 | tf_op jit(solution)/shard_map/ppermute | solution.py:103
  10.9 1.5 %collective-permute-start.4 = (bf16[8,16,1024]{2,1,0:T(8,128)(2,1)S(1)}, bf16[8,16,1024]{2,1,0:T(8,128)(2,1)S(1)}, u32[]{:S(2)}, u32[]{:S(2)}) collective-permute-start(bf16[8,16,1024]{2,1,0:T(8,128)(2,1)S(1)} %collective-permute-done.1.refs_4_), channel_id=1, source_target_pairs={{0,4},{4,0},{8,12},{12,8},{16,20},{20,16},{24,28},{28,24},{1,5},{5... | collective-permute-start | bytes 786440 | tf_op jit(solution)/shard_map/ppermute | solution.py:103
  10.9 2.0 %collective-permute-start.3 = (bf16[8,16,1024]{2,1,0:T(8,128)(2,1)S(1)}, bf16[8,16,1024]{2,1,0:T(8,128)(2,1)S(1)}, u32[]{:S(2)}, u32[]{:S(2)}) collective-permute-start(bf16[8,16,1024]{2,1,0:T(8,128)(2,1)S(1)} %collective-permute-done.refs_2_), channel_id=1, source_target_pairs={{0,4},{4,0},{8,12},{12,8},{16,20},{20,16},{24,28},{28,24},{1,5},{5... | collective-permute-start | bytes 786440 | tf_op jit(solution)/shard_map/ppermute | solution.py:103
  12.5 8.4 %collective-permute-start.6 = (bf16[4,32,1024]{2,1,0:T(8,128)(2,1)S(1)}, bf16[4,32,1024]{2,1,0:T(8,128)(2,1)S(1)}, u32[]{:S(2)}, u32[]{:S(2)}) collective-permute-start(bf16[4,32,1024]{2,1,0:T(8,128)(2,1)S(1)} %pad_maximum_fusion.1), channel_id=1, source_target_pairs={{0,16},{4,20},{8,0},{12,4},{24,8},{28,12},{16,24},{20,28},{1,17},{... | collective-permute-start | bytes 786440 | tf_op jit(solution)/shard_map/ppermute | solution.py:108
  13.0 8.3 %collective-permute-start.5 = (bf16[4,32,1024]{2,1,0:T(8,128)(2,1)S(1)}, bf16[4,32,1024]{2,1,0:T(8,128)(2,1)S(1)}, u32[]{:S(2)}, u32[]{:S(2)}) collective-permute-start(bf16[4,32,1024]{2,1,0:T(8,128)(2,1)S(1)} %pad_maximum_fusion), channel_id=1, source_target_pairs={{0,8},{4,12},{8,24},{12,28},{24,16},{28,20},{16,0},{20,4},{1,9},{5... | collective-permute-start | bytes 786440 | tf_op jit(solution)/shard_map/ppermute | solution.py:108
  16.1 20.1 %copy-start.2 = (f32[8,4]{0,1:T(4,128)S(1)}, f32[8,4]{0,1:T(4,128)}, u32[]{:S(2)}) copy-start(f32[8,4]{0,1:T(4,128)} %param.6) | copy-start | bytes 388
  16.1 21.3 %copy-start.1 = (f32[8,2048]{1,0:T(8,128)S(1)}, f32[8,2048]{1,0:T(8,128)}, u32[]{:S(2)}) copy-start(f32[8,2048]{1,0:T(8,128)} %vir_ref.1) | copy-start | bytes 196612
  16.2 10.5 %collective-permute-start.7 = (f16[8,24,256]{2,1,0:T(8,128)(2,1)S(1)}, f16[8,24,256]{2,1,0:T(8,128)(2,1)S(1)}, u32[]{:S(2)}, u32[]{:S(2)}) collective-permute-start(f16[8,24,256]{2,1,0:T(8,128)(2,1)S(1)} %get-tuple-element.35), channel_id=1, source_target_pairs={{0,2},{1,3},{2,0},{3,1},{4,6},{5,7},{6,4},{7,5},{8,10},{9,11},{10,... | collective-permute-start | bytes 294920 | tf_op jit(solution)/shard_map/ppermute | solution.py:103
  18.9 8.0 %collective-permute-start.8 = (f16[8,24,256]{2,1,0:T(8,128)(2,1)S(1)}, f16[8,24,256]{2,1,0:T(8,128)(2,1)S(1)}, u32[]{:S(2)}, u32[]{:S(2)}) collective-permute-start(f16[8,24,256]{2,1,0:T(8,128)(2,1)S(1)} %get-tuple-element.37), channel_id=1, source_target_pairs={{0,3},{1,2},{2,1},{3,0},{4,7},{5,6},{6,5},{7,4},{8,11},{9,10},{10,... | collective-permute-start | bytes 294920 | tf_op jit(solution)/shard_map/ppermute | solution.py:103
  20.2 6.7 %collective-permute-start.9 = (f16[8,24,256]{2,1,0:T(8,128)(2,1)S(1)}, f16[8,24,256]{2,1,0:T(8,128)(2,1)S(1)}, u32[]{:S(2)}, u32[]{:S(2)}) collective-permute-start(f16[8,24,256]{2,1,0:T(8,128)(2,1)S(1)} %get-tuple-element.36), channel_id=1, source_target_pairs={{0,1},{1,0},{2,3},{3,2},{4,5},{5,4},{6,7},{7,6},{8,9},{9,8},{10,11... | collective-permute-start | bytes 294920 | tf_op jit(solution)/shard_map/ppermute | solution.py:103
  22.7 7.3 %collective-permute-start.12 = (f16[8,8,256]{2,1,0:T(8,128)(2,1)S(1)}, f16[8,8,256]{2,1,0:T(8,128)(2,1)S(1)}, u32[]{:S(2)}, u32[]{:S(2)}) collective-permute-start(f16[8,8,256]{2,1,0:T(8,128)(2,1)S(1)} %get-tuple-element.39), channel_id=1, source_target_pairs={{0,2},{1,3},{2,0},{3,1},{4,6},{5,7},{6,4},{7,5},{8,10},{9,11},{10,... | collective-permute-start | bytes 98312 | tf_op jit(solution)/shard_map/ppermute | solution.py:103
  25.3 5.9 %collective-permute-start.13 = (f16[8,8,256]{2,1,0:T(8,128)(2,1)S(1)}, f16[8,8,256]{2,1,0:T(8,128)(2,1)S(1)}, u32[]{:S(2)}, u32[]{:S(2)}) collective-permute-start(f16[8,8,256]{2,1,0:T(8,128)(2,1)S(1)} %get-tuple-element.41), channel_id=1, source_target_pairs={{0,3},{1,2},{2,1},{3,0},{4,7},{5,6},{6,5},{7,4},{8,11},{9,10},{10,... | collective-permute-start | bytes 98312 | tf_op jit(solution)/shard_map/ppermute | solution.py:103
  26.8 4.4 %collective-permute-start.14 = (f16[8,8,256]{2,1,0:T(8,128)(2,1)S(1)}, f16[8,8,256]{2,1,0:T(8,128)(2,1)S(1)}, u32[]{:S(2)}, u32[]{:S(2)}) collective-permute-start(f16[8,8,256]{2,1,0:T(8,128)(2,1)S(1)} %get-tuple-element.40), channel_id=1, source_target_pairs={{0,1},{1,0},{2,3},{3,2},{4,5},{5,4},{6,7},{7,6},{8,9},{9,8},{10,11... | collective-permute-start | bytes 98312 | tf_op jit(solution)/shard_map/ppermute | solution.py:103
  27.0 6.5 %collective-permute-start.10 = (f32[8,8,256]{2,1,0:T(8,128)S(1)}, f32[8,8,256]{2,1,0:T(8,128)S(1)}, u32[]{:S(2)}, u32[]{:S(2)}) collective-permute-start(f32[8,8,256]{2,1,0:T(8,128)S(1)} %get-tuple-element.43), channel_id=1, source_target_pairs={{0,16},{4,20},{8,0},{12,4},{24,8},{28,12},{16,24},{20,28},{1,17},{... | collective-permute-start | bytes 196616 | tf_op jit(solution)/shard_map/ppermute | solution.py:108
  28.5 5.0 %collective-permute-start.11 = (f32[8,8,256]{2,1,0:T(8,128)S(1)}, f32[8,8,256]{2,1,0:T(8,128)S(1)}, u32[]{:S(2)}, u32[]{:S(2)}) collective-permute-start(f32[8,8,256]{2,1,0:T(8,128)S(1)} %get-tuple-element.42), channel_id=1, source_target_pairs={{0,8},{4,12},{8,24},{12,28},{24,16},{28,20},{16,0},{20,4},{1,9},{5... | collective-permute-start | bytes 196616 | tf_op jit(solution)/shard_map/ppermute | solution.py:108
  31.2 4.9 %collective-permute-start.15 = (f16[8,8,256]{2,1,0:T(8,128)(2,1)S(1)}, f16[8,8,256]{2,1,0:T(8,128)(2,1)S(1)}, u32[]{:S(2)}, u32[]{:S(2)}) collective-permute-start(f16[8,8,256]{2,1,0:T(8,128)(2,1)S(1)} %fusion.4), channel_id=1, source_target_pairs={{0,24},{4,28},{8,16},{12,20},{16,8},{20,12},{24,0},{28,4},{1,25},{... | collective-permute-start | bytes 98312 | tf_op jit(solution)/shard_map/ppermute | solution.py:103
  33.6 3.8 %collective-permute-start.16 = (f32[8,12,256]{2,1,0:T(8,128)S(1)}, f32[8,12,256]{2,1,0:T(8,128)S(1)}, u32[]{:S(2)}, u32[]{:S(2)}) collective-permute-start(f32[8,12,256]{2,1,0:T(8,128)S(1)} %pad_maximum_fusion.2), channel_id=1, source_target_pairs={{0,4},{4,0},{8,12},{12,8},{16,20},{20,16},{24,28},{28,24},{1,5},{5... | collective-permute-start | bytes 294920 | tf_op jit(solution)/shard_map/ppermute | solution.py:103
  36.1 1.3 %collective-permute-start.17 = (f32[8,4,256]{2,1,0:T(4,128)S(1)}, f32[8,4,256]{2,1,0:T(4,128)S(1)}, u32[]{:S(2)}, u32[]{:S(2)}) collective-permute-start(f32[8,4,256]{2,1,0:T(4,128)S(1)} %slice.79), channel_id=1, source_target_pairs={{0,4},{4,0},{8,12},{12,8},{16,20},{20,16},{24,28},{28,24},{1,5},{5... | collective-permute-start | bytes 98312 | tf_op jit(solution)/shard_map/ppermute | solution.py:103

commit v5 on v4

--- a/solution.py
+++ b/solution.py
@@ -134,7 +134,7 @@
     low, high, mark = lax.optimization_barrier((low, high, mark))
     sums_c, mark = contract(mark, [low, high], slab, [(0,), (1,)])
     own, mark = lax.optimization_barrier((sums_b[0], mark))
-    total_b = reduced(own, sums_b, (2, 3, 1))
+    total_b = reduced(own, sums_b, (2, 1, 3))
     from_next = turn(total_b[:, 8:16], -1)
     from_last = turn(total_b[:, 16:24], 1)
     total_c = reduced(sums_c[0], sums_c, (2, 3, 1))

time: 38.4 us -> 38.2 us (level)
  waiting for transfers between devices: 13.2 us -> 12.6 us
  starting transfers between devices: 18.6 us -> 19.1 us
    ppermute x12, starting transfers between devices: 11.4 us -> 11.8 us  [swap(): lax.ppermute(x, axis, [(i, i ^ mask) for i in range(lax.axis_size(axis))])]
    ppermute x12, waiting for transfers between devices: 6.7 us -> 6.3 us  [swap(): lax.ppermute(x, axis, [(i, i ^ mask) for i in range(lax.axis_size(axis))])]
where the time goes in v5:
time: 38.2 us; the launch traced here: 38.1 us
  starting transfers between devices  19.1 us (50%)
  waiting for transfers between devices  12.6 us (33%)
  Pallas kernels  5.86 us (15%)
    ppermute x12, starting transfers between devices, swap(): lax.ppermute(x, axis, [(i, i ^ mask) for i in range(lax.axis_size(axis))])  11.8 us
    ppermute x6, starting transfers between devices, turn(): lax.ppermute(x, 'occ', [(2 * ring[r] + core, 2 * ring[(r + step) % 4] + c...  7.22 us
    ppermute x12, waiting for transfers between devices, swap(): lax.ppermute(x, axis, [(i, i ^ mask) for i in range(lax.axis_size(axis))])  6.3 us
    ppermute x6, waiting for transfers between devices, turn(): lax.ppermute(x, 'occ', [(2 * ring[r] + core, 2 * ring[(r + step) % 4] + c...  6.27 us
    pallas_call x2, Pallas kernels, contract(): pl.pallas_call(functools.partial(contract_kernel, groups), out_shape=(jax...  2.79 us
    pallas_call x1, Pallas kernels, load(): pl.pallas_call(load_kernel, out_shape=(jax.ShapeDtypeStruct(integrals.sha...  2.21 us
    pallas_call x1, Pallas kernels, update(): pl.pallas_call(functools.partial(update_kernel, slabs), out_shape=jax.Sha...  0.85 us
  transfers between devices with their start and end apart: 18, of which 10 were waited for; matrix products, arithmetic and copies ran while one was open for 1% of the time, Pallas kernels for 13%

profile of v5, /device:TPU:0, one launch (start us, length us, event | category | flops | bytes accessed | tf_op | source)
XLA Modules:
  0.0 38.1 jit_solution(13972232577401276303)
XLA Ops:
  0.0 0.0 copy-start
  0.0 2.9 %collective-permute-start = (bf16[8,16,1024]{2,1,0:T(8,128)(2,1)}, bf16[8,16,1024]{2,1,0:T(8,128)(2,1)S(1)}, u32[]{:S(2)}, u32[]{:S(2)}) collective-permute-start(bf16[8,16,1024]{2,1,0:T(8,128)(2,1)} %refs_0_.1), channel_id=1, source_target_pairs={{0,8},{4,12},{8,24},{12,28},{24,16},{28,20},{16,0},{20,4},{1,9},{5... | collective-permute-start | bytes 786440 | tf_op jit(solution)/shard_map/ppermute | solution.py:108
  2.9 0.1 collective-permute-start.1
  3.0 0.0 collective-permute-start.2
  3.0 2.2 %shard_map.46 = (bf16[8,256,1024]{2,1,0:T(8,128)(2,1)S(1)}, f32[8,128]{1,0:T(8,128)S(1)}) custom-call(bf16[8,256,1024]{2,1,0:T(8,128)(2,1)} %int_ref.1), custom_call_target="tpu_custom_call" | custom-call | bytes 8388608 | tf_op jit(solution)/shard_map/pallas_call | solution.py:27
  5.2 4.3 %collective-permute-done.refs_2_ = bf16[8,16,1024]{2,1,0:T(8,128)(2,1)S(1)} collective-permute-done((bf16[8,16,1024]{2,1,0:T(8,128)(2,1)}, bf16[8,16,1024]{2,1,0:T(8,128)(2,1)S(1)}, u32[]{:S(2)}, u32[]{:S(2)}) %collective-permute-start) | collective-permute-done | bytes 262176 | tf_op jit(solution)/shard_map/ppermute | solution.py:108
  9.6 1.4 %collective-permute-done.1.refs_4_ = bf16[8,16,1024]{2,1,0:T(8,128)(2,1)S(1)} collective-permute-done((bf16[8,16,1024]{2,1,0:T(8,128)(2,1)}, bf16[8,16,1024]{2,1,0:T(8,128)(2,1)S(1)}, u32[]{:S(2)}, u32[]{:S(2)}) %collective-permute-start.1) | collective-permute-done | bytes 262176 | tf_op jit(solution)/shard_map/ppermute | solution.py:108
  10.9 0.0 collective-permute-done.2.refs_1_
  10.9 0.0 collective-permute-start.4
  10.9 0.5 %collective-permute-start.3 = (bf16[8,16,1024]{2,1,0:T(8,128)(2,1)S(1)}, bf16[8,16,1024]{2,1,0:T(8,128)(2,1)S(1)}, u32[]{:S(2)}, u32[]{:S(2)}) collective-permute-start(bf16[8,16,1024]{2,1,0:T(8,128)(2,1)S(1)} %collective-permute-done.refs_2_), channel_id=1, source_target_pairs={{0,4},{4,0},{8,12},{12,8},{16,20},{20,16},{24,28},{28,24},{1,5},{5... | collective-permute-start | bytes 786440 | tf_op jit(solution)/shard_map/ppermute | solution.py:103
  11.5 1.0 %collective-permute-done.4.refs_5_ = bf16[8,16,1024]{2,1,0:T(8,128)(2,1)S(1)} collective-permute-done((bf16[8,16,1024]{2,1,0:T(8,128)(2,1)S(1)}, bf16[8,16,1024]{2,1,0:T(8,128)(2,1)S(1)}, u32[]{:S(2)}, u32[]{:S(2)}) %collective-permute-start.4) | collective-permute-done | bytes 262176 | tf_op jit(solution)/shard_map/ppermute | solution.py:103
  12.5 0.4 %collective-permute-start.6 = (bf16[4,32,1024]{2,1,0:T(8,128)(2,1)S(1)}, bf16[4,32,1024]{2,1,0:T(8,128)(2,1)S(1)}, u32[]{:S(2)}, u32[]{:S(2)}) collective-permute-start(bf16[4,32,1024]{2,1,0:T(8,128)(2,1)S(1)} %pad_maximum_fusion.1), channel_id=1, source_target_pairs={{0,16},{4,20},{8,0},{12,4},{24,8},{28,12},{16,24},{20,28},{1,17},{... | collective-permute-start | bytes 786440 | tf_op jit(solution)/shard_map/ppermute | solution.py:108
  12.9 0.0 collective-permute-done.3.refs_3_
  13.0 1.7 %collective-permute-start.5 = (bf16[4,32,1024]{2,1,0:T(8,128)(2,1)S(1)}, bf16[4,32,1024]{2,1,0:T(8,128)(2,1)S(1)}, u32[]{:S(2)}, u32[]{:S(2)}) collective-permute-start(bf16[4,32,1024]{2,1,0:T(8,128)(2,1)S(1)} %pad_maximum_fusion), channel_id=1, source_target_pairs={{0,8},{4,12},{8,24},{12,28},{24,16},{28,20},{16,0},{20,4},{1,9},{5... | collective-permute-start | bytes 786440 | tf_op jit(solution)/shard_map/ppermute | solution.py:108
  14.7 0.0 copy-done
  14.7 1.4 %shard_map.47 = (f32[4,8,24,256]{3,2,1,0:T(8,128)S(1)}, f32[8,128]{1,0:T(8,128)S(1)}) custom-call(f32[8,128]{1,0:T(8,128)S(1)} %get-tuple-element.21.seen_ref, bf16[8,16,1024]{2,1,0:T(8,128)(2,1)S(1)} %copy-done, bf16[8,16,1024]{2,1,0:T(8,128)(2,1)S(1)} %collective-permute-done.2.refs_1_, bf16[8,16,1024]{2,1,0:T(8,128)(2,1)S(1)} %collective-permute-done.refs_2_, ...), custom_call_target="tpu_custom_call" | custom-call | flops 402653184 | bytes 6553600 | tf_op jit(solution)/shard_map/pallas_call | solution.py:62
  16.1 0.0 copy-start.2
  16.1 0.0 copy-start.1
  16.2 0.1 fusion
  16.2 2.7 %collective-permute-start.7 = (f16[8,24,256]{2,1,0:T(8,128)(2,1)S(1)}, f16[8,24,256]{2,1,0:T(8,128)(2,1)S(1)}, u32[]{:S(2)}, u32[]{:S(2)}) collective-permute-start(f16[8,24,256]{2,1,0:T(8,128)(2,1)S(1)} %get-tuple-element.35), channel_id=1, source_target_pairs={{0,2},{1,3},{2,0},{3,1},{4,6},{5,7},{6,4},{7,5},{8,10},{9,11},{10,... | collective-permute-start | bytes 294920 | tf_op jit(solution)/shard_map/ppermute | solution.py:103
  18.9 1.6 %collective-permute-start.8 = (f16[8,24,256]{2,1,0:T(8,128)(2,1)S(1)}, f16[8,24,256]{2,1,0:T(8,128)(2,1)S(1)}, u32[]{:S(2)}, u32[]{:S(2)}) collective-permute-start(f16[8,24,256]{2,1,0:T(8,128)(2,1)S(1)} %get-tuple-element.37), channel_id=1, source_target_pairs={{0,1},{1,0},{2,3},{3,2},{4,5},{5,4},{6,7},{7,6},{8,9},{9,8},{10,11... | collective-permute-start | bytes 294920 | tf_op jit(solution)/shard_map/ppermute | solution.py:103
  20.5 0.2 collective-permute-start.9
  20.7 0.2 collective-permute-done.6.refs_1_
  20.9 0.4 collective-permute-done.5.refs_0_
  21.3 1.3 %shard_map.48 = (f32[4,8,8,256]{3,2,1,0:T(8,128)S(1)}, f32[8,128]{1,0:T(8,128)S(1)}) custom-call(f32[8,128]{1,0:T(8,128)S(1)} %get-tuple-element.28.seen_ref, bf16[4,32,1024]{2,1,0:T(8,128)(2,1)S(1)} %collective-permute-done.5.refs_0_, bf16[4,32,1024]{2,1,0:T(8,128)(2,1)S(1)} %collective-permute-done.6.refs_1_, ...), custom_call_target="tpu_custom_call" | custom-call | flops 134217728 | bytes 4980736 | tf_op jit(solution)/shard_map/pallas_call | solution.py:62
  22.7 2.7 %collective-permute-start.12 = (f16[8,8,256]{2,1,0:T(8,128)(2,1)S(1)}, f16[8,8,256]{2,1,0:T(8,128)(2,1)S(1)}, u32[]{:S(2)}, u32[]{:S(2)}) collective-permute-start(f16[8,8,256]{2,1,0:T(8,128)(2,1)S(1)} %get-tuple-element.39), channel_id=1, source_target_pairs={{0,2},{1,3},{2,0},{3,1},{4,6},{5,7},{6,4},{7,5},{8,10},{9,11},{10,... | collective-permute-start | bytes 98312 | tf_op jit(solution)/shard_map/ppermute | solution.py:103
  25.3 1.3 %collective-permute-start.13 = (f16[8,8,256]{2,1,0:T(8,128)(2,1)S(1)}, f16[8,8,256]{2,1,0:T(8,128)(2,1)S(1)}, u32[]{:S(2)}, u32[]{:S(2)}) collective-permute-start(f16[8,8,256]{2,1,0:T(8,128)(2,1)S(1)} %get-tuple-element.41), channel_id=1, source_target_pairs={{0,3},{1,2},{2,1},{3,0},{4,7},{5,6},{6,5},{7,4},{8,11},{9,10},{10,... | collective-permute-start | bytes 98312 | tf_op jit(solution)/shard_map/ppermute | solution.py:103
  26.7 0.0 collective-permute-done.7
  26.7 0.2 collective-permute-start.14
  26.9 0.0 collective-permute-done.8
  26.9 0.4 %collective-permute-done.9 = f16[8,24,256]{2,1,0:T(8,128)(2,1)S(1)} collective-permute-done((f16[8,24,256]{2,1,0:T(8,128)(2,1)S(1)}, f16[8,24,256]{2,1,0:T(8,128)(2,1)S(1)}, u32[]{:S(2)}, u32[]{:S(2)}) %collective-permute-start.9) | collective-permute-done | bytes 98336 | tf_op jit(solution)/shard_map/ppermute | solution.py:103
  27.4 1.2 %collective-permute-start.10 = (f32[8,8,256]{2,1,0:T(8,128)S(1)}, f32[8,8,256]{2,1,0:T(8,128)S(1)}, u32[]{:S(2)}, u32[]{:S(2)}) collective-permute-start(f32[8,8,256]{2,1,0:T(8,128)S(1)} %get-tuple-element.43), channel_id=1, source_target_pairs={{0,16},{4,20},{8,0},{12,4},{24,8},{28,12},{16,24},{20,28},{1,17},{... | collective-permute-start | bytes 196616 | tf_op jit(solution)/shard_map/ppermute | solution.py:108
  28.5 0.9 %collective-permute-start.11 = (f32[8,8,256]{2,1,0:T(8,128)S(1)}, f32[8,8,256]{2,1,0:T(8,128)S(1)}, u32[]{:S(2)}, u32[]{:S(2)}) collective-permute-start(f32[8,8,256]{2,1,0:T(8,128)S(1)} %get-tuple-element.42), channel_id=1, source_target_pairs={{0,8},{4,12},{8,24},{12,28},{24,16},{28,20},{16,0},{20,4},{1,9},{5... | collective-permute-start | bytes 196616 | tf_op jit(solution)/shard_map/ppermute | solution.py:108
  29.4 0.5 %collective-permute-done.12 = f16[8,8,256]{2,1,0:T(8,128)(2,1)S(1)} collective-permute-done((f16[8,8,256]{2,1,0:T(8,128)(2,1)S(1)}, f16[8,8,256]{2,1,0:T(8,128)(2,1)S(1)}, u32[]{:S(2)}, u32[]{:S(2)}) %collective-permute-start.12) | collective-permute-done | bytes 32800 | tf_op jit(solution)/shard_map/ppermute | solution.py:103
  29.9 1.1 %collective-permute-done.13 = f16[8,8,256]{2,1,0:T(8,128)(2,1)S(1)} collective-permute-done((f16[8,8,256]{2,1,0:T(8,128)(2,1)S(1)}, f16[8,8,256]{2,1,0:T(8,128)(2,1)S(1)}, u32[]{:S(2)}, u32[]{:S(2)}) %collective-permute-start.13) | collective-permute-done | bytes 32800 | tf_op jit(solution)/shard_map/ppermute | solution.py:103
  31.0 0.0 collective-permute-done.14
  31.1 2.5 %collective-permute-start.15 = (f16[8,8,256]{2,1,0:T(8,128)(2,1)S(1)}, f16[8,8,256]{2,1,0:T(8,128)(2,1)S(1)}, u32[]{:S(2)}, u32[]{:S(2)}) collective-permute-start(f16[8,8,256]{2,1,0:T(8,128)(2,1)S(1)} %fusion.4), channel_id=1, source_target_pairs={{0,24},{4,28},{8,16},{12,20},{16,8},{20,12},{24,0},{28,4},{1,25},{... | collective-permute-start | bytes 98312 | tf_op jit(solution)/shard_map/ppermute | solution.py:103
  33.6 0.0 collective-permute-done.10.refs_1_
  33.6 0.0 collective-permute-done.11.refs_2_
  33.6 0.1 collective-permute-start.16
  33.7 2.2 %collective-permute-done.15 = f16[8,8,256]{2,1,0:T(8,128)(2,1)S(1)} collective-permute-done((f16[8,8,256]{2,1,0:T(8,128)(2,1)S(1)}, f16[8,8,256]{2,1,0:T(8,128)(2,1)S(1)}, u32[]{:S(2)}, u32[]{:S(2)}) %collective-permute-start.15) | collective-permute-done | bytes 32800 | tf_op jit(solution)/shard_map/ppermute | solution.py:103
  36.0 0.1 collective-permute-start.17
  36.0 0.0 copy-done.2
  36.1 0.1 copy.5.occ_ref
  36.1 1.1 %collective-permute-done.17.refs_5_ = f32[8,4,256]{2,1,0:T(4,128)S(1)} collective-permute-done((f32[8,4,256]{2,1,0:T(4,128)S(1)}, f32[8,4,256]{2,1,0:T(4,128)S(1)}, u32[]{:S(2)}, u32[]{:S(2)}) %collective-permute-start.17) | collective-permute-done | bytes 32800 | tf_op jit(solution)/shard_map/ppermute | solution.py:103
  37.2 0.0 collective-permute-done.16.refs_4_
  37.2 0.0 copy-done.1
  37.2 0.8 %shard_map.49 = f32[8,4,2048]{2,1,0:T(4,128)} custom-call(f32[8,128]{1,0:T(8,128)S(1)} %get-tuple-element.32.seen_ref, f32[8,4]{1,0:T(8,128)S(1)} %copy.5.occ_ref, f32[8,2048]{1,0:T(8,128)S(1)} %copy-done.1, f32[8,24,256]{2,1,0:T(8,128)S(1)} %multiply_add_fusion.refs_0_, f32[8,8,256]{2,1,0:T(8,128)S(1)} %collective-permute-done.10.refs_1_, ...), custom_call_target="tpu_custom_call" | custom-call | tf_op jit(solution)/shard_map/pallas_call | solution.py:93
  (16 shorter events, 0.3 us)
Async XLA Ops:
  0.0 14.7 %copy-start = (bf16[8,16,1024]{2,1,0:T(8,128)(2,1)S(1)}, bf16[8,16,1024]{2,1,0:T(8,128)(2,1)}, u32[]{:S(2)}) copy-start(bf16[8,16,1024]{2,1,0:T(8,128)(2,1)} %refs_0_.1) | copy-start | bytes 786436
  0.0 9.6 %collective-permute-start = (bf16[8,16,1024]{2,1,0:T(8,128)(2,1)}, bf16[8,16,1024]{2,1,0:T(8,128)(2,1)S(1)}, u32[]{:S(2)}, u32[]{:S(2)}) collective-permute-start(bf16[8,16,1024]{2,1,0:T(8,128)(2,1)} %refs_0_.1), channel_id=1, source_target_pairs={{0,8},{4,12},{8,24},{12,28},{24,16},{28,20},{16,0},{20,4},{1,9},{5... | collective-permute-start | bytes 786440 | tf_op jit(solution)/shard_map/ppermute | solution.py:108
  2.9 8.0 %collective-permute-start.1 = (bf16[8,16,1024]{2,1,0:T(8,128)(2,1)}, bf16[8,16,1024]{2,1,0:T(8,128)(2,1)S(1)}, u32[]{:S(2)}, u32[]{:S(2)}) collective-permute-start(bf16[8,16,1024]{2,1,0:T(8,128)(2,1)} %refs_0_.1), channel_id=1, source_target_pairs={{0,16},{4,20},{8,0},{12,4},{24,8},{28,12},{16,24},{20,28},{1,17},{... | collective-permute-start | bytes 786440 | tf_op jit(solution)/shard_map/ppermute | solution.py:108
  3.0 7.9 %collective-permute-start.2 = (bf16[8,16,1024]{2,1,0:T(8,128)(2,1)}, bf16[8,16,1024]{2,1,0:T(8,128)(2,1)S(1)}, u32[]{:S(2)}, u32[]{:S(2)}) collective-permute-start(bf16[8,16,1024]{2,1,0:T(8,128)(2,1)} %refs_0_.1), channel_id=1, source_target_pairs={{0,4},{4,0},{8,12},{12,8},{16,20},{20,16},{24,28},{28,24},{1,5},{5... | collective-permute-start | bytes 786440 | tf_op jit(solution)/shard_map/ppermute | solution.py:103
  10.9 1.5 %collective-permute-start.4 = (bf16[8,16,1024]{2,1,0:T(8,128)(2,1)S(1)}, bf16[8,16,1024]{2,1,0:T(8,128)(2,1)S(1)}, u32[]{:S(2)}, u32[]{:S(2)}) collective-permute-start(bf16[8,16,1024]{2,1,0:T(8,128)(2,1)S(1)} %collective-permute-done.1.refs_4_), channel_id=1, source_target_pairs={{0,4},{4,0},{8,12},{12,8},{16,20},{20,16},{24,28},{28,24},{1,5},{5... | collective-permute-start | bytes 786440 | tf_op jit(solution)/shard_map/ppermute | solution.py:103
  10.9 2.0 %collective-permute-start.3 = (bf16[8,16,1024]{2,1,0:T(8,128)(2,1)S(1)}, bf16[8,16,1024]{2,1,0:T(8,128)(2,1)S(1)}, u32[]{:S(2)}, u32[]{:S(2)}) collective-permute-start(bf16[8,16,1024]{2,1,0:T(8,128)(2,1)S(1)} %collective-permute-done.refs_2_), channel_id=1, source_target_pairs={{0,4},{4,0},{8,12},{12,8},{16,20},{20,16},{24,28},{28,24},{1,5},{5... | collective-permute-start | bytes 786440 | tf_op jit(solution)/shard_map/ppermute | solution.py:103
  12.5 8.4 %collective-permute-start.6 = (bf16[4,32,1024]{2,1,0:T(8,128)(2,1)S(1)}, bf16[4,32,1024]{2,1,0:T(8,128)(2,1)S(1)}, u32[]{:S(2)}, u32[]{:S(2)}) collective-permute-start(bf16[4,32,1024]{2,1,0:T(8,128)(2,1)S(1)} %pad_maximum_fusion.1), channel_id=1, source_target_pairs={{0,16},{4,20},{8,0},{12,4},{24,8},{28,12},{16,24},{20,28},{1,17},{... | collective-permute-start | bytes 786440 | tf_op jit(solution)/shard_map/ppermute | solution.py:108
  13.0 8.3 %collective-permute-start.5 = (bf16[4,32,1024]{2,1,0:T(8,128)(2,1)S(1)}, bf16[4,32,1024]{2,1,0:T(8,128)(2,1)S(1)}, u32[]{:S(2)}, u32[]{:S(2)}) collective-permute-start(bf16[4,32,1024]{2,1,0:T(8,128)(2,1)S(1)} %pad_maximum_fusion), channel_id=1, source_target_pairs={{0,8},{4,12},{8,24},{12,28},{24,16},{28,20},{16,0},{20,4},{1,9},{5... | collective-permute-start | bytes 786440 | tf_op jit(solution)/shard_map/ppermute | solution.py:108
  16.1 19.9 %copy-start.2 = (f32[8,4]{0,1:T(4,128)S(1)}, f32[8,4]{0,1:T(4,128)}, u32[]{:S(2)}) copy-start(f32[8,4]{0,1:T(4,128)} %param.6) | copy-start | bytes 388
  16.1 21.1 %copy-start.1 = (f32[8,2048]{1,0:T(8,128)S(1)}, f32[8,2048]{1,0:T(8,128)}, u32[]{:S(2)}) copy-start(f32[8,2048]{1,0:T(8,128)} %vir_ref.1) | copy-start | bytes 196612
  16.2 10.4 %collective-permute-start.7 = (f16[8,24,256]{2,1,0:T(8,128)(2,1)S(1)}, f16[8,24,256]{2,1,0:T(8,128)(2,1)S(1)}, u32[]{:S(2)}, u32[]{:S(2)}) collective-permute-start(f16[8,24,256]{2,1,0:T(8,128)(2,1)S(1)} %get-tuple-element.35), channel_id=1, source_target_pairs={{0,2},{1,3},{2,0},{3,1},{4,6},{5,7},{6,4},{7,5},{8,10},{9,11},{10,... | collective-permute-start | bytes 294920 | tf_op jit(solution)/shard_map/ppermute | solution.py:103
  18.9 8.0 %collective-permute-start.8 = (f16[8,24,256]{2,1,0:T(8,128)(2,1)S(1)}, f16[8,24,256]{2,1,0:T(8,128)(2,1)S(1)}, u32[]{:S(2)}, u32[]{:S(2)}) collective-permute-start(f16[8,24,256]{2,1,0:T(8,128)(2,1)S(1)} %get-tuple-element.37), channel_id=1, source_target_pairs={{0,1},{1,0},{2,3},{3,2},{4,5},{5,4},{6,7},{7,6},{8,9},{9,8},{10,11... | collective-permute-start | bytes 294920 | tf_op jit(solution)/shard_map/ppermute | solution.py:103
  20.5 6.8 %collective-permute-start.9 = (f16[8,24,256]{2,1,0:T(8,128)(2,1)S(1)}, f16[8,24,256]{2,1,0:T(8,128)(2,1)S(1)}, u32[]{:S(2)}, u32[]{:S(2)}) collective-permute-start(f16[8,24,256]{2,1,0:T(8,128)(2,1)S(1)} %get-tuple-element.36), channel_id=1, source_target_pairs={{0,3},{1,2},{2,1},{3,0},{4,7},{5,6},{6,5},{7,4},{8,11},{9,10},{10,... | collective-permute-start | bytes 294920 | tf_op jit(solution)/shard_map/ppermute | solution.py:103
  22.7 7.3 %collective-permute-start.12 = (f16[8,8,256]{2,1,0:T(8,128)(2,1)S(1)}, f16[8,8,256]{2,1,0:T(8,128)(2,1)S(1)}, u32[]{:S(2)}, u32[]{:S(2)}) collective-permute-start(f16[8,8,256]{2,1,0:T(8,128)(2,1)S(1)} %get-tuple-element.39), channel_id=1, source_target_pairs={{0,2},{1,3},{2,0},{3,1},{4,6},{5,7},{6,4},{7,5},{8,10},{9,11},{10,... | collective-permute-start | bytes 98312 | tf_op jit(solution)/shard_map/ppermute | solution.py:103
  25.3 5.7 %collective-permute-start.13 = (f16[8,8,256]{2,1,0:T(8,128)(2,1)S(1)}, f16[8,8,256]{2,1,0:T(8,128)(2,1)S(1)}, u32[]{:S(2)}, u32[]{:S(2)}) collective-permute-start(f16[8,8,256]{2,1,0:T(8,128)(2,1)S(1)} %get-tuple-element.41), channel_id=1, source_target_pairs={{0,3},{1,2},{2,1},{3,0},{4,7},{5,6},{6,5},{7,4},{8,11},{9,10},{10,... | collective-permute-start | bytes 98312 | tf_op jit(solution)/shard_map/ppermute | solution.py:103
  26.7 4.4 %collective-permute-start.14 = (f16[8,8,256]{2,1,0:T(8,128)(2,1)S(1)}, f16[8,8,256]{2,1,0:T(8,128)(2,1)S(1)}, u32[]{:S(2)}, u32[]{:S(2)}) collective-permute-start(f16[8,8,256]{2,1,0:T(8,128)(2,1)S(1)} %get-tuple-element.40), channel_id=1, source_target_pairs={{0,1},{1,0},{2,3},{3,2},{4,5},{5,4},{6,7},{7,6},{8,9},{9,8},{10,11... | collective-permute-start | bytes 98312 | tf_op jit(solution)/shard_map/ppermute | solution.py:103
  27.4 6.2 %collective-permute-start.10 = (f32[8,8,256]{2,1,0:T(8,128)S(1)}, f32[8,8,256]{2,1,0:T(8,128)S(1)}, u32[]{:S(2)}, u32[]{:S(2)}) collective-permute-start(f32[8,8,256]{2,1,0:T(8,128)S(1)} %get-tuple-element.43), channel_id=1, source_target_pairs={{0,16},{4,20},{8,0},{12,4},{24,8},{28,12},{16,24},{20,28},{1,17},{... | collective-permute-start | bytes 196616 | tf_op jit(solution)/shard_map/ppermute | solution.py:108
  28.5 5.0 %collective-permute-start.11 = (f32[8,8,256]{2,1,0:T(8,128)S(1)}, f32[8,8,256]{2,1,0:T(8,128)S(1)}, u32[]{:S(2)}, u32[]{:S(2)}) collective-permute-start(f32[8,8,256]{2,1,0:T(8,128)S(1)} %get-tuple-element.42), channel_id=1, source_target_pairs={{0,8},{4,12},{8,24},{12,28},{24,16},{28,20},{16,0},{20,4},{1,9},{5... | collective-permute-start | bytes 196616 | tf_op jit(solution)/shard_map/ppermute | solution.py:108
  31.1 4.9 %collective-permute-start.15 = (f16[8,8,256]{2,1,0:T(8,128)(2,1)S(1)}, f16[8,8,256]{2,1,0:T(8,128)(2,1)S(1)}, u32[]{:S(2)}, u32[]{:S(2)}) collective-permute-start(f16[8,8,256]{2,1,0:T(8,128)(2,1)S(1)} %fusion.4), channel_id=1, source_target_pairs={{0,24},{4,28},{8,16},{12,20},{16,8},{20,12},{24,0},{28,4},{1,25},{... | collective-permute-start | bytes 98312 | tf_op jit(solution)/shard_map/ppermute | solution.py:103
  33.6 3.6 %collective-permute-start.16 = (f32[8,12,256]{2,1,0:T(8,128)S(1)}, f32[8,12,256]{2,1,0:T(8,128)S(1)}, u32[]{:S(2)}, u32[]{:S(2)}) collective-permute-start(f32[8,12,256]{2,1,0:T(8,128)S(1)} %pad_maximum_fusion.2), channel_id=1, source_target_pairs={{0,4},{4,0},{8,12},{12,8},{16,20},{20,16},{24,28},{28,24},{1,5},{5... | collective-permute-start | bytes 294920 | tf_op jit(solution)/shard_map/ppermute | solution.py:103
  36.0 1.3 %collective-permute-start.17 = (f32[8,4,256]{2,1,0:T(4,128)S(1)}, f32[8,4,256]{2,1,0:T(4,128)S(1)}, u32[]{:S(2)}, u32[]{:S(2)}) collective-permute-start(f32[8,4,256]{2,1,0:T(4,128)S(1)} %slice.79), channel_id=1, source_target_pairs={{0,4},{4,0},{8,12},{12,8},{16,20},{20,16},{24,28},{28,24},{1,5},{5... | collective-permute-start | bytes 98312 | tf_op jit(solution)/shard_map/ppermute | solution.py:103

commit v6 on v5

--- a/solution.py
+++ b/solution.py
@@ -35,17 +35,17 @@
     )(pltpu.with_memory_space_constraint(integrals, pltpu.HBM))
 
 
-def contract_kernel(groups, seen_ref, *refs):
+def contract_kernel(groups, start, seen_ref, *refs):
     int_ref, out_ref, mark_ref = refs[-3:]
     mark_ref[...] = jnp.zeros_like(mark_ref)
-    irreps, width = int_ref.shape[:2]
+    irreps, width = out_ref.shape[1], int_ref.shape[1]
     vir = lax.axis_index("vir")
     upper = lax.broadcasted_iota(jnp.int32, (8, width), 0) < 4
     for g in range(irreps):
         held = [refs[n] for n in groups[g * len(groups) // irreps]]
         rows = jnp.concatenate([a[g % a.shape[0]] for a in held], axis=0)
         sums = lax.dot_general(
-            rows, int_ref[g], (((1,), (1,)), ((), ())), preferred_element_type=jnp.float32
+            rows, int_ref[start + g], (((1,), (1,)), ((), ())), preferred_element_type=jnp.float32
         )
         for pair in range(rows.shape[0] // 32):
             for half in range(2):
@@ -56,11 +56,12 @@
                 out_ref[(2 * half + 1) ^ vir, g, at, :] = jnp.where(upper, pltpu.roll(low, 4, 0), high)
 
 
-def contract(seen, pieces, integrals, groups):
-    irreps, width, depth = integrals.shape
+def contract(seen, pieces, integrals, groups, start=0, irreps=None):
+    width, depth = integrals.shape[1:]
+    irreps = irreps or integrals.shape[0]
     rows = sum(pieces[n].shape[1] for n in groups[0]) // 4
     return pl.pallas_call(
-        functools.partial(contract_kernel, groups),
+        functools.partial(contract_kernel, groups, start),
         out_shape=(jax.ShapeDtypeStruct((4, irreps, rows, width), jnp.float32), MARK),
         in_specs=[VMEM] * (len(pieces) + 2),
         out_specs=(VMEM, VMEM),
@@ -131,8 +132,11 @@
     low = turn(jnp.concatenate([last[:half], last_sib[:half]], axis=1), 1)
     high = turn(jnp.concatenate([nxt[half:], nxt_sib[half:]], axis=1), -1)
     sums_b, mark = contract(mark, [amplitudes, sib, last, last_sib, nxt, nxt_sib], slab, [(0, 1, 2, 3, 4, 5)])
-    low, high, mark = lax.optimization_barrier((low, high, mark))
-    sums_c, mark = contract(mark, [low, high], slab, [(0,), (1,)])
+    low, mark = lax.optimization_barrier((low, mark))
+    sums_low, mark = contract(mark, [low], slab, [(0,)], 0, half)
+    high, mark = lax.optimization_barrier((high, mark))
+    sums_high, mark = contract(mark, [high], slab, [(0,)], half, half)
+    sums_c = [jnp.concatenate([sums_low[j], sums_high[j]], axis=0) for j in range(sums_low.shape[0])]
     own, mark = lax.optimization_barrier((sums_b[0], mark))
     total_b = reduced(own, sums_b, (2, 1, 3))
     from_next = turn(total_b[:, 8:16], -1)

time: 38.2 us -> 38.7 us (1.013)
  waiting for transfers between devices: 12.6 us -> 14.2 us
  starting transfers between devices: 19.1 us -> 17.7 us
    ppermute x12, waiting for transfers between devices: 6.3 us -> 7.7 us  [swap(): lax.ppermute(x, axis, [(i, i ^ mask) for i in range(lax.axis_size(axis))])]
    ppermute x12, starting transfers between devices: 11.8 us -> 10.5 us  [swap(): lax.ppermute(x, axis, [(i, i ^ mask) for i in range(lax.axis_size(axis))])]
    pallas_call x2 -> x3, Pallas kernels: 2.79 us -> 2.9 us  [contract(): pl.pallas_call(functools.partial(contract_kernel, groups, start), out_sha...]
  transfers between devices with their start and end apart: 18 -> 18, of which waited for: 10 -> 9; matrix products, arithmetic and copies ran while one was open for 1% -> 1% of each run, Pallas kernels for 13% -> 13%
where the time goes in v6:
time: 38.7 us; the launch traced here: 38.5 us
  starting transfers between devices  17.7 us (46%)
  waiting for transfers between devices  14.2 us (37%)
  Pallas kernels  5.96 us (15%)
    ppermute x12, starting transfers between devices, swap(): lax.ppermute(x, axis, [(i, i ^ mask) for i in range(lax.axis_size(axis))])  10.5 us
    ppermute x12, waiting for transfers between devices, swap(): lax.ppermute(x, axis, [(i, i ^ mask) for i in range(lax.axis_size(axis))])  7.7 us
    ppermute x6, starting transfers between devices, turn(): lax.ppermute(x, 'occ', [(2 * ring[r] + core, 2 * ring[(r + step) % 4] + c...  7.22 us
    ppermute x6, waiting for transfers between devices, turn(): lax.ppermute(x, 'occ', [(2 * ring[r] + core, 2 * ring[(r + step) % 4] + c...  6.5 us
    pallas_call x3, Pallas kernels, contract(): pl.pallas_call(functools.partial(contract_kernel, groups, start), out_sha...  2.9 us
    pallas_call x1, Pallas kernels, load(): pl.pallas_call(load_kernel, out_shape=(jax.ShapeDtypeStruct(integrals.sha...  2.21 us
    pallas_call x1, Pallas kernels, update(): pl.pallas_call(functools.partial(update_kernel, slabs), out_shape=jax.Sha...  0.85 us
  transfers between devices with their start and end apart: 18, of which 9 were waited for; matrix products, arithmetic and copies ran while one was open for 1% of the time, Pallas kernels for 13%

profile of v6, /device:TPU:0, one launch (start us, length us, event | category | flops | bytes accessed | tf_op | source)
XLA Modules:
  0.0 38.5 jit_solution(6817870072140167504)
XLA Ops:
  0.0 2.9 %collective-permute-start = (bf16[8,16,1024]{2,1,0:T(8,128)(2,1)}, bf16[8,16,1024]{2,1,0:T(8,128)(2,1)S(1)}, u32[]{:S(2)}, u32[]{:S(2)}) collective-permute-start(bf16[8,16,1024]{2,1,0:T(8,128)(2,1)} %refs_0_.1), channel_id=1, source_target_pairs={{0,8},{4,12},{8,24},{12,28},{24,16},{28,20},{16,0},{20,4},{1,9},{5... | collective-permute-start | bytes 786440 | tf_op jit(solution)/shard_map/ppermute | solution.py:109
  2.9 0.1 collective-permute-start.1
  3.0 0.0 collective-permute-start.2
  3.0 2.2 %shard_map.46 = (bf16[8,256,1024]{2,1,0:T(8,128)(2,1)S(1)}, f32[8,128]{1,0:T(8,128)S(1)}) custom-call(bf16[8,256,1024]{2,1,0:T(8,128)(2,1)} %int_ref.1), custom_call_target="tpu_custom_call" | custom-call | bytes 8388608 | tf_op jit(solution)/shard_map/pallas_call | solution.py:27
  5.2 4.3 %collective-permute-done.refs_2_ = bf16[8,16,1024]{2,1,0:T(8,128)(2,1)S(1)} collective-permute-done((bf16[8,16,1024]{2,1,0:T(8,128)(2,1)}, bf16[8,16,1024]{2,1,0:T(8,128)(2,1)S(1)}, u32[]{:S(2)}, u32[]{:S(2)}) %collective-permute-start) | collective-permute-done | bytes 262176 | tf_op jit(solution)/shard_map/ppermute | solution.py:109
  9.6 1.4 %collective-permute-done.1.refs_4_ = bf16[8,16,1024]{2,1,0:T(8,128)(2,1)S(1)} collective-permute-done((bf16[8,16,1024]{2,1,0:T(8,128)(2,1)}, bf16[8,16,1024]{2,1,0:T(8,128)(2,1)S(1)}, u32[]{:S(2)}, u32[]{:S(2)}) %collective-permute-start.1) | collective-permute-done | bytes 262176 | tf_op jit(solution)/shard_map/ppermute | solution.py:109
  10.9 0.0 collective-permute-done.2.refs_1_
  10.9 0.0 collective-permute-start.3
  10.9 0.5 %collective-permute-start.4 = (bf16[8,16,1024]{2,1,0:T(8,128)(2,1)S(1)}, bf16[8,16,1024]{2,1,0:T(8,128)(2,1)S(1)}, u32[]{:S(2)}, u32[]{:S(2)}) collective-permute-start(bf16[8,16,1024]{2,1,0:T(8,128)(2,1)S(1)} %collective-permute-done.1.refs_4_), channel_id=1, source_target_pairs={{0,4},{4,0},{8,12},{12,8},{16,20},{20,16},{24,28},{28,24},{1,5},{5... | collective-permute-start | bytes 786440 | tf_op jit(solution)/shard_map/ppermute | solution.py:104
  11.5 1.0 %collective-permute-done.3.refs_3_ = bf16[8,16,1024]{2,1,0:T(8,128)(2,1)S(1)} collective-permute-done((bf16[8,16,1024]{2,1,0:T(8,128)(2,1)S(1)}, bf16[8,16,1024]{2,1,0:T(8,128)(2,1)S(1)}, u32[]{:S(2)}, u32[]{:S(2)}) %collective-permute-start.3) | collective-permute-done | bytes 262176 | tf_op jit(solution)/shard_map/ppermute | solution.py:104
  12.5 1.6 %collective-permute-start.6 = (bf16[4,32,1024]{2,1,0:T(8,128)(2,1)S(1)}, bf16[4,32,1024]{2,1,0:T(8,128)(2,1)S(1)}, u32[]{:S(2)}, u32[]{:S(2)}) collective-permute-start(bf16[4,32,1024]{2,1,0:T(8,128)(2,1)S(1)} %pad_maximum_fusion.1), channel_id=1, source_target_pairs={{0,8},{4,12},{8,24},{12,28},{24,16},{28,20},{16,0},{20,4},{1,9},{5... | collective-permute-start | bytes 786440 | tf_op jit(solution)/shard_map/ppermute | solution.py:109
  14.1 0.0 collective-permute-done.4.refs_5_
  14.1 0.6 %collective-permute-start.5 = (bf16[4,32,1024]{2,1,0:T(8,128)(2,1)S(1)}, bf16[4,32,1024]{2,1,0:T(8,128)(2,1)S(1)}, u32[]{:S(2)}, u32[]{:S(2)}) collective-permute-start(bf16[4,32,1024]{2,1,0:T(8,128)(2,1)S(1)} %pad_maximum_fusion), channel_id=1, source_target_pairs={{0,16},{4,20},{8,0},{12,4},{24,8},{28,12},{16,24},{20,28},{1,17},{... | collective-permute-start | bytes 786440 | tf_op jit(solution)/shard_map/ppermute | solution.py:109
  14.7 0.0 copy-done
  14.7 1.4 %shard_map.47 = (f32[4,8,24,256]{3,2,1,0:T(8,128)S(1)}, f32[8,128]{1,0:T(8,128)S(1)}) custom-call(f32[8,128]{1,0:T(8,128)S(1)} %get-tuple-element.24.seen_ref, bf16[8,16,1024]{2,1,0:T(8,128)(2,1)S(1)} %copy-done, bf16[8,16,1024]{2,1,0:T(8,128)(2,1)S(1)} %collective-permute-done.2.refs_1_, bf16[8,16,1024]{2,1,0:T(8,128)(2,1)S(1)} %collective-permute-done.refs_2_, ...), custom_call_target="tpu_custom_call" | custom-call | flops 402653184 | bytes 6553600 | tf_op jit(solution)/shard_map/pallas_call | solution.py:63
  16.1 0.1 fusion
  16.2 2.7 %collective-permute-start.7 = (f16[8,24,256]{2,1,0:T(8,128)(2,1)S(1)}, f16[8,24,256]{2,1,0:T(8,128)(2,1)S(1)}, u32[]{:S(2)}, u32[]{:S(2)}) collective-permute-start(f16[8,24,256]{2,1,0:T(8,128)(2,1)S(1)} %get-tuple-element.41), channel_id=1, source_target_pairs={{0,2},{1,3},{2,0},{3,1},{4,6},{5,7},{6,4},{7,5},{8,10},{9,11},{10,... | collective-permute-start | bytes 294920 | tf_op jit(solution)/shard_map/ppermute | solution.py:104
  18.9 1.6 %collective-permute-start.8 = (f16[8,24,256]{2,1,0:T(8,128)(2,1)S(1)}, f16[8,24,256]{2,1,0:T(8,128)(2,1)S(1)}, u32[]{:S(2)}, u32[]{:S(2)}) collective-permute-start(f16[8,24,256]{2,1,0:T(8,128)(2,1)S(1)} %get-tuple-element.43), channel_id=1, source_target_pairs={{0,1},{1,0},{2,3},{3,2},{4,5},{5,4},{6,7},{7,6},{8,9},{9,8},{10,11... | collective-permute-start | bytes 294920 | tf_op jit(solution)/shard_map/ppermute | solution.py:104
  20.4 0.2 collective-permute-start.9
  20.7 0.2 collective-permute-done.6.refs_0_
  20.9 0.7 %shard_map.48 = (f32[4,4,8,256]{3,2,1,0:T(8,128)S(1)}, f32[8,128]{1,0:T(8,128)S(1)}) custom-call(f32[8,128]{1,0:T(8,128)S(1)} %get-tuple-element.31.seen_ref, bf16[4,32,1024]{2,1,0:T(8,128)(2,1)S(1)} %collective-permute-done.6.refs_0_, bf16[8,256,1024]{2,1,0:T(8,128)(2,1)S(1)} %get-tuple-element.28.refs_6_.refs_1_), custom_call_target="tpu_custom_call" | custom-call | flops 67108864 | bytes 2490368 | tf_op jit(solution)/shard_map/pallas_call | solution.py:63
  21.6 0.0 copy-start.2
  21.6 0.0 copy-start.1
  21.7 0.6 %collective-permute-done.5.refs_0_ = bf16[4,32,1024]{2,1,0:T(8,128)(2,1)S(1)} collective-permute-done((bf16[4,32,1024]{2,1,0:T(8,128)(2,1)S(1)}, bf16[4,32,1024]{2,1,0:T(8,128)(2,1)S(1)}, u32[]{:S(2)}, u32[]{:S(2)}) %collective-permute-start.5) | collective-permute-done | bytes 262176 | tf_op jit(solution)/shard_map/ppermute | solution.py:109
  22.2 0.7 %shard_map.49 = (f32[4,4,8,256]{3,2,1,0:T(8,128)S(1)}, f32[8,128]{1,0:T(8,128)S(1)}) custom-call(f32[8,128]{1,0:T(8,128)S(1)} %get-tuple-element.34.seen_ref, bf16[4,32,1024]{2,1,0:T(8,128)(2,1)S(1)} %collective-permute-done.5.refs_0_, bf16[8,256,1024]{2,1,0:T(8,128)(2,1)S(1)} %get-tuple-element.28.refs_6_.refs_1_), custom_call_target="tpu_custom_call" | custom-call | flops 67108864 | bytes 2490368 | tf_op jit(solution)/shard_map/pallas_call | solution.py:63
  23.0 2.7 %collective-permute-start.12 = (f16[8,8,256]{2,1,0:T(8,128)(2,1)S(1)}, f16[8,8,256]{2,1,0:T(8,128)(2,1)S(1)}, u32[]{:S(2)}, u32[]{:S(2)}) collective-permute-start(f16[8,8,256]{2,1,0:T(8,128)(2,1)S(1)} %fusion.5), channel_id=1, source_target_pairs={{0,2},{1,3},{2,0},{3,1},{4,6},{5,7},{6,4},{7,5},{8,10},{9,11},{10,... | collective-permute-start | bytes 98312 | tf_op jit(solution)/shard_map/ppermute | solution.py:104
  25.7 1.4 %collective-permute-start.13 = (f16[8,8,256]{2,1,0:T(8,128)(2,1)S(1)}, f16[8,8,256]{2,1,0:T(8,128)(2,1)S(1)}, u32[]{:S(2)}, u32[]{:S(2)}) collective-permute-start(f16[8,8,256]{2,1,0:T(8,128)(2,1)S(1)} %fusion.6), channel_id=1, source_target_pairs={{0,3},{1,2},{2,1},{3,0},{4,7},{5,6},{6,5},{7,4},{8,11},{9,10},{10,... | collective-permute-start | bytes 98312 | tf_op jit(solution)/shard_map/ppermute | solution.py:104
  27.1 0.0 collective-permute-done.7
  27.1 0.3 collective-permute-start.14
  27.4 0.0 collective-permute-done.8
  27.4 0.0 collective-permute-done.9
  27.5 0.6 %collective-permute-start.10 = (f32[8,8,256]{2,1,0:T(8,128)S(1)}, f32[8,8,256]{2,1,0:T(8,128)S(1)}, u32[]{:S(2)}, u32[]{:S(2)}) collective-permute-start(f32[8,8,256]{2,1,0:T(8,128)S(1)} %get-tuple-element.46), channel_id=1, source_target_pairs={{0,16},{4,20},{8,0},{12,4},{24,8},{28,12},{16,24},{20,28},{1,17},{... | collective-permute-start | bytes 196616 | tf_op jit(solution)/shard_map/ppermute | solution.py:109
  28.1 1.5 %collective-permute-start.11 = (f32[8,8,256]{2,1,0:T(8,128)S(1)}, f32[8,8,256]{2,1,0:T(8,128)S(1)}, u32[]{:S(2)}, u32[]{:S(2)}) collective-permute-start(f32[8,8,256]{2,1,0:T(8,128)S(1)} %get-tuple-element.45), channel_id=1, source_target_pairs={{0,8},{4,12},{8,24},{12,28},{24,16},{28,20},{16,0},{20,4},{1,9},{5... | collective-permute-start | bytes 196616 | tf_op jit(solution)/shard_map/ppermute | solution.py:109
  29.6 0.3 collective-permute-done.12
  29.9 1.6 %collective-permute-done.13 = f16[8,8,256]{2,1,0:T(8,128)(2,1)S(1)} collective-permute-done((f16[8,8,256]{2,1,0:T(8,128)(2,1)S(1)}, f16[8,8,256]{2,1,0:T(8,128)(2,1)S(1)}, u32[]{:S(2)}, u32[]{:S(2)}) %collective-permute-start.13) | collective-permute-done | bytes 32800 | tf_op jit(solution)/shard_map/ppermute | solution.py:104
  31.5 0.0 collective-permute-done.14
  31.5 1.0 %collective-permute-start.15 = (f16[8,8,256]{2,1,0:T(8,128)(2,1)S(1)}, f16[8,8,256]{2,1,0:T(8,128)(2,1)S(1)}, u32[]{:S(2)}, u32[]{:S(2)}) collective-permute-start(f16[8,8,256]{2,1,0:T(8,128)(2,1)S(1)} %fusion.4), channel_id=1, source_target_pairs={{0,24},{4,28},{8,16},{12,20},{16,8},{20,12},{24,0},{28,4},{1,25},{... | collective-permute-start | bytes 98312 | tf_op jit(solution)/shard_map/ppermute | solution.py:104
  32.5 0.0 collective-permute-done.10.refs_1_
  32.5 0.0 collective-permute-done.11.refs_2_
  32.6 0.1 collective-permute-start.16
  32.6 3.7 %collective-permute-done.15 = f16[8,8,256]{2,1,0:T(8,128)(2,1)S(1)} collective-permute-done((f16[8,8,256]{2,1,0:T(8,128)(2,1)S(1)}, f16[8,8,256]{2,1,0:T(8,128)(2,1)S(1)}, u32[]{:S(2)}, u32[]{:S(2)}) %collective-permute-start.15) | collective-permute-done | bytes 32800 | tf_op jit(solution)/shard_map/ppermute | solution.py:104
  36.4 0.1 collective-permute-start.17
  36.5 0.0 copy-done.2
  36.5 0.1 copy.5.occ_ref
  36.6 1.1 %collective-permute-done.17.refs_5_ = f32[8,4,256]{2,1,0:T(4,128)S(1)} collective-permute-done((f32[8,4,256]{2,1,0:T(4,128)S(1)}, f32[8,4,256]{2,1,0:T(4,128)S(1)}, u32[]{:S(2)}, u32[]{:S(2)}) %collective-permute-start.17) | collective-permute-done | bytes 32800 | tf_op jit(solution)/shard_map/ppermute | solution.py:104
  37.7 0.0 collective-permute-done.16.refs_4_
  37.7 0.0 copy-done.1
  37.7 0.8 %shard_map.50 = f32[8,4,2048]{2,1,0:T(4,128)} custom-call(f32[8,128]{1,0:T(8,128)S(1)} %get-tuple-element.37.seen_ref, f32[8,4]{1,0:T(8,128)S(1)} %copy.5.occ_ref, f32[8,2048]{1,0:T(8,128)S(1)} %copy-done.1, f32[8,24,256]{2,1,0:T(8,128)S(1)} %multiply_add_fusion.refs_0_, f32[8,8,256]{2,1,0:T(8,128)S(1)} %collective-permute-done.10.refs_1_, ...), custom_call_target="tpu_custom_call" | custom-call | tf_op jit(solution)/shard_map/pallas_call | solution.py:94
  (20 shorter events, 0.3 us)
Async XLA Ops:
  0.0 14.7 %copy-start = (bf16[8,16,1024]{2,1,0:T(8,128)(2,1)S(1)}, bf16[8,16,1024]{2,1,0:T(8,128)(2,1)}, u32[]{:S(2)}) copy-start(bf16[8,16,1024]{2,1,0:T(8,128)(2,1)} %refs_0_.1) | copy-start | bytes 786436
  0.0 9.6 %collective-permute-start = (bf16[8,16,1024]{2,1,0:T(8,128)(2,1)}, bf16[8,16,1024]{2,1,0:T(8,128)(2,1)S(1)}, u32[]{:S(2)}, u32[]{:S(2)}) collective-permute-start(bf16[8,16,1024]{2,1,0:T(8,128)(2,1)} %refs_0_.1), channel_id=1, source_target_pairs={{0,8},{4,12},{8,24},{12,28},{24,16},{28,20},{16,0},{20,4},{1,9},{5... | collective-permute-start | bytes 786440 | tf_op jit(solution)/shard_map/ppermute | solution.py:109
  2.9 8.0 %collective-permute-start.1 = (bf16[8,16,1024]{2,1,0:T(8,128)(2,1)}, bf16[8,16,1024]{2,1,0:T(8,128)(2,1)S(1)}, u32[]{:S(2)}, u32[]{:S(2)}) collective-permute-start(bf16[8,16,1024]{2,1,0:T(8,128)(2,1)} %refs_0_.1), channel_id=1, source_target_pairs={{0,16},{4,20},{8,0},{12,4},{24,8},{28,12},{16,24},{20,28},{1,17},{... | collective-permute-start | bytes 786440 | tf_op jit(solution)/shard_map/ppermute | solution.py:109
  3.0 7.9 %collective-permute-start.2 = (bf16[8,16,1024]{2,1,0:T(8,128)(2,1)}, bf16[8,16,1024]{2,1,0:T(8,128)(2,1)S(1)}, u32[]{:S(2)}, u32[]{:S(2)}) collective-permute-start(bf16[8,16,1024]{2,1,0:T(8,128)(2,1)} %refs_0_.1), channel_id=1, source_target_pairs={{0,4},{4,0},{8,12},{12,8},{16,20},{20,16},{24,28},{28,24},{1,5},{5... | collective-permute-start | bytes 786440 | tf_op jit(solution)/shard_map/ppermute | solution.py:104
  10.9 1.5 %collective-permute-start.3 = (bf16[8,16,1024]{2,1,0:T(8,128)(2,1)S(1)}, bf16[8,16,1024]{2,1,0:T(8,128)(2,1)S(1)}, u32[]{:S(2)}, u32[]{:S(2)}) collective-permute-start(bf16[8,16,1024]{2,1,0:T(8,128)(2,1)S(1)} %collective-permute-done.refs_2_), channel_id=1, source_target_pairs={{0,4},{4,0},{8,12},{12,8},{16,20},{20,16},{24,28},{28,24},{1,5},{5... | collective-permute-start | bytes 786440 | tf_op jit(solution)/shard_map/ppermute | solution.py:104
  10.9 3.1 %collective-permute-start.4 = (bf16[8,16,1024]{2,1,0:T(8,128)(2,1)S(1)}, bf16[8,16,1024]{2,1,0:T(8,128)(2,1)S(1)}, u32[]{:S(2)}, u32[]{:S(2)}) collective-permute-start(bf16[8,16,1024]{2,1,0:T(8,128)(2,1)S(1)} %collective-permute-done.1.refs_4_), channel_id=1, source_target_pairs={{0,4},{4,0},{8,12},{12,8},{16,20},{20,16},{24,28},{28,24},{1,5},{5... | collective-permute-start | bytes 786440 | tf_op jit(solution)/shard_map/ppermute | solution.py:104
  12.5 8.4 %collective-permute-start.6 = (bf16[4,32,1024]{2,1,0:T(8,128)(2,1)S(1)}, bf16[4,32,1024]{2,1,0:T(8,128)(2,1)S(1)}, u32[]{:S(2)}, u32[]{:S(2)}) collective-permute-start(bf16[4,32,1024]{2,1,0:T(8,128)(2,1)S(1)} %pad_maximum_fusion.1), channel_id=1, source_target_pairs={{0,8},{4,12},{8,24},{12,28},{24,16},{28,20},{16,0},{20,4},{1,9},{5... | collective-permute-start | bytes 786440 | tf_op jit(solution)/shard_map/ppermute | solution.py:109
  14.1 8.1 %collective-permute-start.5 = (bf16[4,32,1024]{2,1,0:T(8,128)(2,1)S(1)}, bf16[4,32,1024]{2,1,0:T(8,128)(2,1)S(1)}, u32[]{:S(2)}, u32[]{:S(2)}) collective-permute-start(bf16[4,32,1024]{2,1,0:T(8,128)(2,1)S(1)} %pad_maximum_fusion), channel_id=1, source_target_pairs={{0,16},{4,20},{8,0},{12,4},{24,8},{28,12},{16,24},{20,28},{1,17},{... | collective-permute-start | bytes 786440 | tf_op jit(solution)/shard_map/ppermute | solution.py:109
  16.2 10.9 %collective-permute-start.7 = (f16[8,24,256]{2,1,0:T(8,128)(2,1)S(1)}, f16[8,24,256]{2,1,0:T(8,128)(2,1)S(1)}, u32[]{:S(2)}, u32[]{:S(2)}) collective-permute-start(f16[8,24,256]{2,1,0:T(8,128)(2,1)S(1)} %get-tuple-element.41), channel_id=1, source_target_pairs={{0,2},{1,3},{2,0},{3,1},{4,6},{5,7},{6,4},{7,5},{8,10},{9,11},{10,... | collective-permute-start | bytes 294920 | tf_op jit(solution)/shard_map/ppermute | solution.py:104
  18.9 8.6 %collective-permute-start.8 = (f16[8,24,256]{2,1,0:T(8,128)(2,1)S(1)}, f16[8,24,256]{2,1,0:T(8,128)(2,1)S(1)}, u32[]{:S(2)}, u32[]{:S(2)}) collective-permute-start(f16[8,24,256]{2,1,0:T(8,128)(2,1)S(1)} %get-tuple-element.43), channel_id=1, source_target_pairs={{0,1},{1,0},{2,3},{3,2},{4,5},{5,4},{6,7},{7,6},{8,9},{9,8},{10,11... | collective-permute-start | bytes 294920 | tf_op jit(solution)/shard_map/ppermute | solution.py:104
  20.4 7.0 %collective-permute-start.9 = (f16[8,24,256]{2,1,0:T(8,128)(2,1)S(1)}, f16[8,24,256]{2,1,0:T(8,128)(2,1)S(1)}, u32[]{:S(2)}, u32[]{:S(2)}) collective-permute-start(f16[8,24,256]{2,1,0:T(8,128)(2,1)S(1)} %get-tuple-element.42), channel_id=1, source_target_pairs={{0,3},{1,2},{2,1},{3,0},{4,7},{5,6},{6,5},{7,4},{8,11},{9,10},{10,... | collective-permute-start | bytes 294920 | tf_op jit(solution)/shard_map/ppermute | solution.py:104
  21.6 14.9 %copy-start.2 = (f32[8,4]{0,1:T(4,128)S(1)}, f32[8,4]{0,1:T(4,128)}, u32[]{:S(2)}) copy-start(f32[8,4]{0,1:T(4,128)} %param.6) | copy-start | bytes 388
  21.6 16.0 %copy-start.1 = (f32[8,2048]{1,0:T(8,128)S(1)}, f32[8,2048]{1,0:T(8,128)}, u32[]{:S(2)}) copy-start(f32[8,2048]{1,0:T(8,128)} %vir_ref.1) | copy-start | bytes 196612
  23.0 6.8 %collective-permute-start.12 = (f16[8,8,256]{2,1,0:T(8,128)(2,1)S(1)}, f16[8,8,256]{2,1,0:T(8,128)(2,1)S(1)}, u32[]{:S(2)}, u32[]{:S(2)}) collective-permute-start(f16[8,8,256]{2,1,0:T(8,128)(2,1)S(1)} %fusion.5), channel_id=1, source_target_pairs={{0,2},{1,3},{2,0},{3,1},{4,6},{5,7},{6,4},{7,5},{8,10},{9,11},{10,... | collective-permute-start | bytes 98312 | tf_op jit(solution)/shard_map/ppermute | solution.py:104
  25.7 5.8 %collective-permute-start.13 = (f16[8,8,256]{2,1,0:T(8,128)(2,1)S(1)}, f16[8,8,256]{2,1,0:T(8,128)(2,1)S(1)}, u32[]{:S(2)}, u32[]{:S(2)}) collective-permute-start(f16[8,8,256]{2,1,0:T(8,128)(2,1)S(1)} %fusion.6), channel_id=1, source_target_pairs={{0,3},{1,2},{2,1},{3,0},{4,7},{5,6},{6,5},{7,4},{8,11},{9,10},{10,... | collective-permute-start | bytes 98312 | tf_op jit(solution)/shard_map/ppermute | solution.py:104
  27.1 4.3 %collective-permute-start.14 = (f16[8,8,256]{2,1,0:T(8,128)(2,1)S(1)}, f16[8,8,256]{2,1,0:T(8,128)(2,1)S(1)}, u32[]{:S(2)}, u32[]{:S(2)}) collective-permute-start(f16[8,8,256]{2,1,0:T(8,128)(2,1)S(1)} %fusion.7), channel_id=1, source_target_pairs={{0,1},{1,0},{2,3},{3,2},{4,5},{5,4},{6,7},{7,6},{8,9},{9,8},{10,11... | collective-permute-start | bytes 98312 | tf_op jit(solution)/shard_map/ppermute | solution.py:104
  27.5 5.0 %collective-permute-start.10 = (f32[8,8,256]{2,1,0:T(8,128)S(1)}, f32[8,8,256]{2,1,0:T(8,128)S(1)}, u32[]{:S(2)}, u32[]{:S(2)}) collective-permute-start(f32[8,8,256]{2,1,0:T(8,128)S(1)} %get-tuple-element.46), channel_id=1, source_target_pairs={{0,16},{4,20},{8,0},{12,4},{24,8},{28,12},{16,24},{20,28},{1,17},{... | collective-permute-start | bytes 196616 | tf_op jit(solution)/shard_map/ppermute | solution.py:109
  28.1 4.4 %collective-permute-start.11 = (f32[8,8,256]{2,1,0:T(8,128)S(1)}, f32[8,8,256]{2,1,0:T(8,128)S(1)}, u32[]{:S(2)}, u32[]{:S(2)}) collective-permute-start(f32[8,8,256]{2,1,0:T(8,128)S(1)} %get-tuple-element.45), channel_id=1, source_target_pairs={{0,8},{4,12},{8,24},{12,28},{24,16},{28,20},{16,0},{20,4},{1,9},{5... | collective-permute-start | bytes 196616 | tf_op jit(solution)/shard_map/ppermute | solution.py:109
  31.5 4.9 %collective-permute-start.15 = (f16[8,8,256]{2,1,0:T(8,128)(2,1)S(1)}, f16[8,8,256]{2,1,0:T(8,128)(2,1)S(1)}, u32[]{:S(2)}, u32[]{:S(2)}) collective-permute-start(f16[8,8,256]{2,1,0:T(8,128)(2,1)S(1)} %fusion.4), channel_id=1, source_target_pairs={{0,24},{4,28},{8,16},{12,20},{16,8},{20,12},{24,0},{28,4},{1,25},{... | collective-permute-start | bytes 98312 | tf_op jit(solution)/shard_map/ppermute | solution.py:104
  32.6 5.1 %collective-permute-start.16 = (f32[8,12,256]{2,1,0:T(8,128)S(1)}, f32[8,12,256]{2,1,0:T(8,128)S(1)}, u32[]{:S(2)}, u32[]{:S(2)}) collective-permute-start(f32[8,12,256]{2,1,0:T(8,128)S(1)} %pad_maximum_fusion.2), channel_id=1, source_target_pairs={{0,4},{4,0},{8,12},{12,8},{16,20},{20,16},{24,28},{28,24},{1,5},{5... | collective-permute-start | bytes 294920 | tf_op jit(solution)/shard_map/ppermute | solution.py:104
  36.4 1.3 %collective-permute-start.17 = (f32[8,4,256]{2,1,0:T(4,128)S(1)}, f32[8,4,256]{2,1,0:T(4,128)S(1)}, u32[]{:S(2)}, u32[]{:S(2)}) collective-permute-start(f32[8,4,256]{2,1,0:T(4,128)S(1)} %slice.95), channel_id=1, source_target_pairs={{0,4},{4,0},{8,12},{12,8},{16,20},{20,16},{24,28},{28,24},{1,5},{5... | collective-permute-start | bytes 98312 | tf_op jit(solution)/shard_map/ppermute | solution.py:104

commit v7 on v5

--- a/solution.py
+++ b/solution.py
@@ -139,10 +139,11 @@
     from_last = turn(total_b[:, 16:24], 1)
     total_c = reduced(sums_c[0], sums_c, (2, 3, 1))
     from_far = swap((total_c * SUMS).astype(jnp.float16), "occ", 6).astype(jnp.float32) * (1 / SUMS)
-    odd = swap(jnp.concatenate([total_b[:, 4:8], from_next[:, 4:], from_last[:, 4:]], axis=1), "occ", 1)
+    odd = swap(jnp.concatenate([from_next[:, 4:], from_last[:, 4:]], axis=1), "occ", 1)
+    odd_own = swap(total_b[:, 4:8], "occ", 1)
     odd_far = swap(from_far[:, 4:], "occ", 1)
-    slabs = [("own", 0, 0, 0), ("own", 1, 4, 0), ("next", 0, 1, 0), ("next", 1, 4, 4), ("last", 0, 2, 0), ("last", 1, 4, 8), ("far", 0, 3, 0), ("far", 1, 5, 0)]
-    return update(mark, occ_energy, vir_energy, slabs, [total_b, from_next, from_last, from_far, odd, odd_far])
+    slabs = [("own", 0, 0, 0), ("own", 1, 6, 0), ("next", 0, 1, 0), ("next", 1, 4, 0), ("last", 0, 2, 0), ("last", 1, 4, 4), ("far", 0, 3, 0), ("far", 1, 5, 0)]
+    return update(mark, occ_energy, vir_energy, slabs, [total_b, from_next, from_last, from_far, odd, odd_far, odd_own])
 
 
 def plain(amplitudes, integrals, occ_energy, vir_energy):

time: 38.2 us -> 38.2 us (level)
    ppermute x12 -> x13, waiting for transfers between devices: 6.3 us -> 6.29 us  [swap(): lax.ppermute(x, axis, [(i, i ^ mask) for i in range(lax.axis_size(axis))])]
    ppermute x12 -> x13, starting transfers between devices: 11.8 us -> 11.8 us  [swap(): lax.ppermute(x, axis, [(i, i ^ mask) for i in range(lax.axis_size(axis))])]
  transfers between devices with their start and end apart: 18 -> 19, of which waited for: 10 -> 10; matrix products, arithmetic and copies ran while one was open for 1% -> 1% of each run, Pallas kernels for 13% -> 13%
where the time goes in v7:
time: 38.2 us; the launch traced here: 38.1 us
  starting transfers between devices  19.1 us (50%)
  waiting for transfers between devices  12.6 us (33%)
  Pallas kernels  5.86 us (15%)
    ppermute x13, starting transfers between devices, swap(): lax.ppermute(x, axis, [(i, i ^ mask) for i in range(lax.axis_size(axis))])  11.8 us
    ppermute x6, starting transfers between devices, turn(): lax.ppermute(x, 'occ', [(2 * ring[r] + core, 2 * ring[(r + step) % 4] + c...  7.22 us
    ppermute x13, waiting for transfers between devices, swap(): lax.ppermute(x, axis, [(i, i ^ mask) for i in range(lax.axis_size(axis))])  6.29 us
    ppermute x6, waiting for transfers between devices, turn(): lax.ppermute(x, 'occ', [(2 * ring[r] + core, 2 * ring[(r + step) % 4] + c...  6.27 us
    pallas_call x2, Pallas kernels, contract(): pl.pallas_call(functools.partial(contract_kernel, groups), out_shape=(jax...  2.79 us
    pallas_call x1, Pallas kernels, load(): pl.pallas_call(load_kernel, out_shape=(jax.ShapeDtypeStruct(integrals.sha...  2.21 us
    pallas_call x1, Pallas kernels, update(): pl.pallas_call(functools.partial(update_kernel, slabs), out_shape=jax.Sha...  0.85 us
  transfers between devices with their start and end apart: 19, of which 10 were waited for; matrix products, arithmetic and copies ran while one was open for 1% of the time, Pallas kernels for 13%

profile of v7, /device:TPU:0, one launch (start us, length us, event | category | flops | bytes accessed | tf_op | source)
XLA Modules:
  0.0 38.1 jit_solution(17368616156911490365)
XLA Ops:
  0.0 2.9 %collective-permute-start = (bf16[8,16,1024]{2,1,0:T(8,128)(2,1)}, bf16[8,16,1024]{2,1,0:T(8,128)(2,1)S(1)}, u32[]{:S(2)}, u32[]{:S(2)}) collective-permute-start(bf16[8,16,1024]{2,1,0:T(8,128)(2,1)} %refs_0_.1), channel_id=1, source_target_pairs={{0,8},{4,12},{8,24},{12,28},{24,16},{28,20},{16,0},{20,4},{1,9},{5... | collective-permute-start | bytes 786440 | tf_op jit(solution)/shard_map/ppermute | solution.py:108
  2.9 0.1 collective-permute-start.1
  3.0 0.0 collective-permute-start.2
  3.0 2.2 %shard_map.46 = (bf16[8,256,1024]{2,1,0:T(8,128)(2,1)S(1)}, f32[8,128]{1,0:T(8,128)S(1)}) custom-call(bf16[8,256,1024]{2,1,0:T(8,128)(2,1)} %int_ref.1), custom_call_target="tpu_custom_call" | custom-call | bytes 8388608 | tf_op jit(solution)/shard_map/pallas_call | solution.py:27
  5.2 4.3 %collective-permute-done.refs_2_ = bf16[8,16,1024]{2,1,0:T(8,128)(2,1)S(1)} collective-permute-done((bf16[8,16,1024]{2,1,0:T(8,128)(2,1)}, bf16[8,16,1024]{2,1,0:T(8,128)(2,1)S(1)}, u32[]{:S(2)}, u32[]{:S(2)}) %collective-permute-start) | collective-permute-done | bytes 262176 | tf_op jit(solution)/shard_map/ppermute | solution.py:108
  9.6 1.4 %collective-permute-done.1.refs_4_ = bf16[8,16,1024]{2,1,0:T(8,128)(2,1)S(1)} collective-permute-done((bf16[8,16,1024]{2,1,0:T(8,128)(2,1)}, bf16[8,16,1024]{2,1,0:T(8,128)(2,1)S(1)}, u32[]{:S(2)}, u32[]{:S(2)}) %collective-permute-start.1) | collective-permute-done | bytes 262176 | tf_op jit(solution)/shard_map/ppermute | solution.py:108
  10.9 0.0 collective-permute-done.2.refs_1_
  10.9 0.0 collective-permute-start.4
  10.9 0.5 %collective-permute-start.3 = (bf16[8,16,1024]{2,1,0:T(8,128)(2,1)S(1)}, bf16[8,16,1024]{2,1,0:T(8,128)(2,1)S(1)}, u32[]{:S(2)}, u32[]{:S(2)}) collective-permute-start(bf16[8,16,1024]{2,1,0:T(8,128)(2,1)S(1)} %collective-permute-done.refs_2_), channel_id=1, source_target_pairs={{0,4},{4,0},{8,12},{12,8},{16,20},{20,16},{24,28},{28,24},{1,5},{5... | collective-permute-start | bytes 786440 | tf_op jit(solution)/shard_map/ppermute | solution.py:103
  11.5 1.0 %collective-permute-done.4.refs_5_ = bf16[8,16,1024]{2,1,0:T(8,128)(2,1)S(1)} collective-permute-done((bf16[8,16,1024]{2,1,0:T(8,128)(2,1)S(1)}, bf16[8,16,1024]{2,1,0:T(8,128)(2,1)S(1)}, u32[]{:S(2)}, u32[]{:S(2)}) %collective-permute-start.4) | collective-permute-done | bytes 262176 | tf_op jit(solution)/shard_map/ppermute | solution.py:103
  12.5 0.4 %collective-permute-start.6 = (bf16[4,32,1024]{2,1,0:T(8,128)(2,1)S(1)}, bf16[4,32,1024]{2,1,0:T(8,128)(2,1)S(1)}, u32[]{:S(2)}, u32[]{:S(2)}) collective-permute-start(bf16[4,32,1024]{2,1,0:T(8,128)(2,1)S(1)} %pad_maximum_fusion.1), channel_id=1, source_target_pairs={{0,16},{4,20},{8,0},{12,4},{24,8},{28,12},{16,24},{20,28},{1,17},{... | collective-permute-start | bytes 786440 | tf_op jit(solution)/shard_map/ppermute | solution.py:108
  12.9 0.0 collective-permute-done.3.refs_3_
  13.0 1.7 %collective-permute-start.5 = (bf16[4,32,1024]{2,1,0:T(8,128)(2,1)S(1)}, bf16[4,32,1024]{2,1,0:T(8,128)(2,1)S(1)}, u32[]{:S(2)}, u32[]{:S(2)}) collective-permute-start(bf16[4,32,1024]{2,1,0:T(8,128)(2,1)S(1)} %pad_maximum_fusion), channel_id=1, source_target_pairs={{0,8},{4,12},{8,24},{12,28},{24,16},{28,20},{16,0},{20,4},{1,9},{5... | collective-permute-start | bytes 786440 | tf_op jit(solution)/shard_map/ppermute | solution.py:108
  14.7 0.0 copy-done
  14.7 1.4 %shard_map.47 = (f32[4,8,24,256]{3,2,1,0:T(8,128)S(1)}, f32[8,128]{1,0:T(8,128)S(1)}) custom-call(f32[8,128]{1,0:T(8,128)S(1)} %get-tuple-element.21.seen_ref, bf16[8,16,1024]{2,1,0:T(8,128)(2,1)S(1)} %copy-done, bf16[8,16,1024]{2,1,0:T(8,128)(2,1)S(1)} %collective-permute-done.2.refs_1_, bf16[8,16,1024]{2,1,0:T(8,128)(2,1)S(1)} %collective-permute-done.refs_2_, ...), custom_call_target="tpu_custom_call" | custom-call | flops 402653184 | bytes 6553600 | tf_op jit(solution)/shard_map/pallas_call | solution.py:62
  16.1 0.0 copy-start.2
  16.1 0.0 copy-start.1
  16.2 0.1 fusion
  16.2 2.7 %collective-permute-start.7 = (f16[8,24,256]{2,1,0:T(8,128)(2,1)S(1)}, f16[8,24,256]{2,1,0:T(8,128)(2,1)S(1)}, u32[]{:S(2)}, u32[]{:S(2)}) collective-permute-start(f16[8,24,256]{2,1,0:T(8,128)(2,1)S(1)} %get-tuple-element.35), channel_id=1, source_target_pairs={{0,2},{1,3},{2,0},{3,1},{4,6},{5,7},{6,4},{7,5},{8,10},{9,11},{10,... | collective-permute-start | bytes 294920 | tf_op jit(solution)/shard_map/ppermute | solution.py:103
  18.9 1.6 %collective-permute-start.8 = (f16[8,24,256]{2,1,0:T(8,128)(2,1)S(1)}, f16[8,24,256]{2,1,0:T(8,128)(2,1)S(1)}, u32[]{:S(2)}, u32[]{:S(2)}) collective-permute-start(f16[8,24,256]{2,1,0:T(8,128)(2,1)S(1)} %get-tuple-element.37), channel_id=1, source_target_pairs={{0,1},{1,0},{2,3},{3,2},{4,5},{5,4},{6,7},{7,6},{8,9},{9,8},{10,11... | collective-permute-start | bytes 294920 | tf_op jit(solution)/shard_map/ppermute | solution.py:103
  20.5 0.2 collective-permute-start.9
  20.7 0.2 collective-permute-done.6.refs_1_
  20.9 0.4 collective-permute-done.5.refs_0_
  21.3 1.3 %shard_map.48 = (f32[4,8,8,256]{3,2,1,0:T(8,128)S(1)}, f32[8,128]{1,0:T(8,128)S(1)}) custom-call(f32[8,128]{1,0:T(8,128)S(1)} %get-tuple-element.28.seen_ref, bf16[4,32,1024]{2,1,0:T(8,128)(2,1)S(1)} %collective-permute-done.5.refs_0_, bf16[4,32,1024]{2,1,0:T(8,128)(2,1)S(1)} %collective-permute-done.6.refs_1_, ...), custom_call_target="tpu_custom_call" | custom-call | flops 134217728 | bytes 4980736 | tf_op jit(solution)/shard_map/pallas_call | solution.py:62
  22.7 2.7 %collective-permute-start.12 = (f16[8,8,256]{2,1,0:T(8,128)(2,1)S(1)}, f16[8,8,256]{2,1,0:T(8,128)(2,1)S(1)}, u32[]{:S(2)}, u32[]{:S(2)}) collective-permute-start(f16[8,8,256]{2,1,0:T(8,128)(2,1)S(1)} %get-tuple-element.39), channel_id=1, source_target_pairs={{0,2},{1,3},{2,0},{3,1},{4,6},{5,7},{6,4},{7,5},{8,10},{9,11},{10,... | collective-permute-start | bytes 98312 | tf_op jit(solution)/shard_map/ppermute | solution.py:103
  25.3 1.3 %collective-permute-start.13 = (f16[8,8,256]{2,1,0:T(8,128)(2,1)S(1)}, f16[8,8,256]{2,1,0:T(8,128)(2,1)S(1)}, u32[]{:S(2)}, u32[]{:S(2)}) collective-permute-start(f16[8,8,256]{2,1,0:T(8,128)(2,1)S(1)} %get-tuple-element.41), channel_id=1, source_target_pairs={{0,3},{1,2},{2,1},{3,0},{4,7},{5,6},{6,5},{7,4},{8,11},{9,10},{10,... | collective-permute-start | bytes 98312 | tf_op jit(solution)/shard_map/ppermute | solution.py:103
  26.7 0.0 collective-permute-done.7
  26.7 0.2 collective-permute-start.14
  26.9 0.0 collective-permute-done.8
  26.9 0.4 %collective-permute-done.9 = f16[8,24,256]{2,1,0:T(8,128)(2,1)S(1)} collective-permute-done((f16[8,24,256]{2,1,0:T(8,128)(2,1)S(1)}, f16[8,24,256]{2,1,0:T(8,128)(2,1)S(1)}, u32[]{:S(2)}, u32[]{:S(2)}) %collective-permute-start.9) | collective-permute-done | bytes 98336 | tf_op jit(solution)/shard_map/ppermute | solution.py:103
  27.3 0.1 multiply_add_fusion.refs_0_
  27.4 1.2 %collective-permute-start.10 = (f32[8,8,256]{2,1,0:T(8,128)S(1)}, f32[8,8,256]{2,1,0:T(8,128)S(1)}, u32[]{:S(2)}, u32[]{:S(2)}) collective-permute-start(f32[8,8,256]{2,1,0:T(8,128)S(1)} %get-tuple-element.43), channel_id=1, source_target_pairs={{0,16},{4,20},{8,0},{12,4},{24,8},{28,12},{16,24},{20,28},{1,17},{... | collective-permute-start | bytes 196616 | tf_op jit(solution)/shard_map/ppermute | solution.py:108
  28.6 0.9 %collective-permute-start.11 = (f32[8,8,256]{2,1,0:T(8,128)S(1)}, f32[8,8,256]{2,1,0:T(8,128)S(1)}, u32[]{:S(2)}, u32[]{:S(2)}) collective-permute-start(f32[8,8,256]{2,1,0:T(8,128)S(1)} %get-tuple-element.42), channel_id=1, source_target_pairs={{0,8},{4,12},{8,24},{12,28},{24,16},{28,20},{16,0},{20,4},{1,9},{5... | collective-permute-start | bytes 196616 | tf_op jit(solution)/shard_map/ppermute | solution.py:108
  29.5 0.5 %collective-permute-done.12 = f16[8,8,256]{2,1,0:T(8,128)(2,1)S(1)} collective-permute-done((f16[8,8,256]{2,1,0:T(8,128)(2,1)S(1)}, f16[8,8,256]{2,1,0:T(8,128)(2,1)S(1)}, u32[]{:S(2)}, u32[]{:S(2)}) %collective-permute-start.12) | collective-permute-done | bytes 32800 | tf_op jit(solution)/shard_map/ppermute | solution.py:103
  29.9 0.0 collective-permute-start.18
  29.9 1.1 %collective-permute-done.13 = f16[8,8,256]{2,1,0:T(8,128)(2,1)S(1)} collective-permute-done((f16[8,8,256]{2,1,0:T(8,128)(2,1)S(1)}, f16[8,8,256]{2,1,0:T(8,128)(2,1)S(1)}, u32[]{:S(2)}, u32[]{:S(2)}) %collective-permute-start.13) | collective-permute-done | bytes 32800 | tf_op jit(solution)/shard_map/ppermute | solution.py:103
  31.0 0.0 collective-permute-done.14
  31.1 2.5 %collective-permute-start.15 = (f16[8,8,256]{2,1,0:T(8,128)(2,1)S(1)}, f16[8,8,256]{2,1,0:T(8,128)(2,1)S(1)}, u32[]{:S(2)}, u32[]{:S(2)}) collective-permute-start(f16[8,8,256]{2,1,0:T(8,128)(2,1)S(1)} %fusion.4), channel_id=1, source_target_pairs={{0,24},{4,28},{8,16},{12,20},{16,8},{20,12},{24,0},{28,4},{1,25},{... | collective-permute-start | bytes 98312 | tf_op jit(solution)/shard_map/ppermute | solution.py:103
  33.6 0.0 collective-permute-done.10.refs_1_
  33.6 0.0 collective-permute-done.11.refs_2_
  33.6 0.1 collective-permute-start.16
  33.7 2.2 %collective-permute-done.15 = f16[8,8,256]{2,1,0:T(8,128)(2,1)S(1)} collective-permute-done((f16[8,8,256]{2,1,0:T(8,128)(2,1)S(1)}, f16[8,8,256]{2,1,0:T(8,128)(2,1)S(1)}, u32[]{:S(2)}, u32[]{:S(2)}) %collective-permute-start.15) | collective-permute-done | bytes 32800 | tf_op jit(solution)/shard_map/ppermute | solution.py:103
  36.0 0.1 collective-permute-start.17
  36.1 0.1 copy.5.occ_ref
  36.1 0.0 collective-permute-done.18.refs_6_
  36.1 1.1 %collective-permute-done.17.refs_5_ = f32[8,4,256]{2,1,0:T(4,128)S(1)} collective-permute-done((f32[8,4,256]{2,1,0:T(4,128)S(1)}, f32[8,4,256]{2,1,0:T(4,128)S(1)}, u32[]{:S(2)}, u32[]{:S(2)}) %collective-permute-start.17) | collective-permute-done | bytes 32800 | tf_op jit(solution)/shard_map/ppermute | solution.py:103
  37.2 0.0 collective-permute-done.16.refs_4_
  37.2 0.9 %shard_map.49 = f32[8,4,2048]{2,1,0:T(4,128)} custom-call(f32[8,128]{1,0:T(8,128)S(1)} %get-tuple-element.32.seen_ref, f32[8,4]{1,0:T(8,128)S(1)} %copy.5.occ_ref, f32[8,2048]{1,0:T(8,128)S(1)} %copy-done.1, f32[8,24,256]{2,1,0:T(8,128)S(1)} %multiply_add_fusion.refs_0_, f32[8,8,256]{2,1,0:T(8,128)S(1)} %collective-permute-done.10.refs_1_, ...), custom_call_target="tpu_custom_call" | custom-call | tf_op jit(solution)/shard_map/pallas_call | solution.py:93
  (18 shorter events, 0.2 us)
Async XLA Ops:
  0.0 14.7 %copy-start = (bf16[8,16,1024]{2,1,0:T(8,128)(2,1)S(1)}, bf16[8,16,1024]{2,1,0:T(8,128)(2,1)}, u32[]{:S(2)}) copy-start(bf16[8,16,1024]{2,1,0:T(8,128)(2,1)} %refs_0_.1) | copy-start | bytes 786436
  0.0 9.6 %collective-permute-start = (bf16[8,16,1024]{2,1,0:T(8,128)(2,1)}, bf16[8,16,1024]{2,1,0:T(8,128)(2,1)S(1)}, u32[]{:S(2)}, u32[]{:S(2)}) collective-permute-start(bf16[8,16,1024]{2,1,0:T(8,128)(2,1)} %refs_0_.1), channel_id=1, source_target_pairs={{0,8},{4,12},{8,24},{12,28},{24,16},{28,20},{16,0},{20,4},{1,9},{5... | collective-permute-start | bytes 786440 | tf_op jit(solution)/shard_map/ppermute | solution.py:108
  2.9 8.0 %collective-permute-start.1 = (bf16[8,16,1024]{2,1,0:T(8,128)(2,1)}, bf16[8,16,1024]{2,1,0:T(8,128)(2,1)S(1)}, u32[]{:S(2)}, u32[]{:S(2)}) collective-permute-start(bf16[8,16,1024]{2,1,0:T(8,128)(2,1)} %refs_0_.1), channel_id=1, source_target_pairs={{0,16},{4,20},{8,0},{12,4},{24,8},{28,12},{16,24},{20,28},{1,17},{... | collective-permute-start | bytes 786440 | tf_op jit(solution)/shard_map/ppermute | solution.py:108
  3.0 7.9 %collective-permute-start.2 = (bf16[8,16,1024]{2,1,0:T(8,128)(2,1)}, bf16[8,16,1024]{2,1,0:T(8,128)(2,1)S(1)}, u32[]{:S(2)}, u32[]{:S(2)}) collective-permute-start(bf16[8,16,1024]{2,1,0:T(8,128)(2,1)} %refs_0_.1), channel_id=1, source_target_pairs={{0,4},{4,0},{8,12},{12,8},{16,20},{20,16},{24,28},{28,24},{1,5},{5... | collective-permute-start | bytes 786440 | tf_op jit(solution)/shard_map/ppermute | solution.py:103
  10.9 1.5 %collective-permute-start.4 = (bf16[8,16,1024]{2,1,0:T(8,128)(2,1)S(1)}, bf16[8,16,1024]{2,1,0:T(8,128)(2,1)S(1)}, u32[]{:S(2)}, u32[]{:S(2)}) collective-permute-start(bf16[8,16,1024]{2,1,0:T(8,128)(2,1)S(1)} %collective-permute-done.1.refs_4_), channel_id=1, source_target_pairs={{0,4},{4,0},{8,12},{12,8},{16,20},{20,16},{24,28},{28,24},{1,5},{5... | collective-permute-start | bytes 786440 | tf_op jit(solution)/shard_map/ppermute | solution.py:103
  10.9 2.0 %collective-permute-start.3 = (bf16[8,16,1024]{2,1,0:T(8,128)(2,1)S(1)}, bf16[8,16,1024]{2,1,0:T(8,128)(2,1)S(1)}, u32[]{:S(2)}, u32[]{:S(2)}) collective-permute-start(bf16[8,16,1024]{2,1,0:T(8,128)(2,1)S(1)} %collective-permute-done.refs_2_), channel_id=1, source_target_pairs={{0,4},{4,0},{8,12},{12,8},{16,20},{20,16},{24,28},{28,24},{1,5},{5... | collective-permute-start | bytes 786440 | tf_op jit(solution)/shard_map/ppermute | solution.py:103
  12.5 8.4 %collective-permute-start.6 = (bf16[4,32,1024]{2,1,0:T(8,128)(2,1)S(1)}, bf16[4,32,1024]{2,1,0:T(8,128)(2,1)S(1)}, u32[]{:S(2)}, u32[]{:S(2)}) collective-permute-start(bf16[4,32,1024]{2,1,0:T(8,128)(2,1)S(1)} %pad_maximum_fusion.1), channel_id=1, source_target_pairs={{0,16},{4,20},{8,0},{12,4},{24,8},{28,12},{16,24},{20,28},{1,17},{... | collective-permute-start | bytes 786440 | tf_op jit(solution)/shard_map/ppermute | solution.py:108
  13.0 8.3 %collective-permute-start.5 = (bf16[4,32,1024]{2,1,0:T(8,128)(2,1)S(1)}, bf16[4,32,1024]{2,1,0:T(8,128)(2,1)S(1)}, u32[]{:S(2)}, u32[]{:S(2)}) collective-permute-start(bf16[4,32,1024]{2,1,0:T(8,128)(2,1)S(1)} %pad_maximum_fusion), channel_id=1, source_target_pairs={{0,8},{4,12},{8,24},{12,28},{24,16},{28,20},{16,0},{20,4},{1,9},{5... | collective-permute-start | bytes 786440 | tf_op jit(solution)/shard_map/ppermute | solution.py:108
  16.1 19.9 %copy-start.2 = (f32[8,4]{0,1:T(4,128)S(1)}, f32[8,4]{0,1:T(4,128)}, u32[]{:S(2)}) copy-start(f32[8,4]{0,1:T(4,128)} %param.6) | copy-start | bytes 388
  16.1 21.1 %copy-start.1 = (f32[8,2048]{1,0:T(8,128)S(1)}, f32[8,2048]{1,0:T(8,128)}, u32[]{:S(2)}) copy-start(f32[8,2048]{1,0:T(8,128)} %vir_ref.1) | copy-start | bytes 196612
  16.2 10.4 %collective-permute-start.7 = (f16[8,24,256]{2,1,0:T(8,128)(2,1)S(1)}, f16[8,24,256]{2,1,0:T(8,128)(2,1)S(1)}, u32[]{:S(2)}, u32[]{:S(2)}) collective-permute-start(f16[8,24,256]{2,1,0:T(8,128)(2,1)S(1)} %get-tuple-element.35), channel_id=1, source_target_pairs={{0,2},{1,3},{2,0},{3,1},{4,6},{5,7},{6,4},{7,5},{8,10},{9,11},{10,... | collective-permute-start | bytes 294920 | tf_op jit(solution)/shard_map/ppermute | solution.py:103
  18.9 8.0 %collective-permute-start.8 = (f16[8,24,256]{2,1,0:T(8,128)(2,1)S(1)}, f16[8,24,256]{2,1,0:T(8,128)(2,1)S(1)}, u32[]{:S(2)}, u32[]{:S(2)}) collective-permute-start(f16[8,24,256]{2,1,0:T(8,128)(2,1)S(1)} %get-tuple-element.37), channel_id=1, source_target_pairs={{0,1},{1,0},{2,3},{3,2},{4,5},{5,4},{6,7},{7,6},{8,9},{9,8},{10,11... | collective-permute-start | bytes 294920 | tf_op jit(solution)/shard_map/ppermute | solution.py:103
  20.5 6.8 %collective-permute-start.9 = (f16[8,24,256]{2,1,0:T(8,128)(2,1)S(1)}, f16[8,24,256]{2,1,0:T(8,128)(2,1)S(1)}, u32[]{:S(2)}, u32[]{:S(2)}) collective-permute-start(f16[8,24,256]{2,1,0:T(8,128)(2,1)S(1)} %get-tuple-element.36), channel_id=1, source_target_pairs={{0,3},{1,2},{2,1},{3,0},{4,7},{5,6},{6,5},{7,4},{8,11},{9,10},{10,... | collective-permute-start | bytes 294920 | tf_op jit(solution)/shard_map/ppermute | solution.py:103
  22.7 7.3 %collective-permute-start.12 = (f16[8,8,256]{2,1,0:T(8,128)(2,1)S(1)}, f16[8,8,256]{2,1,0:T(8,128)(2,1)S(1)}, u32[]{:S(2)}, u32[]{:S(2)}) collective-permute-start(f16[8,8,256]{2,1,0:T(8,128)(2,1)S(1)} %get-tuple-element.39), channel_id=1, source_target_pairs={{0,2},{1,3},{2,0},{3,1},{4,6},{5,7},{6,4},{7,5},{8,10},{9,11},{10,... | collective-permute-start | bytes 98312 | tf_op jit(solution)/shard_map/ppermute | solution.py:103
  25.3 5.7 %collective-permute-start.13 = (f16[8,8,256]{2,1,0:T(8,128)(2,1)S(1)}, f16[8,8,256]{2,1,0:T(8,128)(2,1)S(1)}, u32[]{:S(2)}, u32[]{:S(2)}) collective-permute-start(f16[8,8,256]{2,1,0:T(8,128)(2,1)S(1)} %get-tuple-element.41), channel_id=1, source_target_pairs={{0,3},{1,2},{2,1},{3,0},{4,7},{5,6},{6,5},{7,4},{8,11},{9,10},{10,... | collective-permute-start | bytes 98312 | tf_op jit(solution)/shard_map/ppermute | solution.py:103
  26.7 4.4 %collective-permute-start.14 = (f16[8,8,256]{2,1,0:T(8,128)(2,1)S(1)}, f16[8,8,256]{2,1,0:T(8,128)(2,1)S(1)}, u32[]{:S(2)}, u32[]{:S(2)}) collective-permute-start(f16[8,8,256]{2,1,0:T(8,128)(2,1)S(1)} %get-tuple-element.40), channel_id=1, source_target_pairs={{0,1},{1,0},{2,3},{3,2},{4,5},{5,4},{6,7},{7,6},{8,9},{9,8},{10,11... | collective-permute-start | bytes 98312 | tf_op jit(solution)/shard_map/ppermute | solution.py:103
  27.4 6.2 %collective-permute-start.10 = (f32[8,8,256]{2,1,0:T(8,128)S(1)}, f32[8,8,256]{2,1,0:T(8,128)S(1)}, u32[]{:S(2)}, u32[]{:S(2)}) collective-permute-start(f32[8,8,256]{2,1,0:T(8,128)S(1)} %get-tuple-element.43), channel_id=1, source_target_pairs={{0,16},{4,20},{8,0},{12,4},{24,8},{28,12},{16,24},{20,28},{1,17},{... | collective-permute-start | bytes 196616 | tf_op jit(solution)/shard_map/ppermute | solution.py:108
  28.6 5.0 %collective-permute-start.11 = (f32[8,8,256]{2,1,0:T(8,128)S(1)}, f32[8,8,256]{2,1,0:T(8,128)S(1)}, u32[]{:S(2)}, u32[]{:S(2)}) collective-permute-start(f32[8,8,256]{2,1,0:T(8,128)S(1)} %get-tuple-element.42), channel_id=1, source_target_pairs={{0,8},{4,12},{8,24},{12,28},{24,16},{28,20},{16,0},{20,4},{1,9},{5... | collective-permute-start | bytes 196616 | tf_op jit(solution)/shard_map/ppermute | solution.py:108
  29.9 6.2 %collective-permute-start.18 = (f32[8,4,256]{2,1,0:T(4,128)S(1)}, f32[8,4,256]{2,1,0:T(4,128)S(1)}, u32[]{:S(2)}, u32[]{:S(2)}) collective-permute-start(f32[8,4,256]{2,1,0:T(4,128)S(1)} %slice.79), channel_id=1, source_target_pairs={{0,4},{4,0},{8,12},{12,8},{16,20},{20,16},{24,28},{28,24},{1,5},{5... | collective-permute-start | bytes 98312 | tf_op jit(solution)/shard_map/ppermute | solution.py:103
  31.1 4.9 %collective-permute-start.15 = (f16[8,8,256]{2,1,0:T(8,128)(2,1)S(1)}, f16[8,8,256]{2,1,0:T(8,128)(2,1)S(1)}, u32[]{:S(2)}, u32[]{:S(2)}) collective-permute-start(f16[8,8,256]{2,1,0:T(8,128)(2,1)S(1)} %fusion.4), channel_id=1, source_target_pairs={{0,24},{4,28},{8,16},{12,20},{16,8},{20,12},{24,0},{28,4},{1,25},{... | collective-permute-start | bytes 98312 | tf_op jit(solution)/shard_map/ppermute | solution.py:103
  33.6 3.6 %collective-permute-start.16 = (f32[8,8,256]{2,1,0:T(8,128)S(1)}, f32[8,8,256]{2,1,0:T(8,128)S(1)}, u32[]{:S(2)}, u32[]{:S(2)}) collective-permute-start(f32[8,8,256]{2,1,0:T(8,128)S(1)} %pad_maximum_fusion.2), channel_id=1, source_target_pairs={{0,4},{4,0},{8,12},{12,8},{16,20},{20,16},{24,28},{28,24},{1,5},{5... | collective-permute-start | bytes 196616 | tf_op jit(solution)/shard_map/ppermute | solution.py:103
  36.0 1.3 %collective-permute-start.17 = (f32[8,4,256]{2,1,0:T(4,128)S(1)}, f32[8,4,256]{2,1,0:T(4,128)S(1)}, u32[]{:S(2)}, u32[]{:S(2)}) collective-permute-start(f32[8,4,256]{2,1,0:T(4,128)S(1)} %slice.78), channel_id=1, source_target_pairs={{0,4},{4,0},{8,12},{12,8},{16,20},{20,16},{24,28},{28,24},{1,5},{5... | collective-permute-start | bytes 98312 | tf_op jit(solution)/shard_map/ppermute | solution.py:103

commit v8 on v5

--- a/solution.py
+++ b/solution.py
@@ -128,11 +128,11 @@
     slab, mark = load(integrals)
     last, nxt, sib, mark = lax.optimization_barrier((last, nxt, sib, mark))
     last_sib, nxt_sib = swap(last, "occ", 1), swap(nxt, "occ", 1)
-    low = turn(jnp.concatenate([last[:half], last_sib[:half]], axis=1), 1)
-    high = turn(jnp.concatenate([nxt[half:], nxt_sib[half:]], axis=1), -1)
+    low = turn(jnp.concatenate([last[half:], last_sib[half:]], axis=1), 1)
+    high = turn(jnp.concatenate([nxt[:half], nxt_sib[:half]], axis=1), -1)
     sums_b, mark = contract(mark, [amplitudes, sib, last, last_sib, nxt, nxt_sib], slab, [(0, 1, 2, 3, 4, 5)])
     low, high, mark = lax.optimization_barrier((low, high, mark))
-    sums_c, mark = contract(mark, [low, high], slab, [(0,), (1,)])
+    sums_c, mark = contract(mark, [high, low], slab, [(0,), (1,)])
     own, mark = lax.optimization_barrier((sums_b[0], mark))
     total_b = reduced(own, sums_b, (2, 1, 3))
     from_next = turn(total_b[:, 8:16], -1)

time: 38.2 us -> 38.2 us (level)
  no operation moved by 1% of the time
where the time goes in v8:
time: 38.2 us; the launch traced here: 38.1 us
  starting transfers between devices  19.1 us (50%)
  waiting for transfers between devices  12.6 us (33%)
  Pallas kernels  5.85 us (15%)
    ppermute x12, starting transfers between devices, swap(): lax.ppermute(x, axis, [(i, i ^ mask) for i in range(lax.axis_size(axis))])  11.8 us
    ppermute x6, starting transfers between devices, turn(): lax.ppermute(x, 'occ', [(2 * ring[r] + core, 2 * ring[(r + step) % 4] + c...  7.22 us
    ppermute x12, waiting for transfers between devices, swap(): lax.ppermute(x, axis, [(i, i ^ mask) for i in range(lax.axis_size(axis))])  6.3 us
    ppermute x6, waiting for transfers between devices, turn(): lax.ppermute(x, 'occ', [(2 * ring[r] + core, 2 * ring[(r + step) % 4] + c...  6.27 us
    pallas_call x2, Pallas kernels, contract(): pl.pallas_call(functools.partial(contract_kernel, groups), out_shape=(jax...  2.79 us
    pallas_call x1, Pallas kernels, load(): pl.pallas_call(load_kernel, out_shape=(jax.ShapeDtypeStruct(integrals.sha...  2.21 us
    pallas_call x1, Pallas kernels, update(): pl.pallas_call(functools.partial(update_kernel, slabs), out_shape=jax.Sha...  0.85 us
  transfers between devices with their start and end apart: 18, of which 10 were waited for; matrix products, arithmetic and copies ran while one was open for 1% of the time, Pallas kernels for 13%

profile of v8, /device:TPU:0, one launch (start us, length us, event | category | flops | bytes accessed | tf_op | source)
XLA Modules:
  0.0 38.1 jit_solution(11817032561928543897)
XLA Ops:
  0.0 0.0 copy-start
  0.0 2.9 %collective-permute-start = (bf16[8,16,1024]{2,1,0:T(8,128)(2,1)}, bf16[8,16,1024]{2,1,0:T(8,128)(2,1)S(1)}, u32[]{:S(2)}, u32[]{:S(2)}) collective-permute-start(bf16[8,16,1024]{2,1,0:T(8,128)(2,1)} %refs_0_.1), channel_id=1, source_target_pairs={{0,8},{4,12},{8,24},{12,28},{24,16},{28,20},{16,0},{20,4},{1,9},{5... | collective-permute-start | bytes 786440 | tf_op jit(solution)/shard_map/ppermute | solution.py:108
  2.9 0.1 collective-permute-start.1
  3.0 0.0 collective-permute-start.2
  3.0 2.2 %shard_map.46 = (bf16[8,256,1024]{2,1,0:T(8,128)(2,1)S(1)}, f32[8,128]{1,0:T(8,128)S(1)}) custom-call(bf16[8,256,1024]{2,1,0:T(8,128)(2,1)} %int_ref.1), custom_call_target="tpu_custom_call" | custom-call | bytes 8388608 | tf_op jit(solution)/shard_map/pallas_call | solution.py:27
  5.2 4.3 %collective-permute-done.refs_2_ = bf16[8,16,1024]{2,1,0:T(8,128)(2,1)S(1)} collective-permute-done((bf16[8,16,1024]{2,1,0:T(8,128)(2,1)}, bf16[8,16,1024]{2,1,0:T(8,128)(2,1)S(1)}, u32[]{:S(2)}, u32[]{:S(2)}) %collective-permute-start) | collective-permute-done | bytes 262176 | tf_op jit(solution)/shard_map/ppermute | solution.py:108
  9.6 1.4 %collective-permute-done.1.refs_4_ = bf16[8,16,1024]{2,1,0:T(8,128)(2,1)S(1)} collective-permute-done((bf16[8,16,1024]{2,1,0:T(8,128)(2,1)}, bf16[8,16,1024]{2,1,0:T(8,128)(2,1)S(1)}, u32[]{:S(2)}, u32[]{:S(2)}) %collective-permute-start.1) | collective-permute-done | bytes 262176 | tf_op jit(solution)/shard_map/ppermute | solution.py:108
  10.9 0.0 collective-permute-done.2.refs_1_
  10.9 0.0 collective-permute-start.4
  10.9 0.5 %collective-permute-start.3 = (bf16[8,16,1024]{2,1,0:T(8,128)(2,1)S(1)}, bf16[8,16,1024]{2,1,0:T(8,128)(2,1)S(1)}, u32[]{:S(2)}, u32[]{:S(2)}) collective-permute-start(bf16[8,16,1024]{2,1,0:T(8,128)(2,1)S(1)} %collective-permute-done.refs_2_), channel_id=1, source_target_pairs={{0,4},{4,0},{8,12},{12,8},{16,20},{20,16},{24,28},{28,24},{1,5},{5... | collective-permute-start | bytes 786440 | tf_op jit(solution)/shard_map/ppermute | solution.py:103
  11.5 1.0 %collective-permute-done.4.refs_5_ = bf16[8,16,1024]{2,1,0:T(8,128)(2,1)S(1)} collective-permute-done((bf16[8,16,1024]{2,1,0:T(8,128)(2,1)S(1)}, bf16[8,16,1024]{2,1,0:T(8,128)(2,1)S(1)}, u32[]{:S(2)}, u32[]{:S(2)}) %collective-permute-start.4) | collective-permute-done | bytes 262176 | tf_op jit(solution)/shard_map/ppermute | solution.py:103
  12.5 0.4 %collective-permute-start.6 = (bf16[4,32,1024]{2,1,0:T(8,128)(2,1)S(1)}, bf16[4,32,1024]{2,1,0:T(8,128)(2,1)S(1)}, u32[]{:S(2)}, u32[]{:S(2)}) collective-permute-start(bf16[4,32,1024]{2,1,0:T(8,128)(2,1)S(1)} %pad_maximum_fusion.1), channel_id=1, source_target_pairs={{0,16},{4,20},{8,0},{12,4},{24,8},{28,12},{16,24},{20,28},{1,17},{... | collective-permute-start | bytes 786440 | tf_op jit(solution)/shard_map/ppermute | solution.py:108
  12.9 0.0 collective-permute-done.3.refs_3_
  13.0 1.7 %collective-permute-start.5 = (bf16[4,32,1024]{2,1,0:T(8,128)(2,1)S(1)}, bf16[4,32,1024]{2,1,0:T(8,128)(2,1)S(1)}, u32[]{:S(2)}, u32[]{:S(2)}) collective-permute-start(bf16[4,32,1024]{2,1,0:T(8,128)(2,1)S(1)} %pad_maximum_fusion), channel_id=1, source_target_pairs={{0,8},{4,12},{8,24},{12,28},{24,16},{28,20},{16,0},{20,4},{1,9},{5... | collective-permute-start | bytes 786440 | tf_op jit(solution)/shard_map/ppermute | solution.py:108
  14.7 0.0 copy-done
  14.7 1.4 %shard_map.47 = (f32[4,8,24,256]{3,2,1,0:T(8,128)S(1)}, f32[8,128]{1,0:T(8,128)S(1)}) custom-call(f32[8,128]{1,0:T(8,128)S(1)} %get-tuple-element.21.seen_ref, bf16[8,16,1024]{2,1,0:T(8,128)(2,1)S(1)} %copy-done, bf16[8,16,1024]{2,1,0:T(8,128)(2,1)S(1)} %collective-permute-done.2.refs_1_, bf16[8,16,1024]{2,1,0:T(8,128)(2,1)S(1)} %collective-permute-done.refs_2_, ...), custom_call_target="tpu_custom_call" | custom-call | flops 402653184 | bytes 6553600 | tf_op jit(solution)/shard_map/pallas_call | solution.py:62
  16.1 0.0 copy-start.2
  16.1 0.0 copy-start.1
  16.2 0.1 fusion
  16.2 2.7 %collective-permute-start.7 = (f16[8,24,256]{2,1,0:T(8,128)(2,1)S(1)}, f16[8,24,256]{2,1,0:T(8,128)(2,1)S(1)}, u32[]{:S(2)}, u32[]{:S(2)}) collective-permute-start(f16[8,24,256]{2,1,0:T(8,128)(2,1)S(1)} %get-tuple-element.35), channel_id=1, source_target_pairs={{0,2},{1,3},{2,0},{3,1},{4,6},{5,7},{6,4},{7,5},{8,10},{9,11},{10,... | collective-permute-start | bytes 294920 | tf_op jit(solution)/shard_map/ppermute | solution.py:103
  18.9 1.6 %collective-permute-start.8 = (f16[8,24,256]{2,1,0:T(8,128)(2,1)S(1)}, f16[8,24,256]{2,1,0:T(8,128)(2,1)S(1)}, u32[]{:S(2)}, u32[]{:S(2)}) collective-permute-start(f16[8,24,256]{2,1,0:T(8,128)(2,1)S(1)} %get-tuple-element.37), channel_id=1, source_target_pairs={{0,1},{1,0},{2,3},{3,2},{4,5},{5,4},{6,7},{7,6},{8,9},{9,8},{10,11... | collective-permute-start | bytes 294920 | tf_op jit(solution)/shard_map/ppermute | solution.py:103
  20.5 0.2 collective-permute-start.9
  20.7 0.2 collective-permute-done.6.refs_0_
  20.9 0.4 collective-permute-done.5.refs_1_
  21.3 1.3 %shard_map.48 = (f32[4,8,8,256]{3,2,1,0:T(8,128)S(1)}, f32[8,128]{1,0:T(8,128)S(1)}) custom-call(f32[8,128]{1,0:T(8,128)S(1)} %get-tuple-element.28.seen_ref, bf16[4,32,1024]{2,1,0:T(8,128)(2,1)S(1)} %collective-permute-done.6.refs_0_, bf16[4,32,1024]{2,1,0:T(8,128)(2,1)S(1)} %collective-permute-done.5.refs_1_, ...), custom_call_target="tpu_custom_call" | custom-call | flops 134217728 | bytes 4980736 | tf_op jit(solution)/shard_map/pallas_call | solution.py:62
  22.7 2.7 %collective-permute-start.12 = (f16[8,8,256]{2,1,0:T(8,128)(2,1)S(1)}, f16[8,8,256]{2,1,0:T(8,128)(2,1)S(1)}, u32[]{:S(2)}, u32[]{:S(2)}) collective-permute-start(f16[8,8,256]{2,1,0:T(8,128)(2,1)S(1)} %get-tuple-element.39), channel_id=1, source_target_pairs={{0,2},{1,3},{2,0},{3,1},{4,6},{5,7},{6,4},{7,5},{8,10},{9,11},{10,... | collective-permute-start | bytes 98312 | tf_op jit(solution)/shard_map/ppermute | solution.py:103
  25.3 1.3 %collective-permute-start.13 = (f16[8,8,256]{2,1,0:T(8,128)(2,1)S(1)}, f16[8,8,256]{2,1,0:T(8,128)(2,1)S(1)}, u32[]{:S(2)}, u32[]{:S(2)}) collective-permute-start(f16[8,8,256]{2,1,0:T(8,128)(2,1)S(1)} %get-tuple-element.41), channel_id=1, source_target_pairs={{0,3},{1,2},{2,1},{3,0},{4,7},{5,6},{6,5},{7,4},{8,11},{9,10},{10,... | collective-permute-start | bytes 98312 | tf_op jit(solution)/shard_map/ppermute | solution.py:103
  26.7 0.0 collective-permute-done.7
  26.7 0.2 collective-permute-start.14
  26.9 0.0 collective-permute-done.8
  26.9 0.4 %collective-permute-done.9 = f16[8,24,256]{2,1,0:T(8,128)(2,1)S(1)} collective-permute-done((f16[8,24,256]{2,1,0:T(8,128)(2,1)S(1)}, f16[8,24,256]{2,1,0:T(8,128)(2,1)S(1)}, u32[]{:S(2)}, u32[]{:S(2)}) %collective-permute-start.9) | collective-permute-done | bytes 98336 | tf_op jit(solution)/shard_map/ppermute | solution.py:103
  27.4 1.2 %collective-permute-start.10 = (f32[8,8,256]{2,1,0:T(8,128)S(1)}, f32[8,8,256]{2,1,0:T(8,128)S(1)}, u32[]{:S(2)}, u32[]{:S(2)}) collective-permute-start(f32[8,8,256]{2,1,0:T(8,128)S(1)} %get-tuple-element.43), channel_id=1, source_target_pairs={{0,16},{4,20},{8,0},{12,4},{24,8},{28,12},{16,24},{20,28},{1,17},{... | collective-permute-start | bytes 196616 | tf_op jit(solution)/shard_map/ppermute | solution.py:108
  28.5 0.9 %collective-permute-start.11 = (f32[8,8,256]{2,1,0:T(8,128)S(1)}, f32[8,8,256]{2,1,0:T(8,128)S(1)}, u32[]{:S(2)}, u32[]{:S(2)}) collective-permute-start(f32[8,8,256]{2,1,0:T(8,128)S(1)} %get-tuple-element.42), channel_id=1, source_target_pairs={{0,8},{4,12},{8,24},{12,28},{24,16},{28,20},{16,0},{20,4},{1,9},{5... | collective-permute-start | bytes 196616 | tf_op jit(solution)/shard_map/ppermute | solution.py:108
  29.4 0.5 %collective-permute-done.12 = f16[8,8,256]{2,1,0:T(8,128)(2,1)S(1)} collective-permute-done((f16[8,8,256]{2,1,0:T(8,128)(2,1)S(1)}, f16[8,8,256]{2,1,0:T(8,128)(2,1)S(1)}, u32[]{:S(2)}, u32[]{:S(2)}) %collective-permute-start.12) | collective-permute-done | bytes 32800 | tf_op jit(solution)/shard_map/ppermute | solution.py:103
  29.9 1.1 %collective-permute-done.13 = f16[8,8,256]{2,1,0:T(8,128)(2,1)S(1)} collective-permute-done((f16[8,8,256]{2,1,0:T(8,128)(2,1)S(1)}, f16[8,8,256]{2,1,0:T(8,128)(2,1)S(1)}, u32[]{:S(2)}, u32[]{:S(2)}) %collective-permute-start.13) | collective-permute-done | bytes 32800 | tf_op jit(solution)/shard_map/ppermute | solution.py:103
  31.0 0.0 collective-permute-done.14
  31.1 2.5 %collective-permute-start.15 = (f16[8,8,256]{2,1,0:T(8,128)(2,1)S(1)}, f16[8,8,256]{2,1,0:T(8,128)(2,1)S(1)}, u32[]{:S(2)}, u32[]{:S(2)}) collective-permute-start(f16[8,8,256]{2,1,0:T(8,128)(2,1)S(1)} %fusion.4), channel_id=1, source_target_pairs={{0,24},{4,28},{8,16},{12,20},{16,8},{20,12},{24,0},{28,4},{1,25},{... | collective-permute-start | bytes 98312 | tf_op jit(solution)/shard_map/ppermute | solution.py:103
  33.5 0.0 collective-permute-done.10.refs_1_
  33.6 0.0 collective-permute-done.11.refs_2_
  33.6 0.1 collective-permute-start.16
  33.7 2.2 %collective-permute-done.15 = f16[8,8,256]{2,1,0:T(8,128)(2,1)S(1)} collective-permute-done((f16[8,8,256]{2,1,0:T(8,128)(2,1)S(1)}, f16[8,8,256]{2,1,0:T(8,128)(2,1)S(1)}, u32[]{:S(2)}, u32[]{:S(2)}) %collective-permute-start.15) | collective-permute-done | bytes 32800 | tf_op jit(solution)/shard_map/ppermute | solution.py:103
  36.0 0.1 collective-permute-start.17
  36.0 0.0 copy-done.2
  36.1 0.1 copy.5.occ_ref
  36.1 1.1 %collective-permute-done.17.refs_5_ = f32[8,4,256]{2,1,0:T(4,128)S(1)} collective-permute-done((f32[8,4,256]{2,1,0:T(4,128)S(1)}, f32[8,4,256]{2,1,0:T(4,128)S(1)}, u32[]{:S(2)}, u32[]{:S(2)}) %collective-permute-start.17) | collective-permute-done | bytes 32800 | tf_op jit(solution)/shard_map/ppermute | solution.py:103
  37.2 0.0 collective-permute-done.16.refs_4_
  37.2 0.0 copy-done.1
  37.2 0.8 %shard_map.49 = f32[8,4,2048]{2,1,0:T(4,128)} custom-call(f32[8,128]{1,0:T(8,128)S(1)} %get-tuple-element.32.seen_ref, f32[8,4]{1,0:T(8,128)S(1)} %copy.5.occ_ref, f32[8,2048]{1,0:T(8,128)S(1)} %copy-done.1, f32[8,24,256]{2,1,0:T(8,128)S(1)} %multiply_add_fusion.refs_0_, f32[8,8,256]{2,1,0:T(8,128)S(1)} %collective-permute-done.10.refs_1_, ...), custom_call_target="tpu_custom_call" | custom-call | tf_op jit(solution)/shard_map/pallas_call | solution.py:93
  (16 shorter events, 0.3 us)
Async XLA Ops:
  0.0 14.7 %copy-start = (bf16[8,16,1024]{2,1,0:T(8,128)(2,1)S(1)}, bf16[8,16,1024]{2,1,0:T(8,128)(2,1)}, u32[]{:S(2)}) copy-start(bf16[8,16,1024]{2,1,0:T(8,128)(2,1)} %refs_0_.1) | copy-start | bytes 786436
  0.0 9.6 %collective-permute-start = (bf16[8,16,1024]{2,1,0:T(8,128)(2,1)}, bf16[8,16,1024]{2,1,0:T(8,128)(2,1)S(1)}, u32[]{:S(2)}, u32[]{:S(2)}) collective-permute-start(bf16[8,16,1024]{2,1,0:T(8,128)(2,1)} %refs_0_.1), channel_id=1, source_target_pairs={{0,8},{4,12},{8,24},{12,28},{24,16},{28,20},{16,0},{20,4},{1,9},{5... | collective-permute-start | bytes 786440 | tf_op jit(solution)/shard_map/ppermute | solution.py:108
  2.9 8.0 %collective-permute-start.1 = (bf16[8,16,1024]{2,1,0:T(8,128)(2,1)}, bf16[8,16,1024]{2,1,0:T(8,128)(2,1)S(1)}, u32[]{:S(2)}, u32[]{:S(2)}) collective-permute-start(bf16[8,16,1024]{2,1,0:T(8,128)(2,1)} %refs_0_.1), channel_id=1, source_target_pairs={{0,16},{4,20},{8,0},{12,4},{24,8},{28,12},{16,24},{20,28},{1,17},{... | collective-permute-start | bytes 786440 | tf_op jit(solution)/shard_map/ppermute | solution.py:108
  3.0 7.9 %collective-permute-start.2 = (bf16[8,16,1024]{2,1,0:T(8,128)(2,1)}, bf16[8,16,1024]{2,1,0:T(8,128)(2,1)S(1)}, u32[]{:S(2)}, u32[]{:S(2)}) collective-permute-start(bf16[8,16,1024]{2,1,0:T(8,128)(2,1)} %refs_0_.1), channel_id=1, source_target_pairs={{0,4},{4,0},{8,12},{12,8},{16,20},{20,16},{24,28},{28,24},{1,5},{5... | collective-permute-start | bytes 786440 | tf_op jit(solution)/shard_map/ppermute | solution.py:103
  10.9 1.5 %collective-permute-start.4 = (bf16[8,16,1024]{2,1,0:T(8,128)(2,1)S(1)}, bf16[8,16,1024]{2,1,0:T(8,128)(2,1)S(1)}, u32[]{:S(2)}, u32[]{:S(2)}) collective-permute-start(bf16[8,16,1024]{2,1,0:T(8,128)(2,1)S(1)} %collective-permute-done.1.refs_4_), channel_id=1, source_target_pairs={{0,4},{4,0},{8,12},{12,8},{16,20},{20,16},{24,28},{28,24},{1,5},{5... | collective-permute-start | bytes 786440 | tf_op jit(solution)/shard_map/ppermute | solution.py:103
  10.9 2.0 %collective-permute-start.3 = (bf16[8,16,1024]{2,1,0:T(8,128)(2,1)S(1)}, bf16[8,16,1024]{2,1,0:T(8,128)(2,1)S(1)}, u32[]{:S(2)}, u32[]{:S(2)}) collective-permute-start(bf16[8,16,1024]{2,1,0:T(8,128)(2,1)S(1)} %collective-permute-done.refs_2_), channel_id=1, source_target_pairs={{0,4},{4,0},{8,12},{12,8},{16,20},{20,16},{24,28},{28,24},{1,5},{5... | collective-permute-start | bytes 786440 | tf_op jit(solution)/shard_map/ppermute | solution.py:103
  12.5 8.4 %collective-permute-start.6 = (bf16[4,32,1024]{2,1,0:T(8,128)(2,1)S(1)}, bf16[4,32,1024]{2,1,0:T(8,128)(2,1)S(1)}, u32[]{:S(2)}, u32[]{:S(2)}) collective-permute-start(bf16[4,32,1024]{2,1,0:T(8,128)(2,1)S(1)} %pad_maximum_fusion.1), channel_id=1, source_target_pairs={{0,16},{4,20},{8,0},{12,4},{24,8},{28,12},{16,24},{20,28},{1,17},{... | collective-permute-start | bytes 786440 | tf_op jit(solution)/shard_map/ppermute | solution.py:108
  13.0 8.3 %collective-permute-start.5 = (bf16[4,32,1024]{2,1,0:T(8,128)(2,1)S(1)}, bf16[4,32,1024]{2,1,0:T(8,128)(2,1)S(1)}, u32[]{:S(2)}, u32[]{:S(2)}) collective-permute-start(bf16[4,32,1024]{2,1,0:T(8,128)(2,1)S(1)} %pad_maximum_fusion), channel_id=1, source_target_pairs={{0,8},{4,12},{8,24},{12,28},{24,16},{28,20},{16,0},{20,4},{1,9},{5... | collective-permute-start | bytes 786440 | tf_op jit(solution)/shard_map/ppermute | solution.py:108
  16.1 19.9 %copy-start.2 = (f32[8,4]{0,1:T(4,128)S(1)}, f32[8,4]{0,1:T(4,128)}, u32[]{:S(2)}) copy-start(f32[8,4]{0,1:T(4,128)} %param.6) | copy-start | bytes 388
  16.1 21.1 %copy-start.1 = (f32[8,2048]{1,0:T(8,128)S(1)}, f32[8,2048]{1,0:T(8,128)}, u32[]{:S(2)}) copy-start(f32[8,2048]{1,0:T(8,128)} %vir_ref.1) | copy-start | bytes 196612
  16.2 10.4 %collective-permute-start.7 = (f16[8,24,256]{2,1,0:T(8,128)(2,1)S(1)}, f16[8,24,256]{2,1,0:T(8,128)(2,1)S(1)}, u32[]{:S(2)}, u32[]{:S(2)}) collective-permute-start(f16[8,24,256]{2,1,0:T(8,128)(2,1)S(1)} %get-tuple-element.35), channel_id=1, source_target_pairs={{0,2},{1,3},{2,0},{3,1},{4,6},{5,7},{6,4},{7,5},{8,10},{9,11},{10,... | collective-permute-start | bytes 294920 | tf_op jit(solution)/shard_map/ppermute | solution.py:103
  18.9 8.0 %collective-permute-start.8 = (f16[8,24,256]{2,1,0:T(8,128)(2,1)S(1)}, f16[8,24,256]{2,1,0:T(8,128)(2,1)S(1)}, u32[]{:S(2)}, u32[]{:S(2)}) collective-permute-start(f16[8,24,256]{2,1,0:T(8,128)(2,1)S(1)} %get-tuple-element.37), channel_id=1, source_target_pairs={{0,1},{1,0},{2,3},{3,2},{4,5},{5,4},{6,7},{7,6},{8,9},{9,8},{10,11... | collective-permute-start | bytes 294920 | tf_op jit(solution)/shard_map/ppermute | solution.py:103
  20.5 6.8 %collective-permute-start.9 = (f16[8,24,256]{2,1,0:T(8,128)(2,1)S(1)}, f16[8,24,256]{2,1,0:T(8,128)(2,1)S(1)}, u32[]{:S(2)}, u32[]{:S(2)}) collective-permute-start(f16[8,24,256]{2,1,0:T(8,128)(2,1)S(1)} %get-tuple-element.36), channel_id=1, source_target_pairs={{0,3},{1,2},{2,1},{3,0},{4,7},{5,6},{6,5},{7,4},{8,11},{9,10},{10,... | collective-permute-start | bytes 294920 | tf_op jit(solution)/shard_map/ppermute | solution.py:103
  22.7 7.3 %collective-permute-start.12 = (f16[8,8,256]{2,1,0:T(8,128)(2,1)S(1)}, f16[8,8,256]{2,1,0:T(8,128)(2,1)S(1)}, u32[]{:S(2)}, u32[]{:S(2)}) collective-permute-start(f16[8,8,256]{2,1,0:T(8,128)(2,1)S(1)} %get-tuple-element.39), channel_id=1, source_target_pairs={{0,2},{1,3},{2,0},{3,1},{4,6},{5,7},{6,4},{7,5},{8,10},{9,11},{10,... | collective-permute-start | bytes 98312 | tf_op jit(solution)/shard_map/ppermute | solution.py:103
  25.3 5.7 %collective-permute-start.13 = (f16[8,8,256]{2,1,0:T(8,128)(2,1)S(1)}, f16[8,8,256]{2,1,0:T(8,128)(2,1)S(1)}, u32[]{:S(2)}, u32[]{:S(2)}) collective-permute-start(f16[8,8,256]{2,1,0:T(8,128)(2,1)S(1)} %get-tuple-element.41), channel_id=1, source_target_pairs={{0,3},{1,2},{2,1},{3,0},{4,7},{5,6},{6,5},{7,4},{8,11},{9,10},{10,... | collective-permute-start | bytes 98312 | tf_op jit(solution)/shard_map/ppermute | solution.py:103
  26.7 4.4 %collective-permute-start.14 = (f16[8,8,256]{2,1,0:T(8,128)(2,1)S(1)}, f16[8,8,256]{2,1,0:T(8,128)(2,1)S(1)}, u32[]{:S(2)}, u32[]{:S(2)}) collective-permute-start(f16[8,8,256]{2,1,0:T(8,128)(2,1)S(1)} %get-tuple-element.40), channel_id=1, source_target_pairs={{0,1},{1,0},{2,3},{3,2},{4,5},{5,4},{6,7},{7,6},{8,9},{9,8},{10,11... | collective-permute-start | bytes 98312 | tf_op jit(solution)/shard_map/ppermute | solution.py:103
  27.4 6.2 %collective-permute-start.10 = (f32[8,8,256]{2,1,0:T(8,128)S(1)}, f32[8,8,256]{2,1,0:T(8,128)S(1)}, u32[]{:S(2)}, u32[]{:S(2)}) collective-permute-start(f32[8,8,256]{2,1,0:T(8,128)S(1)} %get-tuple-element.43), channel_id=1, source_target_pairs={{0,16},{4,20},{8,0},{12,4},{24,8},{28,12},{16,24},{20,28},{1,17},{... | collective-permute-start | bytes 196616 | tf_op jit(solution)/shard_map/ppermute | solution.py:108
  28.5 5.0 %collective-permute-start.11 = (f32[8,8,256]{2,1,0:T(8,128)S(1)}, f32[8,8,256]{2,1,0:T(8,128)S(1)}, u32[]{:S(2)}, u32[]{:S(2)}) collective-permute-start(f32[8,8,256]{2,1,0:T(8,128)S(1)} %get-tuple-element.42), channel_id=1, source_target_pairs={{0,8},{4,12},{8,24},{12,28},{24,16},{28,20},{16,0},{20,4},{1,9},{5... | collective-permute-start | bytes 196616 | tf_op jit(solution)/shard_map/ppermute | solution.py:108
  31.1 4.9 %collective-permute-start.15 = (f16[8,8,256]{2,1,0:T(8,128)(2,1)S(1)}, f16[8,8,256]{2,1,0:T(8,128)(2,1)S(1)}, u32[]{:S(2)}, u32[]{:S(2)}) collective-permute-start(f16[8,8,256]{2,1,0:T(8,128)(2,1)S(1)} %fusion.4), channel_id=1, source_target_pairs={{0,24},{4,28},{8,16},{12,20},{16,8},{20,12},{24,0},{28,4},{1,25},{... | collective-permute-start | bytes 98312 | tf_op jit(solution)/shard_map/ppermute | solution.py:103
  33.6 3.6 %collective-permute-start.16 = (f32[8,12,256]{2,1,0:T(8,128)S(1)}, f32[8,12,256]{2,1,0:T(8,128)S(1)}, u32[]{:S(2)}, u32[]{:S(2)}) collective-permute-start(f32[8,12,256]{2,1,0:T(8,128)S(1)} %pad_maximum_fusion.2), channel_id=1, source_target_pairs={{0,4},{4,0},{8,12},{12,8},{16,20},{20,16},{24,28},{28,24},{1,5},{5... | collective-permute-start | bytes 294920 | tf_op jit(solution)/shard_map/ppermute | solution.py:103
  36.0 1.3 %collective-permute-start.17 = (f32[8,4,256]{2,1,0:T(4,128)S(1)}, f32[8,4,256]{2,1,0:T(4,128)S(1)}, u32[]{:S(2)}, u32[]{:S(2)}) collective-permute-start(f32[8,4,256]{2,1,0:T(4,128)S(1)} %slice.79), channel_id=1, source_target_pairs={{0,4},{4,0},{8,12},{12,8},{16,20},{20,16},{24,28},{28,24},{1,5},{5... | collective-permute-start | bytes 98312 | tf_op jit(solution)/shard_map/ppermute | solution.py:103
